TPU v7x, 128 devices: a whole 4x4x4 slice. The times are simulated.
128 devices in a mesh: freq: 32 (over x, z_hi, y), src: 4 (over z_lo, core).
Axes of the slice: x: 4, y: 4, z: 4 (z_hi: 2, z_lo: 2; z = z_hi * 2 + z_lo), core: 2. Of those that a mesh axis runs over, the one named last changes fastest.
Arguments:
- reflection: bfloat16 [2, 128, 2048, 2048], P(None, 'freq', None, 'src'), may hold values from -0.125 to 0.125
- aperture: int32 [16, 16], P(None, 'src'), may hold values 0 or 1
- initial: bfloat16 [2, 128, 128, 2048], P(None, 'freq', None, 'src'), may hold values from -6 to 6
- onsets: int32 [128, 2048], P('freq', 'src'), may hold values from 16 to 127
Outputs:
- focusing: bfloat16 [2, 128, 128, 2048], P(None, 'freq', None, 'src')
All inputs are finite; a program needn't handle non-finite values. No bound on the sum of `aperture` on one device may be relied on, other than what follows from the above.
Results may differ from a plain program's by a relative error of at most 0.02.
Values may be sent and summed in bfloat16 or wider, within the bound.
No kernel may reach another device: no remote copies, remote signals or barrier semaphores. Data moves between devices by JAX's collectives and lax.ppermute only.
A program may use at most 128 MiB of HBM per device.

v0:
```python
import functools
import math

import jax
import jax.numpy as jnp
import numpy as np
from jax import lax
from jax.experimental import pallas as pl
from jax.experimental.pallas import tpu as pltpu
from jax.sharding import PartitionSpec as P

ITERS = 2
AHEAD = 4
TOGETHER = 2
LANES = 128
MIB = 1024 * 1024
NT = (((1,), (1,)), ((), ()))
VMEM = pl.BlockSpec(memory_space=pltpu.VMEM)
BF = jnp.bfloat16
LIGHT = pl.CostEstimate(flops=1, bytes_accessed=1, transcendentals=0)


def mm(left, right):
    return jnp.dot(left, right, preferred_element_type=jnp.float32)


def nt(left, right):
    return lax.dot_general(left, right, NT, preferred_element_type=jnp.float32)


def split(values):
    high = values.astype(BF)
    low = (values - high.astype(values.dtype)).astype(BF)
    return high, low


def tables(columns, rows, freq_local, focal_block):
    plane_devices = columns * rows
    half = plane_devices * focal_block
    nfreq = 2 * plane_devices * freq_local
    packed = half * freq_local * 2
    pack = np.zeros((packed, packed), np.float32)
    for xy in range(plane_devices):
        for j in range(focal_block):
            for f in range(freq_local):
                for c in range(2):
                    row = ((xy * focal_block + j) * freq_local + f) * 2 + c
                    pack[row, ((f * 2 + c) * plane_devices + xy) * focal_block + j] = 1
    focal = np.arange(2 * half).reshape(columns, 2, rows * focal_block).transpose(1, 0, 2).reshape(2, half)
    choose = (focal[:, :, None] == np.arange(2 * half)).astype(np.float32)
    positions = np.arange(nfreq)
    phase = (np.outer(positions, positions) % nfreq) * (2.0 * math.pi / nfreq)
    cosine, sine = np.cos(phase), np.sin(phase)
    to_time = np.zeros((2, nfreq, nfreq, 2))
    to_time[0, :, :, 0] = cosine / nfreq
    to_time[0, :, :, 1] = -sine / nfreq
    to_time[1, :, :, 0] = sine / nfreq
    to_time[1, :, :, 1] = cosine / nfreq
    to_freq = np.zeros((nfreq, 2, 2, nfreq))
    to_freq[:, 0, 0, :] = cosine
    to_freq[:, 0, 1, :] = sine
    to_freq[:, 1, 0, :] = -sine
    to_freq[:, 1, 1, :] = cosine
    to_time = to_time.reshape(2 * nfreq, columns, 2, rows, freq_local * 2).transpose(0, 1, 3, 2, 4)
    to_time = to_time.reshape(2 * nfreq, 2 * nfreq).astype(np.float32)
    to_freq = to_freq.reshape(2 * nfreq, 2 * nfreq).astype(np.float32)
    return pack, choose, to_time, to_freq


def pair(matrix):
    high = matrix.astype(BF)
    low = (matrix - high.astype(np.float32)).astype(BF)
    return np.stack([high, low])


def spread(wide_ref, update_ref):
    for slab in range(wide_ref.shape[0]):
        wide_ref[slab] = update_ref[:, slab * LANES : (slab + 1) * LANES].astype(jnp.float32)


def every(wide_ref, start, count, stride):
    slabs = [wide_ref[slab, pl.ds(start, count, stride), :] for slab in range(wide_ref.shape[0])]
    return jnp.concatenate(slabs, axis=1)


def wide(update):
    rows, width = update.shape
    return pltpu.VMEM((width // LANES, rows, LANES), jnp.float32)


def weights(polarity, half, choose_ref, initial_ref, update_ref, wide_ref, left_ref, right_ref):
    nfreq = left_ref.shape[0]
    halves, count, focal = choose_ref.shape
    if update_ref is not None:
        spread(wide_ref, update_ref)
    for freq in range(nfreq):
        planes = []
        for plane in range(2):
            value = initial_ref[plane, freq]
            if update_ref is not None:
                update = every(wide_ref, 2 * freq + plane, focal, 2 * nfreq)
                value = (value.astype(jnp.float32) + update).astype(BF)
            planes.append(value)
        for place in range(halves):
            pick = choose_ref[jnp.bitwise_xor(half, place)]
            real, imag = mm(pick, planes[0]), mm(pick, planes[1])
            low = place * 2 * count
            left_ref[freq, :, low : low + 2 * count] = jnp.concatenate([real, imag], axis=0).T.astype(BF)
            right = jnp.concatenate([-polarity * imag, polarity * real], axis=0)
            right_ref[freq, :, low : low + 2 * count] = right.T.astype(BF)


def product_kernel(polarity, rels, build, tokens, src_ref, mask_ref, reflection_ref, *refs):
    update_ref = wide_ref = None
    if build == "first":
        choose_ref, initial_ref, *refs = refs
    elif build == "update":
        choose_ref, initial_ref, update_ref, *refs = refs
    else:
        left_ref, right_ref, *refs = refs
    refs = refs[tokens:]
    outs, refs = refs[: len(rels)], refs[len(rels) :]
    if build:
        left_ref, right_ref, *refs = refs
    held_ref, sems, *refs = refs
    if build == "update":
        (wide_ref,) = refs
    nfreq, width, _ = outs[0].shape
    pieces = [(place, freq) for place in range(len(rels)) for freq in range(nfreq)]
    source = src_ref[0]

    def fetch(piece, plane):
        place, freq = pieces[piece]
        block = jnp.bitwise_xor(source, rels[place])
        return pltpu.make_async_copy(
            reflection_ref.at[plane, freq, pl.ds(block * width, width), :],
            held_ref.at[piece, plane],
            sems.at[piece, plane],
        )

    def begin(piece):
        if piece < len(pieces):
            for plane in range(2):
                fetch(piece, plane).start()

    for piece in range(AHEAD):
        begin(piece)
    if build:
        weights(polarity, src_ref[1], choose_ref, initial_ref, update_ref, wide_ref, left_ref, right_ref)

    rows, pack = mask_ref.shape[0] // 4, mask_ref.shape[1]
    tall = width // rows
    for low in range(0, len(pieces), TOGETHER):
        both = range(low, min(low + TOGETHER, len(pieces)))
        for piece in both:
            for plane in range(2):
                fetch(piece, plane).wait()
        for piece in both:
            begin(piece + AHEAD)
        for piece in both:
            place, freq = pieces[piece]
            masked = []
            for plane in range(2):
                strips = []
                for strip in range(rows):
                    mask = mask_ref[jnp.bitwise_xor(source, rels[place]) * rows + strip]
                    part = held_ref[piece, plane, strip * tall : (strip + 1) * tall, :]
                    part = part.reshape(tall // pack, pack, part.shape[1]) * mask[None]
                    strips.append(part.reshape(tall, part.shape[2]))
                masked.append(jnp.concatenate(strips, axis=0))
            total = mm(masked[0], left_ref[freq]) + mm(masked[1], right_ref[freq])
            outs[place][freq] = total.astype(BF)


def products(polarity, rels, src, mask, reflection, choose, initial=None, update=None, built=None, after=()):
    planes, nfreq, receivers, sources = reflection.shape
    halves, half, focal = choose.shape
    lanes = 2 * half * halves
    out = jax.ShapeDtypeStruct((nfreq, sources, lanes), BF)
    scratch = [
        pltpu.VMEM((len(rels) * nfreq, 2, sources, sources), BF),
        pltpu.SemaphoreType.DMA((len(rels) * nfreq, 2)),
    ]
    outs = [out] * len(rels)
    if built is not None:
        build, extra = "", list(built)
    elif update is None:
        build, extra = "first", [choose, initial]
    else:
        build, extra = "update", [choose, initial, update]
        scratch.append(wide(update))
    if build:
        outs += [out] * 2
    anywhere = pl.BlockSpec(memory_space=pl.ANY)
    return pl.pallas_call(
        functools.partial(product_kernel, polarity, rels, build, len(after)),
        in_specs=[pl.BlockSpec(memory_space=pltpu.SMEM), VMEM, anywhere]
        + [VMEM] * len(extra)
        + [anywhere] * len(after),
        out_specs=[VMEM] * len(outs),
        scratch_shapes=scratch,
        out_shape=outs,
        compiler_params=pltpu.CompilerParams(vmem_limit_bytes=46 * MIB),
        cost_estimate=LIGHT,
        name="products",
    )(src, mask, reflection, *extra, *after)


def call(kernel, name, outs, *args, after=()):
    return pl.pallas_call(
        kernel,
        in_specs=[VMEM] * len(args) + [pl.BlockSpec(memory_space=pl.ANY)] * len(after),
        out_specs=[VMEM] * len(outs),
        out_shape=[jax.ShapeDtypeStruct(shape, BF) for shape in outs],
        compiler_params=pltpu.CompilerParams(vmem_limit_bytes=16 * MIB),
        cost_estimate=LIGHT,
        name=name,
    )(*args, *after)


def add_kernel(place, mine_ref, core_ref, out_ref):
    lanes = out_ref.shape[2]
    here = slice(place * lanes, (place + 1) * lanes)
    total = mine_ref[:, :, here].astype(jnp.float32) + core_ref[:, :, here].astype(jnp.float32)
    out_ref[...] = total.astype(BF)


def packed_sum(place, pack_ref, mine_ref, core_ref, far_ref):
    nfreq, width, lanes = far_ref.shape
    here = slice(place * lanes, (place + 1) * lanes)
    parts = []
    for f in range(nfreq):
        total = mine_ref[f, :, here].astype(jnp.float32) + core_ref[f, :, here].astype(jnp.float32)
        parts.append((total + far_ref[f].astype(jnp.float32)).astype(BF))
    return nt(pack_ref[...], jnp.concatenate(parts, axis=1)).astype(BF)


def pack_other_kernel(pack_ref, mine_ref, core_ref, far_ref, *refs):
    out_ref = refs[-1]
    out_ref[...] = packed_sum(1, pack_ref, mine_ref, core_ref, far_ref).reshape(out_ref.shape)


def pack_own_kernel(where_ref, pack_ref, mine_ref, core_ref, far_ref, outer_ref, out_ref):
    devices, rows, width = outer_ref.shape
    half = where_ref[1]
    own = packed_sum(0, pack_ref, mine_ref, core_ref, far_ref).reshape(outer_ref.shape)
    out_ref[:, pl.ds(pl.multiple_of(half * rows, rows), rows), :] = own
    out_ref[:, pl.ds(pl.multiple_of((1 - half) * rows, rows), rows), :] = outer_ref[...]


def pack_own(where, *args):
    devices, rows, width = args[-1].shape
    return pl.pallas_call(
        pack_own_kernel,
        in_specs=[pl.BlockSpec(memory_space=pltpu.SMEM)] + [VMEM] * len(args),
        out_specs=VMEM,
        out_shape=jax.ShapeDtypeStruct((devices, 2 * rows, width), BF),
        compiler_params=pltpu.CompilerParams(vmem_limit_bytes=16 * MIB),
        cost_estimate=LIGHT,
        name="pack_own",
    )(where, *args)


def window_kernel(dft_ref, onsets_ref, traces_ref, out_ref):
    focal, width = onsets_ref.shape
    devices, rows, _ = traces_ref.shape
    group = rows // (2 * focal)
    nfreq = dft_ref.shape[1] // 2
    step = lax.broadcasted_iota(jnp.int32, (nfreq, width), 0)
    traces = traces_ref[...].astype(jnp.float32).reshape(2 * devices, focal, group, width)
    results = []
    for j in range(focal):
        column = traces[:, j].reshape(2 * nfreq, width).astype(BF)
        time = mm(dft_ref[0], column) + mm(dft_ref[1], column)
        keep = step < onsets_ref[j : j + 1, :]
        keep = jnp.concatenate([keep, keep], axis=0)
        high, low = split(jnp.where(keep, time, 0.0))
        back = mm(dft_ref[2], high) + mm(dft_ref[2], low) + mm(dft_ref[3], high)
        results.append(back.reshape(2 * devices, group, width))
    out_ref[...] = jnp.stack(results, axis=1).reshape(out_ref.shape).astype(BF)


def final_kernel(initial_ref, update_ref, out_ref, wide_ref, block_ref, sems):
    planes, nfreq, focal, _ = initial_ref.shape
    spread(wide_ref, update_ref)
    copies = []
    for freq in range(nfreq):
        for plane in range(planes):
            value = initial_ref[plane, freq].astype(jnp.float32)
            value = value + every(wide_ref, planes * freq + plane, focal, planes * nfreq)
            block_ref[plane, freq] = value.astype(BF)
            copy = pltpu.make_async_copy(
                block_ref.at[plane, freq], out_ref.at[plane, freq], sems.at[plane, freq]
            )
            copy.start()
            copies.append(copy)
    for copy in copies:
        copy.wait()


def finish(initial, update):
    planes, nfreq, focal, sources = initial.shape
    return pl.pallas_call(
        final_kernel,
        in_specs=[VMEM, VMEM],
        out_specs=pl.BlockSpec(memory_space=pl.ANY),
        scratch_shapes=[
            wide(update),
            pltpu.VMEM(initial.shape, BF),
            pltpu.SemaphoreType.DMA((planes, nfreq)),
        ],
        out_shape=jax.ShapeDtypeStruct(initial.shape, BF),
        compiler_params=pltpu.CompilerParams(vmem_limit_bytes=16 * MIB),
        name="finish",
    )(initial, update)


def swap(values, bit):
    return lax.ppermute(values, "src", [(i, i ^ bit) for i in range(lax.axis_size("src"))])


def outward(values, columns, rows):
    pairs = []
    for x in range(columns):
        for h in range(2):
            for y in range(rows):
                for s in range(4):
                    here = ((x * 2 + h) * rows + y) * 4 + s
                    there = ((x * 2 + 1 - h) * rows + y) * 4 + (s ^ 2)
                    pairs.append((here, there))
    return lax.ppermute(values, ("freq", "src"), pairs)


def local(reflection, aperture, initial, onsets):
    planes, freq_local, receivers, sources = reflection.shape
    devices = lax.axis_size("freq")
    focal = initial.shape[2]
    focal_block = focal // devices
    block = receivers // aperture.shape[0]
    columns = rows = math.isqrt(devices // 2)
    pack, choose, to_time, to_freq = tables(columns, rows, freq_local, focal_block)
    pack = jnp.asarray(pack, BF)
    choose = jnp.asarray(choose, BF)
    dft = jnp.asarray(np.concatenate([pair(to_time), pair(to_freq)]))
    half = (lax.axis_index("freq") // rows) % 2
    where = jnp.stack([lax.axis_index("src"), half]).astype(jnp.int32)
    mask = jnp.repeat(aperture.astype(BF), block, axis=1)
    mask = jnp.broadcast_to(mask[:, None], (mask.shape[0], 16, sources))
    plane_groups = [
        [(x * 2 + h) * rows + y for x in range(columns) for y in range(rows)] for h in range(2)
    ]
    block_rows = focal_block * freq_local * planes
    part = (freq_local, sources, focal * planes // 2)

    update = None
    for iteration in range(ITERS):
        polarity = 1.0 if iteration % 2 == 0 else -1.0

        def respond(rel, **more):
            return products(polarity, (rel,), where, mask, reflection, choose, **more)

        send, left, right = respond(1, initial=initial, update=update)
        core_near = swap(send, 1)
        (near,) = respond(0, built=(left, right))
        (total,) = call(functools.partial(add_kernel, 1), "add", [part], near, core_near)
        far_other = swap(total, 2)
        (send,) = respond(3, built=(left, right), after=(total,))
        core_far = swap(send, 1)
        (remote,) = respond(2, built=(left, right), after=(total,))
        (total,) = call(functools.partial(add_kernel, 0), "add", [part], remote, core_far)
        far_own = swap(total, 2)
        shape = (devices // 2, block_rows, sources)
        (other,) = call(pack_other_kernel, "pack_other", [shape], pack, remote, core_far, far_other, after=(total,))
        outer = outward(other, columns, rows)
        responses = pack_own(where, pack, near, core_near, far_own, outer)
        traces = lax.all_to_all(responses, "freq", 0, 0, tiled=True, axis_index_groups=plane_groups)
        (truncated,) = call(
            window_kernel, "window", [(devices, block_rows, sources)], dft, onsets, traces
        )
        update = lax.all_to_all(truncated, "freq", 0, 0, tiled=True)
        update = update.reshape(devices * block_rows, sources)
    return finish(initial, update)


def solution(mesh):
    placed = (
        P(None, "freq", None, "src"),
        P(None, "src"),
        P(None, "freq", None, "src"),
        P("freq", "src"),
    )
    return jax.shard_map(
        local, mesh=mesh, in_specs=placed, out_specs=P(None, "freq", None, "src"), check_vma=False
    )
```

profile of v0, /device:TPU:0, one launch (start us, length us, event | category | flops | bytes accessed | tf_op | source)
XLA Modules:
  0.0 174.8 jit_solution(1846075795518113149)
XLA Ops:
  0.0 0.7 convert_element_type.3
  0.7 0.1 copy.8
  0.8 0.1 broadcast_in_dim.10
  0.9 0.1 pad_add_fusion.src_ref.where_ref
  1.0 1.2 copy-done
  2.2 0.8 copy-done.4
  3.0 4.2 %products.8 = (bf16[4,512,256]{2,1,0:T(8,128)(2,1)S(1)}, bf16[4,512,256]{2,1,0:T(8,128)(2,1)S(1)}, bf16[4,512,256]{2,1,0:T(8,128)(2,1)S(1)}) custom-call(s32[2]{0:T(128)S(1)} %pad_add_fusion.src_ref.where_ref, bf16[16,16,512]{2,1,0:T(8,128)(2,1)S(1)} %broadcast_in_dim.12.mask_ref, bf16[2,4,2048,512]{3,2,1,0:T(8,128)(2,1)} %reflection_ref.15, ...), custom_call_target="tpu_custom_call" | custom-call | flops 1 | bytes 1 | tf_op jit(solution)/shard_map/products/pallas_call | solution.py:195
  7.1 0.1 collective-permute-start
  7.2 3.6 %products.9.mine_ref = bf16[4,512,256]{2,1,0:T(8,128)(2,1)S(1)} custom-call(s32[2]{0:T(128)S(1)} %pad_add_fusion.src_ref.where_ref, bf16[16,16,512]{2,1,0:T(8,128)(2,1)S(1)} %broadcast_in_dim.12.mask_ref, bf16[2,4,2048,512]{3,2,1,0:T(8,128)(2,1)} %reflection_ref.15, bf16[4,512,256]{2,1,0:T(8,128)(2,1)S(1)} %get-tuple-element.11.refs_0_, ...), custom_call_target="tpu_custom_call" | custom-call | flops 1 | bytes 1 | tf_op jit(solution)/shard_map/products/pallas_call | solution.py:195
  10.8 0.1 add.12.refs_2_
  11.0 3.6 %products.11 = bf16[4,512,256]{2,1,0:T(8,128)(2,1)S(1)} custom-call(s32[2]{0:T(128)S(1)} %pad_add_fusion.src_ref.where_ref, bf16[16,16,512]{2,1,0:T(8,128)(2,1)S(1)} %broadcast_in_dim.12.mask_ref, bf16[2,4,2048,512]{3,2,1,0:T(8,128)(2,1)} %reflection_ref.15, bf16[4,512,256]{2,1,0:T(8,128)(2,1)S(1)} %get-tuple-element.11.refs_0_, ...), custom_call_target="tpu_custom_call" | custom-call | flops 1 | bytes 1 | tf_op jit(solution)/shard_map/products/pallas_call | solution.py:195
  14.6 0.0 copy-start.2
  14.6 0.0 copy-start.3
  14.6 0.0 copy-start.5
  14.7 0.6 collective-permute-start.1
  15.3 2.0 %collective-permute-start.3 = (bf16[4,512,128]{2,1,0:T(8,128)(2,1)S(1)}, bf16[4,512,128]{2,1,0:T(8,128)(2,1)S(1)}, u32[]{:S(2)}, u32[]{:S(2)}) collective-permute-start(bf16[4,512,128]{2,1,0:T(8,128)(2,1)S(1)} %add.12.refs_2_), channel_id=1, source_target_pairs={{0,2},{1,3},{2,0},{3,1},{4,6},{5,7},{6,4},{7,5},{8,10},{9,11},{10,... | collective-permute-start | bytes 1572872 | tf_op jit(solution)/shard_map/ppermute | solution.py:319
  17.2 3.6 %products.10.mine_ref = bf16[4,512,256]{2,1,0:T(8,128)(2,1)S(1)} custom-call(s32[2]{0:T(128)S(1)} %pad_add_fusion.src_ref.where_ref, bf16[16,16,512]{2,1,0:T(8,128)(2,1)S(1)} %broadcast_in_dim.12.mask_ref, bf16[2,4,2048,512]{3,2,1,0:T(8,128)(2,1)} %reflection_ref.15, bf16[4,512,256]{2,1,0:T(8,128)(2,1)S(1)} %get-tuple-element.11.refs_0_, ...), custom_call_target="tpu_custom_call" | custom-call | flops 1 | bytes 1 | tf_op jit(solution)/shard_map/products/pallas_call | solution.py:195
  20.9 0.1 add.13.refs_0_
  21.0 0.1 collective-permute-start.2
  21.1 8.9 %collective-permute-done.3.far_ref = bf16[4,512,128]{2,1,0:T(8,128)(2,1)S(1)} collective-permute-done((bf16[4,512,128]{2,1,0:T(8,128)(2,1)S(1)}, bf16[4,512,128]{2,1,0:T(8,128)(2,1)S(1)}, u32[]{:S(2)}, u32[]{:S(2)}) %collective-permute-start.3) | collective-permute-done | bytes 524320 | tf_op jit(solution)/shard_map/ppermute | solution.py:319
  30.0 0.5 pack_other.2
  30.5 4.2 %collective-permute-start.4 = (bf16[16,32,512]{2,1,0:T(8,128)(2,1)S(1)}, bf16[16,32,512]{2,1,0:T(8,128)(2,1)S(1)}, u32[]{:S(2)}, u32[]{:S(2)}) collective-permute-start(bf16[16,32,512]{2,1,0:T(8,128)(2,1)S(1)} %pack_other.2), channel_id=1, source_target_pairs={{0,18},{1,19},{2,16},{3,17},{4,22},{5,23},{6,20},{7,21},{8,26},{9,... | collective-permute-start | bytes 1572872 | tf_op jit(solution)/shard_map/ppermute | solution.py:331
  34.7 5.9 %collective-permute-done.2.far_ref = bf16[4,512,128]{2,1,0:T(8,128)(2,1)S(1)} collective-permute-done((bf16[4,512,128]{2,1,0:T(8,128)(2,1)S(1)}, bf16[4,512,128]{2,1,0:T(8,128)(2,1)S(1)}, u32[]{:S(2)}, u32[]{:S(2)}) %collective-permute-start.2) | collective-permute-done | bytes 524320 | tf_op jit(solution)/shard_map/ppermute | solution.py:319
  40.6 4.6 %collective-permute-done.4.outer_ref = bf16[16,32,512]{2,1,0:T(8,128)(2,1)S(1)} collective-permute-done((bf16[16,32,512]{2,1,0:T(8,128)(2,1)S(1)}, bf16[16,32,512]{2,1,0:T(8,128)(2,1)S(1)}, u32[]{:S(2)}, u32[]{:S(2)}) %collective-permute-start.4) | collective-permute-done | bytes 524320 | tf_op jit(solution)/shard_map/ppermute | solution.py:331
  45.2 1.1 pack_own.2
  46.3 21.9 %all_to_all.20.traces_ref = bf16[16,64,512]{2,1,0:T(8,128)(2,1)S(1)} all-to-all(bf16[16,64,512]{2,1,0:T(8,128)(2,1)S(1)} %pack_own.2), channel_id=1, replica_groups={{0,4,8,12,32,36,40,44,64,68,72,76,96,100,104,108},{16,20,24,28,48,52,56..., dimensions={0} | all-to-all | bytes 2097152 | tf_op jit(solution)/shard_map/all_to_all | solution.py:376
  68.2 2.3 %window.2 = bf16[32,32,512]{2,1,0:T(8,128)(2,1)S(1)} custom-call(bf16[4,256,256]{2,1,0:T(8,128)(2,1)S(1)} %copy-done.3, s32[4,512]{1,0:T(4,128)S(1)} %copy-done.6, bf16[16,64,512]{2,1,0:T(8,128)(2,1)S(1)} %all_to_all.20.traces_ref), custom_call_target="tpu_custom_call" | custom-call | flops 1 | bytes 1 | tf_op jit(solution)/shard_map/window/pallas_call | solution.py:210
  70.4 19.7 %all_to_all.21 = bf16[32,32,512]{2,1,0:T(8,128)(2,1)S(1)} all-to-all(bf16[32,32,512]{2,1,0:T(8,128)(2,1)S(1)} %window.2), channel_id=1, replica_groups=mesh['freq'=32,'src'=4] {'freq'}, dimensions={0} | all-to-all | bytes 2097152 | tf_op jit(solution)/shard_map/all_to_all | solution.py:380
  90.1 4.6 %products.12 = (bf16[4,512,256]{2,1,0:T(8,128)(2,1)S(1)}, bf16[4,512,256]{2,1,0:T(8,128)(2,1)S(1)}, bf16[4,512,256]{2,1,0:T(8,128)(2,1)S(1)}) custom-call(s32[2]{0:T(128)S(1)} %pad_add_fusion.src_ref.where_ref, bf16[16,16,512]{2,1,0:T(8,128)(2,1)S(1)} %broadcast_in_dim.12.mask_ref, bf16[2,4,2048,512]{3,2,1,0:T(8,128)(2,1)} %reflection_ref.15, ...), custom_call_target="tpu_custom_call" | custom-call | flops 1 | bytes 1 | tf_op jit(solution)/shard_map/products/pallas_call | solution.py:195
  94.8 0.1 collective-permute-start.5
  94.8 3.6 %products.13.mine_ref = bf16[4,512,256]{2,1,0:T(8,128)(2,1)S(1)} custom-call(s32[2]{0:T(128)S(1)} %pad_add_fusion.src_ref.where_ref, bf16[16,16,512]{2,1,0:T(8,128)(2,1)S(1)} %broadcast_in_dim.12.mask_ref, bf16[2,4,2048,512]{3,2,1,0:T(8,128)(2,1)} %reflection_ref.15, bf16[4,512,256]{2,1,0:T(8,128)(2,1)S(1)} %get-tuple-element.14.refs_0_, ...), custom_call_target="tpu_custom_call" | custom-call | flops 1 | bytes 1 | tf_op jit(solution)/shard_map/products/pallas_call | solution.py:195
  98.5 0.1 add.14.refs_2_
  98.6 3.6 %products.15 = bf16[4,512,256]{2,1,0:T(8,128)(2,1)S(1)} custom-call(s32[2]{0:T(128)S(1)} %pad_add_fusion.src_ref.where_ref, bf16[16,16,512]{2,1,0:T(8,128)(2,1)S(1)} %broadcast_in_dim.12.mask_ref, bf16[2,4,2048,512]{3,2,1,0:T(8,128)(2,1)} %reflection_ref.15, bf16[4,512,256]{2,1,0:T(8,128)(2,1)S(1)} %get-tuple-element.14.refs_0_, ...), custom_call_target="tpu_custom_call" | custom-call | flops 1 | bytes 1 | tf_op jit(solution)/shard_map/products/pallas_call | solution.py:195
  102.2 0.6 collective-permute-start.6
  102.8 2.2 %collective-permute-start.8 = (bf16[4,512,128]{2,1,0:T(8,128)(2,1)S(1)}, bf16[4,512,128]{2,1,0:T(8,128)(2,1)S(1)}, u32[]{:S(2)}, u32[]{:S(2)}) collective-permute-start(bf16[4,512,128]{2,1,0:T(8,128)(2,1)S(1)} %add.14.refs_2_), channel_id=1, source_target_pairs={{0,2},{1,3},{2,0},{3,1},{4,6},{5,7},{6,4},{7,5},{8,10},{9,11},{10,... | collective-permute-start | bytes 1572872 | tf_op jit(solution)/shard_map/ppermute | solution.py:319
  105.0 3.6 %products.14.mine_ref = bf16[4,512,256]{2,1,0:T(8,128)(2,1)S(1)} custom-call(s32[2]{0:T(128)S(1)} %pad_add_fusion.src_ref.where_ref, bf16[16,16,512]{2,1,0:T(8,128)(2,1)S(1)} %broadcast_in_dim.12.mask_ref, bf16[2,4,2048,512]{3,2,1,0:T(8,128)(2,1)} %reflection_ref.15, bf16[4,512,256]{2,1,0:T(8,128)(2,1)S(1)} %get-tuple-element.14.refs_0_, ...), custom_call_target="tpu_custom_call" | custom-call | flops 1 | bytes 1 | tf_op jit(solution)/shard_map/products/pallas_call | solution.py:195
  108.6 0.1 add.15.refs_0_
  108.7 0.1 collective-permute-start.7
  108.8 8.9 %collective-permute-done.8.far_ref = bf16[4,512,128]{2,1,0:T(8,128)(2,1)S(1)} collective-permute-done((bf16[4,512,128]{2,1,0:T(8,128)(2,1)S(1)}, bf16[4,512,128]{2,1,0:T(8,128)(2,1)S(1)}, u32[]{:S(2)}, u32[]{:S(2)}) %collective-permute-start.8) | collective-permute-done | bytes 524320 | tf_op jit(solution)/shard_map/ppermute | solution.py:319
  117.7 0.5 pack_other.3
  118.2 1.5 collective-permute-start.9
  119.7 8.7 %collective-permute-done.7.far_ref = bf16[4,512,128]{2,1,0:T(8,128)(2,1)S(1)} collective-permute-done((bf16[4,512,128]{2,1,0:T(8,128)(2,1)S(1)}, bf16[4,512,128]{2,1,0:T(8,128)(2,1)S(1)}, u32[]{:S(2)}, u32[]{:S(2)}) %collective-permute-start.7) | collective-permute-done | bytes 524320 | tf_op jit(solution)/shard_map/ppermute | solution.py:319
  128.4 4.0 %collective-permute-done.9.outer_ref = bf16[16,32,512]{2,1,0:T(8,128)(2,1)S(1)} collective-permute-done((bf16[16,32,512]{2,1,0:T(8,128)(2,1)S(1)}, bf16[16,32,512]{2,1,0:T(8,128)(2,1)S(1)}, u32[]{:S(2)}, u32[]{:S(2)}) %collective-permute-start.9) | collective-permute-done | bytes 524320 | tf_op jit(solution)/shard_map/ppermute | solution.py:331
  132.4 1.1 pack_own.3
  133.5 18.4 %all_to_all.22.traces_ref = bf16[16,64,512]{2,1,0:T(8,128)(2,1)S(1)} all-to-all(bf16[16,64,512]{2,1,0:T(8,128)(2,1)S(1)} %pack_own.3), channel_id=1, replica_groups={{0,4,8,12,32,36,40,44,64,68,72,76,96,100,104,108},{16,20,24,28,48,52,56..., dimensions={0} | all-to-all | bytes 2097152 | tf_op jit(solution)/shard_map/all_to_all | solution.py:376
  151.8 2.3 %window.3 = bf16[32,32,512]{2,1,0:T(8,128)(2,1)S(1)} custom-call(bf16[4,256,256]{2,1,0:T(8,128)(2,1)S(1)} %copy-done.3, s32[4,512]{1,0:T(4,128)S(1)} %copy-done.6, bf16[16,64,512]{2,1,0:T(8,128)(2,1)S(1)} %all_to_all.22.traces_ref), custom_call_target="tpu_custom_call" | custom-call | flops 1 | bytes 1 | tf_op jit(solution)/shard_map/window/pallas_call | solution.py:210
  154.1 19.1 %all_to_all.23 = bf16[32,32,512]{2,1,0:T(8,128)(2,1)S(1)} all-to-all(bf16[32,32,512]{2,1,0:T(8,128)(2,1)S(1)} %window.3), channel_id=1, replica_groups=mesh['freq'=32,'src'=4] {'freq'}, dimensions={0} | all-to-all | bytes 2097152 | tf_op jit(solution)/shard_map/all_to_all | solution.py:380
  173.2 1.5 finish.1
  (15 shorter events, 0.1 us)
Async XLA Ops:
  1.0 1.2 copy-start
  2.2 0.8 copy-start.4
  7.1 3.7 %collective-permute-start = (bf16[4,512,256]{2,1,0:T(8,128)(2,1)S(1)}, bf16[4,512,256]{2,1,0:T(8,128)(2,1)S(1)}, u32[]{:S(2)}, u32[]{:S(2)}) collective-permute-start(bf16[4,512,256]{2,1,0:T(8,128)(2,1)S(1)} %get-tuple-element.13), channel_id=1, source_target_pairs={{0,1},{1,0},{2,3},{3,2},{4,5},{5,4},{6,7},{7,6},{8,9},{9,8},{10,11... | collective-permute-start | bytes 3145736 | tf_op jit(solution)/shard_map/ppermute | solution.py:319
  14.6 15.4 %copy-start.2 = (bf16[512,512]{1,0:T(8,128)(2,1)S(1)}, bf16[512,512]{1,0:T(8,128)(2,1)}, u32[]{:S(2)}) copy-start(bf16[512,512]{1,0:T(8,128)(2,1)} %constant.41.clone.pack_ref) | copy-start | bytes 1572868
  14.6 53.6 %copy-start.3 = (bf16[4,256,256]{2,1,0:T(8,128)(2,1)S(1)}, bf16[4,256,256]{2,1,0:T(8,128)(2,1)}, u32[]{:S(2)}) copy-start(bf16[4,256,256]{2,1,0:T(8,128)(2,1)} %constant.43.clone.dft_ref) | copy-start | bytes 1572868
  14.6 53.6 %copy-start.6 = (s32[4,512]{1,0:T(4,128)S(1)}, s32[4,512]{1,0:T(4,128)}, u32[]{:S(2)}) copy-start(s32[4,512]{1,0:T(4,128)} %onsets_ref.3) | copy-start | bytes 24580
  14.6 75.5 %copy-start.1 = (bf16[2,4,128,512]{3,2,1,0:T(8,128)(2,1)S(1)}, bf16[2,4,128,512]{3,2,1,0:T(8,128)(2,1)}, u32[]{:S(2)}) copy-start(bf16[2,4,128,512]{3,2,1,0:T(8,128)(2,1)} %initial_ref.1) | copy-start | bytes 3145732
  14.6 75.5 %copy-start.5 = (bf16[2,64,128]{2,1,0:T(8,128)(2,1)S(1)}, bf16[2,64,128]{2,1,0:T(8,128)(2,1)}, u32[]{:S(2)}) copy-start(bf16[2,64,128]{2,1,0:T(8,128)(2,1)} %constant.42.clone.refs_0_) | copy-start | bytes 98308
  14.7 6.2 %collective-permute-start.1 = (bf16[4,512,256]{2,1,0:T(8,128)(2,1)S(1)}, bf16[4,512,256]{2,1,0:T(8,128)(2,1)S(1)}, u32[]{:S(2)}, u32[]{:S(2)}) collective-permute-start(bf16[4,512,256]{2,1,0:T(8,128)(2,1)S(1)} %products.11), channel_id=1, source_target_pairs={{0,1},{1,0},{2,3},{3,2},{4,5},{5,4},{6,7},{7,6},{8,9},{9,8},{10,11... | collective-permute-start | bytes 3145736 | tf_op jit(solution)/shard_map/ppermute | solution.py:319
  15.3 14.7 %collective-permute-start.3 = (bf16[4,512,128]{2,1,0:T(8,128)(2,1)S(1)}, bf16[4,512,128]{2,1,0:T(8,128)(2,1)S(1)}, u32[]{:S(2)}, u32[]{:S(2)}) collective-permute-start(bf16[4,512,128]{2,1,0:T(8,128)(2,1)S(1)} %add.12.refs_2_), channel_id=1, source_target_pairs={{0,2},{1,3},{2,0},{3,1},{4,6},{5,7},{6,4},{7,5},{8,10},{9,11},{10,... | collective-permute-start | bytes 1572872 | tf_op jit(solution)/shard_map/ppermute | solution.py:319
  21.0 19.7 %collective-permute-start.2 = (bf16[4,512,128]{2,1,0:T(8,128)(2,1)S(1)}, bf16[4,512,128]{2,1,0:T(8,128)(2,1)S(1)}, u32[]{:S(2)}, u32[]{:S(2)}) collective-permute-start(bf16[4,512,128]{2,1,0:T(8,128)(2,1)S(1)} %add.13.refs_0_), channel_id=1, source_target_pairs={{0,2},{1,3},{2,0},{3,1},{4,6},{5,7},{6,4},{7,5},{8,10},{9,11},{10,... | collective-permute-start | bytes 1572872 | tf_op jit(solution)/shard_map/ppermute | solution.py:319
  30.5 14.7 %collective-permute-start.4 = (bf16[16,32,512]{2,1,0:T(8,128)(2,1)S(1)}, bf16[16,32,512]{2,1,0:T(8,128)(2,1)S(1)}, u32[]{:S(2)}, u32[]{:S(2)}) collective-permute-start(bf16[16,32,512]{2,1,0:T(8,128)(2,1)S(1)} %pack_other.2), channel_id=1, source_target_pairs={{0,18},{1,19},{2,16},{3,17},{4,22},{5,23},{6,20},{7,21},{8,26},{9,... | collective-permute-start | bytes 1572872 | tf_op jit(solution)/shard_map/ppermute | solution.py:331
  94.8 3.7 %collective-permute-start.5 = (bf16[4,512,256]{2,1,0:T(8,128)(2,1)S(1)}, bf16[4,512,256]{2,1,0:T(8,128)(2,1)S(1)}, u32[]{:S(2)}, u32[]{:S(2)}) collective-permute-start(bf16[4,512,256]{2,1,0:T(8,128)(2,1)S(1)} %get-tuple-element.16), channel_id=1, source_target_pairs={{0,1},{1,0},{2,3},{3,2},{4,5},{5,4},{6,7},{7,6},{8,9},{9,8},{10,11... | collective-permute-start | bytes 3145736 | tf_op jit(solution)/shard_map/ppermute | solution.py:319
  102.2 6.4 %collective-permute-start.6 = (bf16[4,512,256]{2,1,0:T(8,128)(2,1)S(1)}, bf16[4,512,256]{2,1,0:T(8,128)(2,1)S(1)}, u32[]{:S(2)}, u32[]{:S(2)}) collective-permute-start(bf16[4,512,256]{2,1,0:T(8,128)(2,1)S(1)} %products.15), channel_id=1, source_target_pairs={{0,1},{1,0},{2,3},{3,2},{4,5},{5,4},{6,7},{7,6},{8,9},{9,8},{10,11... | collective-permute-start | bytes 3145736 | tf_op jit(solution)/shard_map/ppermute | solution.py:319
  102.8 14.9 %collective-permute-start.8 = (bf16[4,512,128]{2,1,0:T(8,128)(2,1)S(1)}, bf16[4,512,128]{2,1,0:T(8,128)(2,1)S(1)}, u32[]{:S(2)}, u32[]{:S(2)}) collective-permute-start(bf16[4,512,128]{2,1,0:T(8,128)(2,1)S(1)} %add.14.refs_2_), channel_id=1, source_target_pairs={{0,2},{1,3},{2,0},{3,1},{4,6},{5,7},{6,4},{7,5},{8,10},{9,11},{10,... | collective-permute-start | bytes 1572872 | tf_op jit(solution)/shard_map/ppermute | solution.py:319
  108.7 19.7 %collective-permute-start.7 = (bf16[4,512,128]{2,1,0:T(8,128)(2,1)S(1)}, bf16[4,512,128]{2,1,0:T(8,128)(2,1)S(1)}, u32[]{:S(2)}, u32[]{:S(2)}) collective-permute-start(bf16[4,512,128]{2,1,0:T(8,128)(2,1)S(1)} %add.15.refs_0_), channel_id=1, source_target_pairs={{0,2},{1,3},{2,0},{3,1},{4,6},{5,7},{6,4},{7,5},{8,10},{9,11},{10,... | collective-permute-start | bytes 1572872 | tf_op jit(solution)/shard_map/ppermute | solution.py:319
  118.2 14.2 %collective-permute-start.9 = (bf16[16,32,512]{2,1,0:T(8,128)(2,1)S(1)}, bf16[16,32,512]{2,1,0:T(8,128)(2,1)S(1)}, u32[]{:S(2)}, u32[]{:S(2)}) collective-permute-start(bf16[16,32,512]{2,1,0:T(8,128)(2,1)S(1)} %pack_other.3), channel_id=1, source_target_pairs={{0,18},{1,19},{2,16},{3,17},{4,22},{5,23},{6,20},{7,21},{8,26},{9,... | collective-permute-start | bytes 1572872 | tf_op jit(solution)/shard_map/ppermute | solution.py:331
where the time goes:
time: 175 us
  blocking collectives  79 us (45%)
  waiting for transfers between devices  40.9 us (23%)
  Pallas kernels  40 us (23%)
  starting transfers between devices  11.4 us (7%)
  local copies, waits for them, and re-layouts  2.22 us (1%)
    all_to_all x2, blocking collectives, local(): lax.all_to_all(responses, 'freq', 0, 0, tiled=True, axis_index_groups=pla...  40.2 us
    all_to_all x2, blocking collectives, local(): update = lax.all_to_all(truncated, 'freq', 0, 0, tiled=True)  38.7 us
    ppermute x8, waiting for transfers between devices, swap(): lax.ppermute(values, 'src', [(i, i ^ bit) for i in range(lax.axis_size('s...  32.4 us
    pallas_call x8, Pallas kernels, products(): pl.pallas_call(functools.partial(product_kernel, polarity, rels, build, l...  30.4 us
    ppermute x2, waiting for transfers between devices, outward(): return lax.ppermute(values, ('freq', 'src'), pairs)  8.53 us
    pallas_call x8, Pallas kernels, call(): pl.pallas_call(kernel, in_specs=[VMEM] * len(args) + [pl.BlockSpec(memory...  6 us
    ppermute x8, starting transfers between devices, swap(): lax.ppermute(values, 'src', [(i, i ^ bit) for i in range(lax.axis_size('s...  5.75 us
    ppermute x2, starting transfers between devices, outward(): return lax.ppermute(values, ('freq', 'src'), pairs)  5.69 us
  transfers between devices with their start and end apart: 10, of which 6 were waited for; matrix products, arithmetic and copies ran while one was open for 0% of the time, Pallas kernels for 9%

commit v1 on v0

v1 whole, which is shorter than its diff:
```python
import functools
import math

import jax
import jax.numpy as jnp
import numpy as np
from jax import lax
from jax.experimental import pallas as pl
from jax.experimental.pallas import tpu as pltpu
from jax.sharding import PartitionSpec as P

ITERS = 2
AHEAD = 4
TOGETHER = 2
CUTS = 2
TILE = 16
LANES = 128
MIB = 1024 * 1024
NT = (((1,), (1,)), ((), ()))
VMEM = pl.BlockSpec(memory_space=pltpu.VMEM)
BF = jnp.bfloat16
LIGHT = pl.CostEstimate(flops=1, bytes_accessed=1, transcendentals=0)


def mm(left, right):
    return jnp.dot(left, right, preferred_element_type=jnp.float32)


def nt(left, right):
    return lax.dot_general(left, right, NT, preferred_element_type=jnp.float32)


def split(values):
    high = values.astype(BF)
    low = (values - high.astype(values.dtype)).astype(BF)
    return high, low


def tables(columns, rows, freq_local, focal_block):
    plane_devices = columns * rows
    half = plane_devices * focal_block
    nfreq = 2 * plane_devices * freq_local
    packed = half * freq_local * 2
    pack = np.zeros((packed, packed), np.float32)
    for xy in range(plane_devices):
        for j in range(focal_block):
            for f in range(freq_local):
                for c in range(2):
                    row = ((xy * focal_block + j) * freq_local + f) * 2 + c
                    pack[row, ((f * 2 + c) * plane_devices + xy) * focal_block + j] = 1
    positions = np.arange(nfreq)
    phase = (np.outer(positions, positions) % nfreq) * (2.0 * math.pi / nfreq)
    cosine, sine = np.cos(phase), np.sin(phase)
    to_time = np.zeros((2, nfreq, nfreq, 2))
    to_time[0, :, :, 0] = cosine / nfreq
    to_time[0, :, :, 1] = -sine / nfreq
    to_time[1, :, :, 0] = sine / nfreq
    to_time[1, :, :, 1] = cosine / nfreq
    to_freq = np.zeros((nfreq, 2, 2, nfreq))
    to_freq[:, 0, 0, :] = cosine
    to_freq[:, 0, 1, :] = sine
    to_freq[:, 1, 0, :] = -sine
    to_freq[:, 1, 1, :] = cosine
    to_time = to_time.reshape(2 * nfreq, columns, 2, rows, freq_local * 2).transpose(0, 1, 3, 2, 4)
    to_time = to_time.reshape(2 * nfreq, 2 * nfreq).astype(np.float32)
    to_freq = to_freq.reshape(2 * nfreq, 2 * nfreq).astype(np.float32)
    return pack, to_time, to_freq


def pair(matrix):
    high = matrix.astype(BF)
    low = (matrix - high.astype(np.float32)).astype(BF)
    return np.stack([high, low])


def spread(wide_ref, update_ref):
    for slab in range(wide_ref.shape[0]):
        wide_ref[slab] = update_ref[:, slab * LANES : (slab + 1) * LANES].astype(jnp.float32)


def every(wide_ref, start, count, stride):
    slabs = [wide_ref[slab, pl.ds(start, count, stride), :] for slab in range(wide_ref.shape[0])]
    return jnp.concatenate(slabs, axis=1)


def wide(update):
    rows, width = update.shape
    return pltpu.VMEM((width // LANES, rows, LANES), jnp.float32)


def weights(polarity, half, block, initial_ref, update_ref, wide_ref, left_ref, right_ref):
    _, nfreq, focal, width = initial_ref.shape
    if update_ref is not None:
        spread(wide_ref, update_ref)
    for freq in range(nfreq):
        planes = []
        for plane in range(2):
            value = initial_ref[plane, freq].astype(jnp.float32)
            if update_ref is not None:
                value = value + every(wide_ref, 2 * freq + plane, focal, 2 * nfreq)
                value = value.astype(BF).astype(jnp.float32)
            value = value.reshape(focal // (2 * block), 2, block, width)
            planes.append([value[:, h].reshape(focal // 2, width) for h in range(2)])
        for place in range(2):
            real, imag = [jnp.where(half == place, low, high) for low, high in planes]
            here = slice(place * focal, (place + 1) * focal)
            left_ref[freq, :, here] = jnp.concatenate([real, imag], axis=0).T.astype(BF)
            right = jnp.concatenate([-polarity * imag, polarity * real], axis=0)
            right_ref[freq, :, here] = right.T.astype(BF)


def product_kernel(polarity, rels, build, tokens, focal_rows, where_ref, aperture_ref, reflection_ref, *refs):
    update_ref = wide_ref = None
    if build == "first":
        source_ref, *refs = refs
    elif build == "update":
        source_ref, update_ref, *refs = refs
    else:
        left_ref, right_ref, *refs = refs
    refs = refs[tokens:]
    outs, refs = refs[: len(rels)], refs[len(rels) :]
    if build:
        left_ref, right_ref, *refs = refs
    held_ref, sems, *refs = refs
    if build:
        initial_ref, initial_sem, *refs = refs
    if build == "update":
        (wide_ref,) = refs
    nfreq, width, _ = outs[0].shape
    pieces = [(place, freq) for place in range(len(rels)) for freq in range(nfreq)]
    blocks = [jnp.bitwise_xor(where_ref[0], rel) for rel in rels]

    def fetch(piece, plane):
        place, freq = pieces[piece]
        return pltpu.make_async_copy(
            reflection_ref.at[plane, freq, pl.ds(blocks[place] * width, width), :],
            held_ref.at[piece, plane],
            sems.at[piece, plane],
        )

    def begin(piece):
        if piece < len(pieces):
            for plane in range(2):
                fetch(piece, plane).start()

    if build:
        load = pltpu.make_async_copy(source_ref, initial_ref, initial_sem)
        load.start()
    for piece in range(AHEAD):
        begin(piece)
    if build:
        load.wait()
        weights(polarity, where_ref[1], focal_rows, initial_ref, update_ref, wide_ref, left_ref, right_ref)

    source_blocks, receiver_blocks = aperture_ref.shape
    strips = receiver_blocks // 4
    tall = width // strips
    wide_block = width // source_blocks

    def mask_of(place, strip):
        row = blocks[place] * strips + strip
        parts = [
            jnp.full((TILE, wide_block), aperture_ref[column, row].astype(jnp.float32)) for column in range(source_blocks)
        ]
        return jnp.concatenate(parts, axis=1).astype(BF)

    for low in range(0, len(pieces), TOGETHER):
        both = range(low, min(low + TOGETHER, len(pieces)))
        for piece in both:
            for plane in range(2):
                fetch(piece, plane).wait()
        for piece in both:
            begin(piece + AHEAD)
        for piece in both:
            place, freq = pieces[piece]
            masks = [mask_of(place, strip) for strip in range(strips)]
            masked = []
            for plane in range(2):
                parts = []
                for strip in range(strips):
                    part = held_ref[piece, plane, strip * tall : (strip + 1) * tall, :]
                    part = part.reshape(tall // TILE, TILE, width) * masks[strip][None]
                    parts.append(part.reshape(tall, width))
                masked.append(jnp.concatenate(parts, axis=0))
            total = mm(masked[0], left_ref[freq]) + mm(masked[1], right_ref[freq])
            outs[place][freq] = total.astype(BF)


def products(polarity, rels, focal_rows, where, aperture, reflection, initial, update=None, built=None, after=()):
    planes, nfreq, receivers, sources = reflection.shape
    focal = initial.shape[2]
    out = jax.ShapeDtypeStruct((nfreq, sources, 2 * focal), BF)
    scratch = [
        pltpu.VMEM((len(rels) * nfreq, 2, sources, sources), BF),
        pltpu.SemaphoreType.DMA((len(rels) * nfreq, 2)),
    ]
    outs = [out] * len(rels)
    anywhere = pl.BlockSpec(memory_space=pl.ANY)
    smem = pl.BlockSpec(memory_space=pltpu.SMEM)
    if built is not None:
        build, extra, specs = "", list(built), [VMEM] * 2
    else:
        outs += [out] * 2
        scratch += [pltpu.VMEM(initial.shape, BF), pltpu.SemaphoreType.DMA(())]
        if update is None:
            build, extra, specs = "first", [initial], [anywhere]
        else:
            build, extra, specs = "update", [initial, update], [anywhere, VMEM]
            scratch.append(wide(update))
    return pl.pallas_call(
        functools.partial(product_kernel, polarity, rels, build, len(after), focal_rows),
        in_specs=[smem, smem, anywhere] + specs + [anywhere] * len(after),
        out_specs=[VMEM] * len(outs),
        scratch_shapes=scratch,
        out_shape=outs,
        compiler_params=pltpu.CompilerParams(vmem_limit_bytes=46 * MIB),
        cost_estimate=LIGHT,
        name="products",
    )(where, aperture, reflection, *extra, *after)


def call(kernel, name, outs, *args, after=()):
    return pl.pallas_call(
        kernel,
        in_specs=[VMEM] * len(args) + [pl.BlockSpec(memory_space=pl.ANY)] * len(after),
        out_specs=[VMEM] * len(outs),
        out_shape=[jax.ShapeDtypeStruct(shape, BF) for shape in outs],
        compiler_params=pltpu.CompilerParams(vmem_limit_bytes=16 * MIB),
        cost_estimate=LIGHT,
        name=name,
    )(*args, *after)


def add_kernel(place, tokens, mine_ref, core_ref, *refs):
    outs = refs[tokens:]
    lanes = outs[0].shape[2]
    here = slice(place * lanes, (place + 1) * lanes)
    for index, out_ref in enumerate(outs):
        count = out_ref.shape[0]
        some = slice(index * count, (index + 1) * count)
        total = mine_ref[some, :, here].astype(jnp.float32) + core_ref[some, :, here].astype(jnp.float32)
        out_ref[...] = total.astype(BF)


def total_kernel(index, mine_ref, core_ref, far_ref, *refs):
    out_ref = refs[-1]
    count, _, lanes = out_ref.shape
    some = slice(index * count, (index + 1) * count)
    total = mine_ref[some, :, lanes:].astype(jnp.float32) + core_ref[some, :, lanes:].astype(jnp.float32)
    out_ref[...] = (total + far_ref[...].astype(jnp.float32)).astype(BF)


def pack_own_kernel(where_ref, pack_ref, mine_ref, core_ref, far_ref, *refs):
    *outer_refs, out_ref = refs
    nfreq, width, lanes = far_ref.shape
    devices, rows, _ = out_ref.shape
    rows = rows // 2
    half = where_ref[1]
    own = []
    for f in range(nfreq):
        total = mine_ref[f, :, :lanes].astype(jnp.float32) + core_ref[f, :, :lanes].astype(jnp.float32)
        own.append((total + far_ref[f].astype(jnp.float32)).astype(BF))
    outer = [ref[f] for ref in outer_refs for f in range(ref.shape[0])]
    for h, parts in ((half, own), (1 - half, outer)):
        packed = nt(pack_ref[...], jnp.concatenate(parts, axis=1)).astype(BF)
        out_ref[:, pl.ds(pl.multiple_of(h * rows, rows), rows), :] = packed.reshape(devices, rows, width)


def pack_own(where, shape, *args):
    return pl.pallas_call(
        pack_own_kernel,
        in_specs=[pl.BlockSpec(memory_space=pltpu.SMEM)] + [VMEM] * len(args),
        out_specs=VMEM,
        out_shape=jax.ShapeDtypeStruct(shape, BF),
        compiler_params=pltpu.CompilerParams(vmem_limit_bytes=16 * MIB),
        cost_estimate=LIGHT,
        name="pack_own",
    )(where, *args)


def window_kernel(dft_ref, onsets_ref, traces_ref, out_ref):
    focal, width = onsets_ref.shape
    devices, rows, _ = traces_ref.shape
    group = rows // (2 * focal)
    nfreq = dft_ref.shape[1] // 2
    step = lax.broadcasted_iota(jnp.int32, (nfreq, width), 0)
    traces = traces_ref[...].astype(jnp.float32).reshape(2 * devices, focal, group, width)
    results = []
    for j in range(focal):
        column = traces[:, j].reshape(2 * nfreq, width).astype(BF)
        time = mm(dft_ref[0], column) + mm(dft_ref[1], column)
        keep = step < onsets_ref[j : j + 1, :]
        keep = jnp.concatenate([keep, keep], axis=0)
        high, low = split(jnp.where(keep, time, 0.0))
        back = mm(dft_ref[2], high) + mm(dft_ref[2], low) + mm(dft_ref[3], high)
        results.append(back.reshape(2 * devices, group, width))
    out_ref[...] = jnp.stack(results, axis=1).reshape(out_ref.shape).astype(BF)


def final_kernel(initial_ref, update_ref, out_ref, wide_ref, block_ref, sems):
    planes, nfreq, focal, _ = initial_ref.shape
    spread(wide_ref, update_ref)
    copies = []
    for freq in range(nfreq):
        for plane in range(planes):
            value = initial_ref[plane, freq].astype(jnp.float32)
            value = value + every(wide_ref, planes * freq + plane, focal, planes * nfreq)
            block_ref[plane, freq] = value.astype(BF)
            copy = pltpu.make_async_copy(
                block_ref.at[plane, freq], out_ref.at[plane, freq], sems.at[plane, freq]
            )
            copy.start()
            copies.append(copy)
    for copy in copies:
        copy.wait()


def finish(initial, update):
    planes, nfreq, focal, sources = initial.shape
    return pl.pallas_call(
        final_kernel,
        in_specs=[VMEM, VMEM],
        out_specs=pl.BlockSpec(memory_space=pl.ANY),
        scratch_shapes=[
            wide(update),
            pltpu.VMEM(initial.shape, BF),
            pltpu.SemaphoreType.DMA((planes, nfreq)),
        ],
        out_shape=jax.ShapeDtypeStruct(initial.shape, BF),
        compiler_params=pltpu.CompilerParams(vmem_limit_bytes=16 * MIB),
        name="finish",
    )(initial, update)


def swap(values, bit):
    return lax.ppermute(values, "src", [(i, i ^ bit) for i in range(lax.axis_size("src"))])


def outward(values, columns, rows):
    pairs = []
    for x in range(columns):
        for h in range(2):
            for y in range(rows):
                for s in range(4):
                    here = ((x * 2 + h) * rows + y) * 4 + s
                    there = ((x * 2 + 1 - h) * rows + y) * 4 + (s ^ 2)
                    pairs.append((here, there))
    return lax.ppermute(values, ("freq", "src"), pairs)


def local(reflection, aperture, initial, onsets):
    planes, freq_local, receivers, sources = reflection.shape
    devices = lax.axis_size("freq")
    focal = initial.shape[2]
    focal_block = focal // devices
    columns = rows = math.isqrt(devices // 2)
    pack, to_time, to_freq = tables(columns, rows, freq_local, focal_block)
    pack = jnp.asarray(pack, BF)
    dft = jnp.asarray(np.concatenate([pair(to_time), pair(to_freq)]))
    half = (lax.axis_index("freq") // rows) % 2
    where = jnp.stack([lax.axis_index("src"), half]).astype(jnp.int32)
    plane_groups = [
        [(x * 2 + h) * rows + y for x in range(columns) for y in range(rows)] for h in range(2)
    ]
    block_rows = focal_block * freq_local * planes
    part = (freq_local, sources, focal)
    cut = (freq_local // CUTS, sources, focal)

    update = None
    for iteration in range(ITERS):
        polarity = 1.0 if iteration % 2 == 0 else -1.0

        def respond(rels, **more):
            return products(polarity, rels, rows * focal_block, where, aperture.T, reflection, initial, **more)

        send_near, send_far, left, right = respond((1, 3), update=update)
        core_near, core_far = swap(send_near, 1), swap(send_far, 1)
        (near,) = respond((0,), built=(left, right))
        totals = call(functools.partial(add_kernel, 1, 0), "add", [cut] * CUTS, near, core_near)
        far_other = [swap(total, 2) for total in totals]
        (remote,) = respond((2,), built=(left, right), after=totals)
        (total,) = call(functools.partial(add_kernel, 0, 1), "add", [part], remote, core_far, after=far_other[:1])
        far_own = swap(total, 2)
        outer = []
        for index, far in enumerate(far_other):
            (other,) = call(
                functools.partial(total_kernel, index), "total", [cut], remote, core_far, far, after=(total,)
            )
            outer.append(outward(other, columns, rows))
        shape = (devices // 2, 2 * block_rows, sources)
        responses = pack_own(where, shape, pack, near, core_near, far_own, *outer)
        traces = lax.all_to_all(responses, "freq", 0, 0, tiled=True, axis_index_groups=plane_groups)
        (truncated,) = call(
            window_kernel, "window", [(devices, block_rows, sources)], dft, onsets, traces
        )
        update = lax.all_to_all(truncated, "freq", 0, 0, tiled=True)
        update = update.reshape(devices * block_rows, sources)
    return finish(initial, update)


def solution(mesh):
    placed = (
        P(None, "freq", None, "src"),
        P(None, "src"),
        P(None, "freq", None, "src"),
        P("freq", "src"),
    )
    return jax.shard_map(
        local, mesh=mesh, in_specs=placed, out_specs=P(None, "freq", None, "src"), check_vma=False
    )
```

time: 175 us -> 169 us (0.966)
  waiting for transfers between devices: 40.9 us -> 27.8 us
  blocking collectives: 79 us -> 87.4 us
  Pallas kernels: 40 us -> 34.9 us
  starting transfers between devices: 11.4 us -> 16.2 us
    ppermute x8 -> x10, waiting for transfers between devices: 32.4 us -> 14.4 us  [swap(): lax.ppermute(values, 'src', [(i, i ^ bit) for i in range(lax.axis_size('s...]
    all_to_all x2, blocking collectives: 38.7 us -> 43.8 us  [local(): update = lax.all_to_all(truncated, 'freq', 0, 0, tiled=True)]
    pallas_call x8 -> x6, Pallas kernels: 30.4 us -> 25.3 us  [products(): pl.pallas_call(functools.partial(product_kernel, polarity, rels, build, l...]
    ppermute x2 -> x4, waiting for transfers between devices: 8.53 us -> 13.4 us  [outward(): return lax.ppermute(values, ('freq', 'src'), pairs)]
    all_to_all x2, blocking collectives: 40.2 us -> 43.6 us  [local(): lax.all_to_all(responses, 'freq', 0, 0, tiled=True, axis_index_groups=pla...]
    ppermute x2 -> x4, starting transfers between devices: 5.69 us -> 8.1 us  [outward(): return lax.ppermute(values, ('freq', 'src'), pairs)]
    ppermute x8 -> x10, starting transfers between devices: 5.75 us -> 8.09 us  [swap(): lax.ppermute(values, 'src', [(i, i ^ bit) for i in range(lax.axis_size('s...]
    pallas_call x8 -> x10, Pallas kernels: 6 us -> 5.45 us  [call(): pl.pallas_call(kernel, in_specs=[VMEM] * len(args) + [pl.BlockSpec(memory...]
  transfers between devices with their start and end apart: 10 -> 14, of which waited for: 6 -> 10; matrix products, arithmetic and copies ran while one was open for 0% -> 0% of each run, Pallas kernels for 9% -> 9%
where the time goes in v1:
time: 169 us
  blocking collectives  87.4 us (52%)
  Pallas kernels  34.9 us (21%)
  waiting for transfers between devices  27.8 us (16%)
  starting transfers between devices  16.2 us (10%)
  local copies, waits for them, and re-layouts  1.92 us (1%)
    all_to_all x2, blocking collectives, local(): update = lax.all_to_all(truncated, 'freq', 0, 0, tiled=True)  43.8 us
    all_to_all x2, blocking collectives, local(): lax.all_to_all(responses, 'freq', 0, 0, tiled=True, axis_index_groups=pla...  43.6 us
    pallas_call x6, Pallas kernels, products(): pl.pallas_call(functools.partial(product_kernel, polarity, rels, build, l...  25.3 us
    ppermute x10, waiting for transfers between devices, swap(): lax.ppermute(values, 'src', [(i, i ^ bit) for i in range(lax.axis_size('s...  14.4 us
    ppermute x4, waiting for transfers between devices, outward(): return lax.ppermute(values, ('freq', 'src'), pairs)  13.4 us
    ppermute x4, starting transfers between devices, outward(): return lax.ppermute(values, ('freq', 'src'), pairs)  8.1 us
    ppermute x10, starting transfers between devices, swap(): lax.ppermute(values, 'src', [(i, i ^ bit) for i in range(lax.axis_size('s...  8.09 us
    pallas_call x10, Pallas kernels, call(): pl.pallas_call(kernel, in_specs=[VMEM] * len(args) + [pl.BlockSpec(memory...  5.45 us
  transfers between devices with their start and end apart: 14, of which 10 were waited for; matrix products, arithmetic and copies ran while one was open for 0% of the time, Pallas kernels for 9%

profile of v1, /device:TPU:0, one launch (start us, length us, event | category | flops | bytes accessed | tf_op | source)
XLA Modules:
  0.0 168.6 jit_solution(15426884087404999391)
XLA Ops:
  0.1 1.2 copy-done
  1.3 0.7 copy-done.4
  2.0 5.4 %products.6 = (bf16[4,512,256]{2,1,0:T(8,128)(2,1)S(1)}, bf16[4,512,256]{2,1,0:T(8,128)(2,1)S(1)}, bf16[4,512,256]{2,1,0:T(8,128)(2,1)S(1)}, bf16[4,512,256]{2,1,0:T(8,128)(2,1)S(1)}) custom-call(s32[2]{0:T(128)S(1)} %pad_add_fusion.where_ref, s32[4,16]{1,0:T(4,128)S(1)} %bitcast.7, bf16[2,4,2048,512]{3,2,1,0:T(8,128)(2,1)} %reflection_ref.11, ...), custom_call_target="tpu_custom_call" | custom-call | flops 1 | bytes 1 | tf_op jit(solution)/shard_map/products/pallas_call | solution.py:210
  7.4 0.1 collective-permute-start
  7.5 0.5 collective-permute-start.1
  8.0 3.6 %products.7.mine_ref = bf16[4,512,256]{2,1,0:T(8,128)(2,1)S(1)} custom-call(s32[2]{0:T(128)S(1)} %pad_add_fusion.where_ref, s32[4,16]{1,0:T(4,128)S(1)} %bitcast.8, bf16[2,4,2048,512]{3,2,1,0:T(8,128)(2,1)} %reflection_ref.11, bf16[4,512,256]{2,1,0:T(8,128)(2,1)S(1)} %get-tuple-element.17.refs_0_, bf16[4,512,256]{2,1,0:T(8,128)(2,1)S(1)} %get-tuple-element.18.refs_1_), custom_call_target="tpu_custom_call" | custom-call | flops 1 | bytes 1 | tf_op jit(solution)/shard_map/products/pallas_call | solution.py:210
  11.7 0.1 add.12
  11.8 2.1 %collective-permute-start.2 = (bf16[2,512,128]{2,1,0:T(8,128)(2,1)S(1)}, bf16[2,512,128]{2,1,0:T(8,128)(2,1)S(1)}, u32[]{:S(2)}, u32[]{:S(2)}) collective-permute-start(bf16[2,512,128]{2,1,0:T(8,128)(2,1)S(1)} %get-tuple-element.20.refs_2_), channel_id=1, source_target_pairs={{0,2},{1,3},{2,0},{3,1},{4,6},{5,7},{6,4},{7,5},{8,10},{9,11},{10,... | collective-permute-start | bytes 786440 | tf_op jit(solution)/shard_map/ppermute | solution.py:336
  13.9 3.6 %products.8.mine_ref = bf16[4,512,256]{2,1,0:T(8,128)(2,1)S(1)} custom-call(s32[2]{0:T(128)S(1)} %pad_add_fusion.where_ref, s32[4,16]{1,0:T(4,128)S(1)} %bitcast.9, bf16[2,4,2048,512]{3,2,1,0:T(8,128)(2,1)} %reflection_ref.11, bf16[4,512,256]{2,1,0:T(8,128)(2,1)S(1)} %get-tuple-element.17.refs_0_, bf16[4,512,256]{2,1,0:T(8,128)(2,1)S(1)} %get-tuple-element.18.refs_1_, ...), custom_call_target="tpu_custom_call" | custom-call | flops 1 | bytes 1 | tf_op jit(solution)/shard_map/products/pallas_call | solution.py:210
  17.5 0.1 collective-permute-start.5
  17.6 3.2 %collective-permute-done.2.refs_0_.far_ref = bf16[2,512,128]{2,1,0:T(8,128)(2,1)S(1)} collective-permute-done((bf16[2,512,128]{2,1,0:T(8,128)(2,1)S(1)}, bf16[2,512,128]{2,1,0:T(8,128)(2,1)S(1)}, u32[]{:S(2)}, u32[]{:S(2)}) %collective-permute-start.2) | collective-permute-done | bytes 262176 | tf_op jit(solution)/shard_map/ppermute | solution.py:336
  20.8 0.1 add.13.refs_0_
  20.9 2.3 %collective-permute-start.3 = (bf16[4,512,128]{2,1,0:T(8,128)(2,1)S(1)}, bf16[4,512,128]{2,1,0:T(8,128)(2,1)S(1)}, u32[]{:S(2)}, u32[]{:S(2)}) collective-permute-start(bf16[4,512,128]{2,1,0:T(8,128)(2,1)S(1)} %add.13.refs_0_), channel_id=1, source_target_pairs={{0,2},{1,3},{2,0},{3,1},{4,6},{5,7},{6,4},{7,5},{8,10},{9,11},{10,... | collective-permute-start | bytes 1572872 | tf_op jit(solution)/shard_map/ppermute | solution.py:336
  23.2 0.1 total.4
  23.3 2.3 %collective-permute-start.4 = (bf16[2,512,128]{2,1,0:T(8,128)(2,1)S(1)}, bf16[2,512,128]{2,1,0:T(8,128)(2,1)S(1)}, u32[]{:S(2)}, u32[]{:S(2)}) collective-permute-start(bf16[2,512,128]{2,1,0:T(8,128)(2,1)S(1)} %total.4), channel_id=1, source_target_pairs={{0,18},{1,19},{2,16},{3,17},{4,22},{5,23},{6,20},{7,21},{8,26},{9,... | collective-permute-start | bytes 786440 | tf_op jit(solution)/shard_map/ppermute | solution.py:348
  25.6 1.2 collective-permute-done.5.far_ref
  26.8 0.1 total.5
  26.9 4.1 %collective-permute-start.6 = (bf16[2,512,128]{2,1,0:T(8,128)(2,1)S(1)}, bf16[2,512,128]{2,1,0:T(8,128)(2,1)S(1)}, u32[]{:S(2)}, u32[]{:S(2)}) collective-permute-start(bf16[2,512,128]{2,1,0:T(8,128)(2,1)S(1)} %total.5), channel_id=1, source_target_pairs={{0,18},{1,19},{2,16},{3,17},{4,22},{5,23},{6,20},{7,21},{8,26},{9,... | collective-permute-start | bytes 786440 | tf_op jit(solution)/shard_map/ppermute | solution.py:348
  31.0 0.8 collective-permute-done.4.refs_0_
  31.7 4.9 %collective-permute-done.6.refs_1_ = bf16[2,512,128]{2,1,0:T(8,128)(2,1)S(1)} collective-permute-done((bf16[2,512,128]{2,1,0:T(8,128)(2,1)S(1)}, bf16[2,512,128]{2,1,0:T(8,128)(2,1)S(1)}, u32[]{:S(2)}, u32[]{:S(2)}) %collective-permute-start.6) | collective-permute-done | bytes 262176 | tf_op jit(solution)/shard_map/ppermute | solution.py:348
  36.6 0.7 collective-permute-done.3.far_ref
  37.3 1.3 pack_own.2
  38.6 23.5 %all_to_all.20.traces_ref = bf16[16,64,512]{2,1,0:T(8,128)(2,1)S(1)} all-to-all(bf16[16,64,512]{2,1,0:T(8,128)(2,1)S(1)} %pack_own.2), channel_id=1, replica_groups={{0,4,8,12,32,36,40,44,64,68,72,76,96,100,104,108},{16,20,24,28,48,52,56..., dimensions={0} | all-to-all | bytes 2097152 | tf_op jit(solution)/shard_map/all_to_all | solution.py:392
  62.1 2.3 %window.2 = bf16[32,32,512]{2,1,0:T(8,128)(2,1)S(1)} custom-call(bf16[4,256,256]{2,1,0:T(8,128)(2,1)S(1)} %copy-done.2, s32[4,512]{1,0:T(4,128)S(1)} %copy-done.5, bf16[16,64,512]{2,1,0:T(8,128)(2,1)S(1)} %all_to_all.20.traces_ref), custom_call_target="tpu_custom_call" | custom-call | flops 1 | bytes 1 | tf_op jit(solution)/shard_map/window/pallas_call | solution.py:223
  64.4 23.7 %all_to_all.21 = bf16[32,32,512]{2,1,0:T(8,128)(2,1)S(1)} all-to-all(bf16[32,32,512]{2,1,0:T(8,128)(2,1)S(1)} %window.2), channel_id=1, replica_groups=mesh['freq'=32,'src'=4] {'freq'}, dimensions={0} | all-to-all | bytes 2097152 | tf_op jit(solution)/shard_map/all_to_all | solution.py:396
  88.1 5.4 %products.9 = (bf16[4,512,256]{2,1,0:T(8,128)(2,1)S(1)}, bf16[4,512,256]{2,1,0:T(8,128)(2,1)S(1)}, bf16[4,512,256]{2,1,0:T(8,128)(2,1)S(1)}, bf16[4,512,256]{2,1,0:T(8,128)(2,1)S(1)}) custom-call(s32[2]{0:T(128)S(1)} %pad_add_fusion.where_ref, s32[4,16]{1,0:T(4,128)S(1)} %bitcast.10, bf16[2,4,2048,512]{3,2,1,0:T(8,128)(2,1)} %reflection_ref.11, ...), custom_call_target="tpu_custom_call" | custom-call | flops 1 | bytes 1 | tf_op jit(solution)/shard_map/products/pallas_call | solution.py:210
  93.7 0.5 collective-permute-start.8
  94.1 3.6 %products.10.mine_ref = bf16[4,512,256]{2,1,0:T(8,128)(2,1)S(1)} custom-call(s32[2]{0:T(128)S(1)} %pad_add_fusion.where_ref, s32[4,16]{1,0:T(4,128)S(1)} %bitcast.11, bf16[2,4,2048,512]{3,2,1,0:T(8,128)(2,1)} %reflection_ref.11, bf16[4,512,256]{2,1,0:T(8,128)(2,1)S(1)} %get-tuple-element.23.refs_0_, bf16[4,512,256]{2,1,0:T(8,128)(2,1)S(1)} %get-tuple-element.24.refs_1_), custom_call_target="tpu_custom_call" | custom-call | flops 1 | bytes 1 | tf_op jit(solution)/shard_map/products/pallas_call | solution.py:210
  97.8 0.1 add.14
  97.9 0.5 collective-permute-start.9
  98.5 3.6 %products.11.mine_ref = bf16[4,512,256]{2,1,0:T(8,128)(2,1)S(1)} custom-call(s32[2]{0:T(128)S(1)} %pad_add_fusion.where_ref, s32[4,16]{1,0:T(4,128)S(1)} %bitcast.12, bf16[2,4,2048,512]{3,2,1,0:T(8,128)(2,1)} %reflection_ref.11, bf16[4,512,256]{2,1,0:T(8,128)(2,1)S(1)} %get-tuple-element.23.refs_0_, bf16[4,512,256]{2,1,0:T(8,128)(2,1)S(1)} %get-tuple-element.24.refs_1_, ...), custom_call_target="tpu_custom_call" | custom-call | flops 1 | bytes 1 | tf_op jit(solution)/shard_map/products/pallas_call | solution.py:210
  102.1 1.6 collective-permute-start.12
  103.7 3.4 %collective-permute-done.9.refs_0_.far_ref = bf16[2,512,128]{2,1,0:T(8,128)(2,1)S(1)} collective-permute-done((bf16[2,512,128]{2,1,0:T(8,128)(2,1)S(1)}, bf16[2,512,128]{2,1,0:T(8,128)(2,1)S(1)}, u32[]{:S(2)}, u32[]{:S(2)}) %collective-permute-start.9) | collective-permute-done | bytes 262176 | tf_op jit(solution)/shard_map/ppermute | solution.py:336
  107.2 0.1 add.15.refs_0_
  107.3 0.2 collective-permute-start.10
  107.5 0.1 total.6
  107.6 1.3 collective-permute-start.11
  108.9 3.9 %collective-permute-done.12.far_ref = bf16[2,512,128]{2,1,0:T(8,128)(2,1)S(1)} collective-permute-done((bf16[2,512,128]{2,1,0:T(8,128)(2,1)S(1)}, bf16[2,512,128]{2,1,0:T(8,128)(2,1)S(1)}, u32[]{:S(2)}, u32[]{:S(2)}) %collective-permute-start.12) | collective-permute-done | bytes 262176 | tf_op jit(solution)/shard_map/ppermute | solution.py:336
  112.8 0.1 total.7
  112.9 0.5 collective-permute-start.13
  113.4 2.5 %collective-permute-done.11.refs_0_ = bf16[2,512,128]{2,1,0:T(8,128)(2,1)S(1)} collective-permute-done((bf16[2,512,128]{2,1,0:T(8,128)(2,1)S(1)}, bf16[2,512,128]{2,1,0:T(8,128)(2,1)S(1)}, u32[]{:S(2)}, u32[]{:S(2)}) %collective-permute-start.11) | collective-permute-done | bytes 262176 | tf_op jit(solution)/shard_map/ppermute | solution.py:348
  115.8 5.3 %collective-permute-done.13.refs_1_ = bf16[2,512,128]{2,1,0:T(8,128)(2,1)S(1)} collective-permute-done((bf16[2,512,128]{2,1,0:T(8,128)(2,1)S(1)}, bf16[2,512,128]{2,1,0:T(8,128)(2,1)S(1)}, u32[]{:S(2)}, u32[]{:S(2)}) %collective-permute-start.13) | collective-permute-done | bytes 262176 | tf_op jit(solution)/shard_map/ppermute | solution.py:348
  121.2 2.0 %collective-permute-done.10.far_ref = bf16[4,512,128]{2,1,0:T(8,128)(2,1)S(1)} collective-permute-done((bf16[4,512,128]{2,1,0:T(8,128)(2,1)S(1)}, bf16[4,512,128]{2,1,0:T(8,128)(2,1)S(1)}, u32[]{:S(2)}, u32[]{:S(2)}) %collective-permute-start.10) | collective-permute-done | bytes 524320 | tf_op jit(solution)/shard_map/ppermute | solution.py:336
  123.2 1.3 pack_own.3
  124.5 20.1 %all_to_all.22.traces_ref = bf16[16,64,512]{2,1,0:T(8,128)(2,1)S(1)} all-to-all(bf16[16,64,512]{2,1,0:T(8,128)(2,1)S(1)} %pack_own.3), channel_id=1, replica_groups={{0,4,8,12,32,36,40,44,64,68,72,76,96,100,104,108},{16,20,24,28,48,52,56..., dimensions={0} | all-to-all | bytes 2097152 | tf_op jit(solution)/shard_map/all_to_all | solution.py:392
  144.6 2.3 %window.3 = bf16[32,32,512]{2,1,0:T(8,128)(2,1)S(1)} custom-call(bf16[4,256,256]{2,1,0:T(8,128)(2,1)S(1)} %copy-done.2, s32[4,512]{1,0:T(4,128)S(1)} %copy-done.5, bf16[16,64,512]{2,1,0:T(8,128)(2,1)S(1)} %all_to_all.22.traces_ref), custom_call_target="tpu_custom_call" | custom-call | flops 1 | bytes 1 | tf_op jit(solution)/shard_map/window/pallas_call | solution.py:223
  146.9 20.1 %all_to_all.23 = bf16[32,32,512]{2,1,0:T(8,128)(2,1)S(1)} all-to-all(bf16[32,32,512]{2,1,0:T(8,128)(2,1)S(1)} %window.3), channel_id=1, replica_groups=mesh['freq'=32,'src'=4] {'freq'}, dimensions={0} | all-to-all | bytes 2097152 | tf_op jit(solution)/shard_map/all_to_all | solution.py:396
  167.0 1.5 finish.1
  (16 shorter events, 0.2 us)
Async XLA Ops:
  0.1 1.2 copy-start
  1.3 0.7 copy-start.4
  7.4 4.2 %collective-permute-start = (bf16[4,512,256]{2,1,0:T(8,128)(2,1)S(1)}, bf16[4,512,256]{2,1,0:T(8,128)(2,1)S(1)}, u32[]{:S(2)}, u32[]{:S(2)}) collective-permute-start(bf16[4,512,256]{2,1,0:T(8,128)(2,1)S(1)} %get-tuple-element.19), channel_id=1, source_target_pairs={{0,1},{1,0},{2,3},{3,2},{4,5},{5,4},{6,7},{7,6},{8,9},{9,8},{10,11... | collective-permute-start | bytes 3145736 | tf_op jit(solution)/shard_map/ppermute | solution.py:336
  7.5 10.1 %collective-permute-start.1 = (bf16[4,512,256]{2,1,0:T(8,128)(2,1)S(1)}, bf16[4,512,256]{2,1,0:T(8,128)(2,1)S(1)}, u32[]{:S(2)}, u32[]{:S(2)}) collective-permute-start(bf16[4,512,256]{2,1,0:T(8,128)(2,1)S(1)} %get-tuple-element.22), channel_id=1, source_target_pairs={{0,1},{1,0},{2,3},{3,2},{4,5},{5,4},{6,7},{7,6},{8,9},{9,8},{10,11... | collective-permute-start | bytes 3145736 | tf_op jit(solution)/shard_map/ppermute | solution.py:336
  11.6 25.7 %copy-start.3 = (bf16[512,512]{1,0:T(8,128)(2,1)S(1)}, bf16[512,512]{1,0:T(8,128)(2,1)}, u32[]{:S(2)}) copy-start(bf16[512,512]{1,0:T(8,128)(2,1)} %constant.39.clone.pack_ref) | copy-start | bytes 1572868
  11.8 9.0 %collective-permute-start.2 = (bf16[2,512,128]{2,1,0:T(8,128)(2,1)S(1)}, bf16[2,512,128]{2,1,0:T(8,128)(2,1)S(1)}, u32[]{:S(2)}, u32[]{:S(2)}) collective-permute-start(bf16[2,512,128]{2,1,0:T(8,128)(2,1)S(1)} %get-tuple-element.20.refs_2_), channel_id=1, source_target_pairs={{0,2},{1,3},{2,0},{3,1},{4,6},{5,7},{6,4},{7,5},{8,10},{9,11},{10,... | collective-permute-start | bytes 786440 | tf_op jit(solution)/shard_map/ppermute | solution.py:336
  13.9 48.2 %copy-start.2 = (bf16[4,256,256]{2,1,0:T(8,128)(2,1)S(1)}, bf16[4,256,256]{2,1,0:T(8,128)(2,1)}, u32[]{:S(2)}) copy-start(bf16[4,256,256]{2,1,0:T(8,128)(2,1)} %constant.40.clone.dft_ref) | copy-start | bytes 1572868
  13.9 48.2 %copy-start.5 = (s32[4,512]{1,0:T(4,128)S(1)}, s32[4,512]{1,0:T(4,128)}, u32[]{:S(2)}) copy-start(s32[4,512]{1,0:T(4,128)} %onsets_ref.3) | copy-start | bytes 24580
  13.9 74.2 %copy-start.1 = (bf16[2,4,128,512]{3,2,1,0:T(8,128)(2,1)S(1)}, bf16[2,4,128,512]{3,2,1,0:T(8,128)(2,1)}, u32[]{:S(2)}) copy-start(bf16[2,4,128,512]{3,2,1,0:T(8,128)(2,1)} %initial_ref.1) | copy-start | bytes 3145732
  17.5 9.3 %collective-permute-start.5 = (bf16[2,512,128]{2,1,0:T(8,128)(2,1)S(1)}, bf16[2,512,128]{2,1,0:T(8,128)(2,1)S(1)}, u32[]{:S(2)}, u32[]{:S(2)}) collective-permute-start(bf16[2,512,128]{2,1,0:T(8,128)(2,1)S(1)} %get-tuple-element.21.refs_3_), channel_id=1, source_target_pairs={{0,2},{1,3},{2,0},{3,1},{4,6},{5,7},{6,4},{7,5},{8,10},{9,11},{10,... | collective-permute-start | bytes 786440 | tf_op jit(solution)/shard_map/ppermute | solution.py:336
  20.9 16.4 %collective-permute-start.3 = (bf16[4,512,128]{2,1,0:T(8,128)(2,1)S(1)}, bf16[4,512,128]{2,1,0:T(8,128)(2,1)S(1)}, u32[]{:S(2)}, u32[]{:S(2)}) collective-permute-start(bf16[4,512,128]{2,1,0:T(8,128)(2,1)S(1)} %add.13.refs_0_), channel_id=1, source_target_pairs={{0,2},{1,3},{2,0},{3,1},{4,6},{5,7},{6,4},{7,5},{8,10},{9,11},{10,... | collective-permute-start | bytes 1572872 | tf_op jit(solution)/shard_map/ppermute | solution.py:336
  23.3 8.4 %collective-permute-start.4 = (bf16[2,512,128]{2,1,0:T(8,128)(2,1)S(1)}, bf16[2,512,128]{2,1,0:T(8,128)(2,1)S(1)}, u32[]{:S(2)}, u32[]{:S(2)}) collective-permute-start(bf16[2,512,128]{2,1,0:T(8,128)(2,1)S(1)} %total.4), channel_id=1, source_target_pairs={{0,18},{1,19},{2,16},{3,17},{4,22},{5,23},{6,20},{7,21},{8,26},{9,... | collective-permute-start | bytes 786440 | tf_op jit(solution)/shard_map/ppermute | solution.py:348
  26.9 9.7 %collective-permute-start.6 = (bf16[2,512,128]{2,1,0:T(8,128)(2,1)S(1)}, bf16[2,512,128]{2,1,0:T(8,128)(2,1)S(1)}, u32[]{:S(2)}, u32[]{:S(2)}) collective-permute-start(bf16[2,512,128]{2,1,0:T(8,128)(2,1)S(1)} %total.5), channel_id=1, source_target_pairs={{0,18},{1,19},{2,16},{3,17},{4,22},{5,23},{6,20},{7,21},{8,26},{9,... | collective-permute-start | bytes 786440 | tf_op jit(solution)/shard_map/ppermute | solution.py:348
  93.6 4.2 %collective-permute-start.7 = (bf16[4,512,256]{2,1,0:T(8,128)(2,1)S(1)}, bf16[4,512,256]{2,1,0:T(8,128)(2,1)S(1)}, u32[]{:S(2)}, u32[]{:S(2)}) collective-permute-start(bf16[4,512,256]{2,1,0:T(8,128)(2,1)S(1)} %get-tuple-element.25), channel_id=1, source_target_pairs={{0,1},{1,0},{2,3},{3,2},{4,5},{5,4},{6,7},{7,6},{8,9},{9,8},{10,11... | collective-permute-start | bytes 3145736 | tf_op jit(solution)/shard_map/ppermute | solution.py:336
  93.7 10.1 %collective-permute-start.8 = (bf16[4,512,256]{2,1,0:T(8,128)(2,1)S(1)}, bf16[4,512,256]{2,1,0:T(8,128)(2,1)S(1)}, u32[]{:S(2)}, u32[]{:S(2)}) collective-permute-start(bf16[4,512,256]{2,1,0:T(8,128)(2,1)S(1)} %get-tuple-element.28), channel_id=1, source_target_pairs={{0,1},{1,0},{2,3},{3,2},{4,5},{5,4},{6,7},{7,6},{8,9},{9,8},{10,11... | collective-permute-start | bytes 3145736 | tf_op jit(solution)/shard_map/ppermute | solution.py:336
  97.9 9.2 %collective-permute-start.9 = (bf16[2,512,128]{2,1,0:T(8,128)(2,1)S(1)}, bf16[2,512,128]{2,1,0:T(8,128)(2,1)S(1)}, u32[]{:S(2)}, u32[]{:S(2)}) collective-permute-start(bf16[2,512,128]{2,1,0:T(8,128)(2,1)S(1)} %get-tuple-element.26.refs_2_), channel_id=1, source_target_pairs={{0,2},{1,3},{2,0},{3,1},{4,6},{5,7},{6,4},{7,5},{8,10},{9,11},{10,... | collective-permute-start | bytes 786440 | tf_op jit(solution)/shard_map/ppermute | solution.py:336
  102.1 10.7 %collective-permute-start.12 = (bf16[2,512,128]{2,1,0:T(8,128)(2,1)S(1)}, bf16[2,512,128]{2,1,0:T(8,128)(2,1)S(1)}, u32[]{:S(2)}, u32[]{:S(2)}) collective-permute-start(bf16[2,512,128]{2,1,0:T(8,128)(2,1)S(1)} %get-tuple-element.27.refs_3_), channel_id=1, source_target_pairs={{0,2},{1,3},{2,0},{3,1},{4,6},{5,7},{6,4},{7,5},{8,10},{9,11},{10,... | collective-permute-start | bytes 786440 | tf_op jit(solution)/shard_map/ppermute | solution.py:336
  107.3 15.9 %collective-permute-start.10 = (bf16[4,512,128]{2,1,0:T(8,128)(2,1)S(1)}, bf16[4,512,128]{2,1,0:T(8,128)(2,1)S(1)}, u32[]{:S(2)}, u32[]{:S(2)}) collective-permute-start(bf16[4,512,128]{2,1,0:T(8,128)(2,1)S(1)} %add.15.refs_0_), channel_id=1, source_target_pairs={{0,2},{1,3},{2,0},{3,1},{4,6},{5,7},{6,4},{7,5},{8,10},{9,11},{10,... | collective-permute-start | bytes 1572872 | tf_op jit(solution)/shard_map/ppermute | solution.py:336
  107.6 8.2 %collective-permute-start.11 = (bf16[2,512,128]{2,1,0:T(8,128)(2,1)S(1)}, bf16[2,512,128]{2,1,0:T(8,128)(2,1)S(1)}, u32[]{:S(2)}, u32[]{:S(2)}) collective-permute-start(bf16[2,512,128]{2,1,0:T(8,128)(2,1)S(1)} %total.6), channel_id=1, source_target_pairs={{0,18},{1,19},{2,16},{3,17},{4,22},{5,23},{6,20},{7,21},{8,26},{9,... | collective-permute-start | bytes 786440 | tf_op jit(solution)/shard_map/ppermute | solution.py:348
  112.9 8.3 %collective-permute-start.13 = (bf16[2,512,128]{2,1,0:T(8,128)(2,1)S(1)}, bf16[2,512,128]{2,1,0:T(8,128)(2,1)S(1)}, u32[]{:S(2)}, u32[]{:S(2)}) collective-permute-start(bf16[2,512,128]{2,1,0:T(8,128)(2,1)S(1)} %total.7), channel_id=1, source_target_pairs={{0,18},{1,19},{2,16},{3,17},{4,22},{5,23},{6,20},{7,21},{8,26},{9,... | collective-permute-start | bytes 786440 | tf_op jit(solution)/shard_map/ppermute | solution.py:348

commit v2 on v1

--- a/solution.py
+++ b/solution.py
@@ -19,6 +19,7 @@
 NT = (((1,), (1,)), ((), ()))
 VMEM = pl.BlockSpec(memory_space=pltpu.VMEM)
 BF = jnp.bfloat16
+STAGES = (((1, 3), 38), ((0,), 36), ((2,), 32))
 LIGHT = pl.CostEstimate(flops=1, bytes_accessed=1, transcendentals=0)
 
 
@@ -110,22 +111,18 @@
 
 
 def product_kernel(polarity, rels, build, tokens, focal_rows, where_ref, aperture_ref, reflection_ref, *refs):
-    update_ref = wide_ref = None
-    if build == "first":
+    if build:
         source_ref, *refs = refs
-    elif build == "update":
-        source_ref, update_ref, *refs = refs
     else:
         left_ref, right_ref, *refs = refs
     refs = refs[tokens:]
     outs, refs = refs[: len(rels)], refs[len(rels) :]
+    held_ref, *refs = refs
     if build:
         left_ref, right_ref, *refs = refs
-    held_ref, sems, *refs = refs
-    if build:
-        initial_ref, initial_sem, *refs = refs
-    if build == "update":
-        (wide_ref,) = refs
+    sems, *refs = refs
+    if build:
+        initial_ref, initial_sem = refs
     nfreq, width, _ = outs[0].shape
     pieces = [(place, freq) for place in range(len(rels)) for freq in range(nfreq)]
     blocks = [jnp.bitwise_xor(where_ref[0], rel) for rel in rels]
@@ -150,7 +147,7 @@
         begin(piece)
     if build:
         load.wait()
-        weights(polarity, where_ref[1], focal_rows, initial_ref, update_ref, wide_ref, left_ref, right_ref)
+        weights(polarity, where_ref[1], focal_rows, initial_ref, None, None, left_ref, right_ref)
 
     source_blocks, receiver_blocks = aperture_ref.shape
     strips = receiver_blocks // 4
@@ -182,41 +179,73 @@
                     part = part.reshape(tall // TILE, TILE, width) * masks[strip][None]
                     parts.append(part.reshape(tall, width))
                 masked.append(jnp.concatenate(parts, axis=0))
+                held_ref[piece, plane] = masked[plane]
             total = mm(masked[0], left_ref[freq]) + mm(masked[1], right_ref[freq])
             outs[place][freq] = total.astype(BF)
 
 
-def products(polarity, rels, focal_rows, where, aperture, reflection, initial, update=None, built=None, after=()):
+def products(polarity, rels, focal_rows, limit, where, aperture, reflection, initial, built=None, after=()):
     planes, nfreq, receivers, sources = reflection.shape
     focal = initial.shape[2]
     out = jax.ShapeDtypeStruct((nfreq, sources, 2 * focal), BF)
-    scratch = [
-        pltpu.VMEM((len(rels) * nfreq, 2, sources, sources), BF),
-        pltpu.SemaphoreType.DMA((len(rels) * nfreq, 2)),
-    ]
-    outs = [out] * len(rels)
+    pieces = len(rels) * nfreq
+    outs = [out] * len(rels) + [jax.ShapeDtypeStruct((pieces, planes, sources, sources), BF)]
+    scratch = [pltpu.SemaphoreType.DMA((pieces, planes))]
     anywhere = pl.BlockSpec(memory_space=pl.ANY)
     smem = pl.BlockSpec(memory_space=pltpu.SMEM)
-    if built is not None:
-        build, extra, specs = "", list(built), [VMEM] * 2
-    else:
+    build = built is None
+    if build:
         outs += [out] * 2
         scratch += [pltpu.VMEM(initial.shape, BF), pltpu.SemaphoreType.DMA(())]
-        if update is None:
-            build, extra, specs = "first", [initial], [anywhere]
-        else:
-            build, extra, specs = "update", [initial, update], [anywhere, VMEM]
-            scratch.append(wide(update))
+        extra, specs = [initial], [anywhere]
+    else:
+        extra, specs = list(built), [VMEM] * 2
     return pl.pallas_call(
         functools.partial(product_kernel, polarity, rels, build, len(after), focal_rows),
         in_specs=[smem, smem, anywhere] + specs + [anywhere] * len(after),
         out_specs=[VMEM] * len(outs),
         scratch_shapes=scratch,
         out_shape=outs,
-        compiler_params=pltpu.CompilerParams(vmem_limit_bytes=46 * MIB),
+        compiler_params=pltpu.CompilerParams(vmem_limit_bytes=limit * MIB),
         cost_estimate=LIGHT,
         name="products",
     )(where, aperture, reflection, *extra, *after)
+
+
+def product_again_kernel(polarity, build, tokens, focal_rows, where_ref, held_ref, *refs):
+    if build:
+        initial_ref, update_ref, *refs = refs
+        refs = refs[tokens:]
+        *outs, left_ref, right_ref, wide_ref = refs
+        weights(polarity, where_ref[1], focal_rows, initial_ref, update_ref, wide_ref, left_ref, right_ref)
+    else:
+        left_ref, right_ref, *refs = refs
+        outs = refs[tokens:]
+    nfreq = left_ref.shape[0]
+    for piece in range(held_ref.shape[0]):
+        freq = piece % nfreq
+        total = mm(held_ref[piece, 0], left_ref[freq]) + mm(held_ref[piece, 1], right_ref[freq])
+        outs[piece // nfreq][freq] = total.astype(BF)
+
+
+def products_again(polarity, focal_rows, where, held, initial, update=None, built=None, after=()):
+    _, nfreq, focal, sources = initial.shape
+    build = built is None
+    out = jax.ShapeDtypeStruct((nfreq, sources, 2 * focal), BF)
+    extra = [initial, update] if build else list(built)
+    outs = [out] * (held.shape[0] // nfreq + (2 if build else 0))
+    return pl.pallas_call(
+        functools.partial(product_again_kernel, polarity, build, len(after), focal_rows),
+        in_specs=[pl.BlockSpec(memory_space=pltpu.SMEM)]
+        + [VMEM] * (1 + len(extra))
+        + [pl.BlockSpec(memory_space=pl.ANY)] * len(after),
+        out_specs=[VMEM] * len(outs),
+        scratch_shapes=[wide(update)] if build else [],
+        out_shape=outs,
+        compiler_params=pltpu.CompilerParams(vmem_limit_bytes=16 * MIB),
+        cost_estimate=LIGHT,
+        name="products_again",
+    )(where, held, *extra, *after)
 
 
 def call(kernel, name, outs, *args, after=()):
@@ -366,19 +395,27 @@
     part = (freq_local, sources, focal)
     cut = (freq_local // CUTS, sources, focal)
 
+    focal_rows = rows * focal_block
+    held = []
     update = None
     for iteration in range(ITERS):
         polarity = 1.0 if iteration % 2 == 0 else -1.0
 
-        def respond(rels, **more):
-            return products(polarity, rels, rows * focal_block, where, aperture.T, reflection, initial, **more)
-
-        send_near, send_far, left, right = respond((1, 3), update=update)
+        def respond(stage, **more):
+            if iteration:
+                return products_again(polarity, focal_rows, where, held[stage], initial, **more)
+            rels, limit = STAGES[stage]
+            results = list(products(polarity, rels, focal_rows, limit, where, aperture.T, reflection, initial, **more))
+            held.append(results.pop(len(rels)))
+            return results
+
+        first = {"update": update} if iteration else {}
+        send_near, send_far, left, right = respond(0, **first)
         core_near, core_far = swap(send_near, 1), swap(send_far, 1)
-        (near,) = respond((0,), built=(left, right))
+        (near,) = respond(1, built=(left, right))
         totals = call(functools.partial(add_kernel, 1, 0), "add", [cut] * CUTS, near, core_near)
         far_other = [swap(total, 2) for total in totals]
-        (remote,) = respond((2,), built=(left, right), after=totals)
+        (remote,) = respond(2, built=(left, right), after=totals)
         (total,) = call(functools.partial(add_kernel, 0, 1), "add", [part], remote, core_far, after=far_other[:1])
         far_own = swap(total, 2)
         outer = []

time: 169 us -> 165 us (0.976)
  Pallas kernels: 34.9 us -> 29.2 us
  waiting for transfers between devices: 27.8 us -> 30.1 us
    pallas_call x6 -> x3, Pallas kernels: 25.3 us -> 12.6 us  [products(): pl.pallas_call(functools.partial(product_kernel, polarity, rels, build, l...]
    pallas_call x0 -> x3, Pallas kernels: none -> 7.03 us  [products_again(): pl.pallas_call(functools.partial(product_again_kernel, polarity, build, l...]
    ppermute x10, waiting for transfers between devices: 14.4 us -> 16.5 us  [swap(): lax.ppermute(values, 'src', [(i, i ^ bit) for i in range(lax.axis_size('s...]
  transfers between devices with their start and end apart: 14 -> 14, of which waited for: 10 -> 11; matrix products, arithmetic and copies ran while one was open for 0% -> 0% of each run, Pallas kernels for 9% -> 7%
where the time goes in v2:
time: 165 us
  blocking collectives  87.4 us (53%)
  waiting for transfers between devices  30.1 us (18%)
  Pallas kernels  29.2 us (18%)
  starting transfers between devices  16.1 us (10%)
  local copies, waits for them, and re-layouts  1.94 us (1%)
    all_to_all x2, blocking collectives, local(): update = lax.all_to_all(truncated, 'freq', 0, 0, tiled=True)  43.8 us
    all_to_all x2, blocking collectives, local(): lax.all_to_all(responses, 'freq', 0, 0, tiled=True, axis_index_groups=pla...  43.6 us
    ppermute x10, waiting for transfers between devices, swap(): lax.ppermute(values, 'src', [(i, i ^ bit) for i in range(lax.axis_size('s...  16.5 us
    ppermute x4, waiting for transfers between devices, outward(): return lax.ppermute(values, ('freq', 'src'), pairs)  13.6 us
    pallas_call x3, Pallas kernels, products(): pl.pallas_call(functools.partial(product_kernel, polarity, rels, build, l...  12.6 us
    ppermute x10, starting transfers between devices, swap(): lax.ppermute(values, 'src', [(i, i ^ bit) for i in range(lax.axis_size('s...  8.39 us
    ppermute x4, starting transfers between devices, outward(): return lax.ppermute(values, ('freq', 'src'), pairs)  7.7 us
    pallas_call x3, Pallas kernels, products_again(): pl.pallas_call(functools.partial(product_again_kernel, polarity, build, l...  7.03 us
  transfers between devices with their start and end apart: 14, of which 11 were waited for; matrix products, arithmetic and copies ran while one was open for 0% of the time, Pallas kernels for 7%

profile of v2, /device:TPU:0, one launch (start us, length us, event | category | flops | bytes accessed | tf_op | source)
XLA Modules:
  0.0 165.1 jit_solution(17040040421723292839)
XLA Ops:
  0.1 1.2 copy-done
  1.3 0.7 copy-done.5
  2.0 5.4 %products.3 = (bf16[4,512,256]{2,1,0:T(8,128)(2,1)S(1)}, bf16[4,512,256]{2,1,0:T(8,128)(2,1)S(1)}, bf16[8,2,512,512]{3,2,1,0:T(8,128)(2,1)S(1)}, bf16[4,512,256]...) custom-call(s32[2]{0:T(128)S(1)} %pad_add_fusion.where_ref, s32[4,16]{1,0:T(4,128)S(1)} %bitcast.7, ...), custom_call_target="tpu_custom_call" | custom-call | flops 1 | bytes 1 | tf_op jit(solution)/shard_map/products/pallas_call | solution.py:203
  7.5 0.5 collective-permute-start.1
  8.0 3.6 %products.4 = (bf16[4,512,256]{2,1,0:T(8,128)(2,1)S(1)}, bf16[4,2,512,512]{3,2,1,0:T(8,128)(2,1)S(1)}) custom-call(s32[2]{0:T(128)S(1)} %pad_add_fusion.where_ref, s32[4,16]{1,0:T(4,128)S(1)} %bitcast.8, bf16[2,4,2048,512]{3,2,1,0:T(8,128)(2,1)} %reflection_ref.5, bf16[4,512,256]{2,1,0:T(8,128)(2,1)S(1)} %get-tuple-element.22.refs_0_, ...), custom_call_target="tpu_custom_call" | custom-call | flops 1 | bytes 1 | tf_op jit(solution)/shard_map/products/pallas_call | solution.py:203
  11.6 0.1 add.12
  11.8 2.1 %collective-permute-start.2 = (bf16[2,512,128]{2,1,0:T(8,128)(2,1)S(1)}, bf16[2,512,128]{2,1,0:T(8,128)(2,1)S(1)}, u32[]{:S(2)}, u32[]{:S(2)}) collective-permute-start(bf16[2,512,128]{2,1,0:T(8,128)(2,1)S(1)} %get-tuple-element.28.refs_2_), channel_id=1, source_target_pairs={{0,2},{1,3},{2,0},{3,1},{4,6},{5,7},{6,4},{7,5},{8,10},{9,11},{10,... | collective-permute-start | bytes 786440 | tf_op jit(solution)/shard_map/ppermute | solution.py:365
  13.8 3.6 %products.5 = (bf16[4,512,256]{2,1,0:T(8,128)(2,1)S(1)}, bf16[4,2,512,512]{3,2,1,0:T(8,128)(2,1)S(1)}) custom-call(s32[2]{0:T(128)S(1)} %pad_add_fusion.where_ref, s32[4,16]{1,0:T(4,128)S(1)} %bitcast.9, bf16[2,4,2048,512]{3,2,1,0:T(8,128)(2,1)} %reflection_ref.5, bf16[4,512,256]{2,1,0:T(8,128)(2,1)S(1)} %get-tuple-element.22.refs_0_, ...), custom_call_target="tpu_custom_call" | custom-call | flops 1 | bytes 1 | tf_op jit(solution)/shard_map/products/pallas_call | solution.py:203
  17.5 0.1 collective-permute-start.5
  17.6 3.1 %collective-permute-done.2.refs_0_.far_ref = bf16[2,512,128]{2,1,0:T(8,128)(2,1)S(1)} collective-permute-done((bf16[2,512,128]{2,1,0:T(8,128)(2,1)S(1)}, bf16[2,512,128]{2,1,0:T(8,128)(2,1)S(1)}, u32[]{:S(2)}, u32[]{:S(2)}) %collective-permute-start.2) | collective-permute-done | bytes 262176 | tf_op jit(solution)/shard_map/ppermute | solution.py:365
  20.8 0.1 add.13.refs_0_
  20.9 2.3 %collective-permute-start.3 = (bf16[4,512,128]{2,1,0:T(8,128)(2,1)S(1)}, bf16[4,512,128]{2,1,0:T(8,128)(2,1)S(1)}, u32[]{:S(2)}, u32[]{:S(2)}) collective-permute-start(bf16[4,512,128]{2,1,0:T(8,128)(2,1)S(1)} %add.13.refs_0_), channel_id=1, source_target_pairs={{0,2},{1,3},{2,0},{3,1},{4,6},{5,7},{6,4},{7,5},{8,10},{9,11},{10,... | collective-permute-start | bytes 1572872 | tf_op jit(solution)/shard_map/ppermute | solution.py:365
  23.2 0.1 total.4
  23.3 2.2 %collective-permute-start.4 = (bf16[2,512,128]{2,1,0:T(8,128)(2,1)S(1)}, bf16[2,512,128]{2,1,0:T(8,128)(2,1)S(1)}, u32[]{:S(2)}, u32[]{:S(2)}) collective-permute-start(bf16[2,512,128]{2,1,0:T(8,128)(2,1)S(1)} %total.4), channel_id=1, source_target_pairs={{0,18},{1,19},{2,16},{3,17},{4,22},{5,23},{6,20},{7,21},{8,26},{9,... | collective-permute-start | bytes 786440 | tf_op jit(solution)/shard_map/ppermute | solution.py:377
  25.5 1.3 collective-permute-done.5.far_ref
  26.8 0.1 total.5
  26.9 4.0 %collective-permute-start.6 = (bf16[2,512,128]{2,1,0:T(8,128)(2,1)S(1)}, bf16[2,512,128]{2,1,0:T(8,128)(2,1)S(1)}, u32[]{:S(2)}, u32[]{:S(2)}) collective-permute-start(bf16[2,512,128]{2,1,0:T(8,128)(2,1)S(1)} %total.5), channel_id=1, source_target_pairs={{0,18},{1,19},{2,16},{3,17},{4,22},{5,23},{6,20},{7,21},{8,26},{9,... | collective-permute-start | bytes 786440 | tf_op jit(solution)/shard_map/ppermute | solution.py:377
  30.9 0.8 collective-permute-done.4.refs_0_
  31.7 4.9 %collective-permute-done.6.refs_1_ = bf16[2,512,128]{2,1,0:T(8,128)(2,1)S(1)} collective-permute-done((bf16[2,512,128]{2,1,0:T(8,128)(2,1)S(1)}, bf16[2,512,128]{2,1,0:T(8,128)(2,1)S(1)}, u32[]{:S(2)}, u32[]{:S(2)}) %collective-permute-start.6) | collective-permute-done | bytes 262176 | tf_op jit(solution)/shard_map/ppermute | solution.py:377
  36.6 0.6 collective-permute-done.3.far_ref
  37.2 1.3 pack_own.2
  38.6 23.5 %all_to_all.20.traces_ref = bf16[16,64,512]{2,1,0:T(8,128)(2,1)S(1)} all-to-all(bf16[16,64,512]{2,1,0:T(8,128)(2,1)S(1)} %pack_own.2), channel_id=1, replica_groups={{0,4,8,12,32,36,40,44,64,68,72,76,96,100,104,108},{16,20,24,28,48,52,56..., dimensions={0} | all-to-all | bytes 2097152 | tf_op jit(solution)/shard_map/all_to_all | solution.py:429
  62.1 2.3 %window.2 = bf16[32,32,512]{2,1,0:T(8,128)(2,1)S(1)} custom-call(bf16[4,256,256]{2,1,0:T(8,128)(2,1)S(1)} %copy-done.2, s32[4,512]{1,0:T(4,128)S(1)} %copy-done.4, bf16[16,64,512]{2,1,0:T(8,128)(2,1)S(1)} %all_to_all.20.traces_ref), custom_call_target="tpu_custom_call" | custom-call | flops 1 | bytes 1 | tf_op jit(solution)/shard_map/window/pallas_call | solution.py:252
  64.3 23.6 %all_to_all.21 = bf16[32,32,512]{2,1,0:T(8,128)(2,1)S(1)} all-to-all(bf16[32,32,512]{2,1,0:T(8,128)(2,1)S(1)} %window.2), channel_id=1, replica_groups=mesh['freq'=32,'src'=4] {'freq'}, dimensions={0} | all-to-all | bytes 2097152 | tf_op jit(solution)/shard_map/all_to_all | solution.py:433
  88.0 3.5 %products_again.3 = (bf16[4,512,256]{2,1,0:T(8,128)(2,1)S(1)}, bf16[4,512,256]{2,1,0:T(8,128)(2,1)S(1)}, bf16[4,512,256]{2,1,0:T(8,128)(2,1)S(1)}, bf16[4,512,256]{2,1,0:T(8,128)(2,1)S(1)}) custom-call(s32[2]{0:T(128)S(1)} %pad_add_fusion.where_ref, bf16[8,2,512,512]{3,2,1,0:T(8,128)(2,1)S(1)} %get-tuple-element.25.held_ref, ...), custom_call_target="tpu_custom_call" | custom-call | flops 1 | bytes 1 | tf_op jit(solution)/shard_map/products_again/pallas_call | solution.py:237
  91.5 0.5 collective-permute-start.8
  92.0 1.8 %products_again.4.mine_ref = bf16[4,512,256]{2,1,0:T(8,128)(2,1)S(1)} custom-call(s32[2]{0:T(128)S(1)} %pad_add_fusion.where_ref, bf16[4,2,512,512]{3,2,1,0:T(8,128)(2,1)S(1)} %get-tuple-element.24.held_ref, bf16[4,512,256]{2,1,0:T(8,128)(2,1)S(1)} %get-tuple-element.32.refs_0_, bf16[4,512,256]{2,1,0:T(8,128)(2,1)S(1)} %get-tuple-element.33.refs_1_), custom_call_target="tpu_custom_call" | custom-call | flops 1 | bytes 1 | tf_op jit(solution)/shard_map/products_again/pallas_call | solution.py:237
  93.8 0.4 collective-permute-done.7.core_ref
  94.2 0.1 add.14
  94.3 0.6 collective-permute-start.9
  94.9 1.5 collective-permute-start.12
  96.4 1.8 %products_again.5.mine_ref = bf16[4,512,256]{2,1,0:T(8,128)(2,1)S(1)} custom-call(s32[2]{0:T(128)S(1)} %pad_add_fusion.where_ref, bf16[4,2,512,512]{3,2,1,0:T(8,128)(2,1)S(1)} %get-tuple-element.35.held_ref, bf16[4,512,256]{2,1,0:T(8,128)(2,1)S(1)} %get-tuple-element.32.refs_0_, bf16[4,512,256]{2,1,0:T(8,128)(2,1)S(1)} %get-tuple-element.33.refs_1_, ...), custom_call_target="tpu_custom_call" | custom-call | flops 1 | bytes 1 | tf_op jit(solution)/shard_map/products_again/pallas_call | solution.py:237
  98.2 5.3 %collective-permute-done.9.refs_0_.far_ref = bf16[2,512,128]{2,1,0:T(8,128)(2,1)S(1)} collective-permute-done((bf16[2,512,128]{2,1,0:T(8,128)(2,1)S(1)}, bf16[2,512,128]{2,1,0:T(8,128)(2,1)S(1)}, u32[]{:S(2)}, u32[]{:S(2)}) %collective-permute-start.9) | collective-permute-done | bytes 262176 | tf_op jit(solution)/shard_map/ppermute | solution.py:365
  103.6 0.1 add.15.refs_0_
  103.7 0.6 collective-permute-start.10
  104.3 0.1 total.6
  104.4 0.9 collective-permute-start.11
  105.3 3.9 %collective-permute-done.12.far_ref = bf16[2,512,128]{2,1,0:T(8,128)(2,1)S(1)} collective-permute-done((bf16[2,512,128]{2,1,0:T(8,128)(2,1)S(1)}, bf16[2,512,128]{2,1,0:T(8,128)(2,1)S(1)}, u32[]{:S(2)}, u32[]{:S(2)}) %collective-permute-start.12) | collective-permute-done | bytes 262176 | tf_op jit(solution)/shard_map/ppermute | solution.py:365
  109.2 0.1 total.7
  109.3 0.5 collective-permute-start.13
  109.8 2.7 %collective-permute-done.11.refs_0_ = bf16[2,512,128]{2,1,0:T(8,128)(2,1)S(1)} collective-permute-done((bf16[2,512,128]{2,1,0:T(8,128)(2,1)S(1)}, bf16[2,512,128]{2,1,0:T(8,128)(2,1)S(1)}, u32[]{:S(2)}, u32[]{:S(2)}) %collective-permute-start.11) | collective-permute-done | bytes 262176 | tf_op jit(solution)/shard_map/ppermute | solution.py:377
  112.5 5.2 %collective-permute-done.13.refs_1_ = bf16[2,512,128]{2,1,0:T(8,128)(2,1)S(1)} collective-permute-done((bf16[2,512,128]{2,1,0:T(8,128)(2,1)S(1)}, bf16[2,512,128]{2,1,0:T(8,128)(2,1)S(1)}, u32[]{:S(2)}, u32[]{:S(2)}) %collective-permute-start.13) | collective-permute-done | bytes 262176 | tf_op jit(solution)/shard_map/ppermute | solution.py:377
  117.7 1.9 %collective-permute-done.10.far_ref = bf16[4,512,128]{2,1,0:T(8,128)(2,1)S(1)} collective-permute-done((bf16[4,512,128]{2,1,0:T(8,128)(2,1)S(1)}, bf16[4,512,128]{2,1,0:T(8,128)(2,1)S(1)}, u32[]{:S(2)}, u32[]{:S(2)}) %collective-permute-start.10) | collective-permute-done | bytes 524320 | tf_op jit(solution)/shard_map/ppermute | solution.py:365
  119.6 1.3 pack_own.3
  120.9 20.1 %all_to_all.22.traces_ref = bf16[16,64,512]{2,1,0:T(8,128)(2,1)S(1)} all-to-all(bf16[16,64,512]{2,1,0:T(8,128)(2,1)S(1)} %pack_own.3), channel_id=1, replica_groups={{0,4,8,12,32,36,40,44,64,68,72,76,96,100,104,108},{16,20,24,28,48,52,56..., dimensions={0} | all-to-all | bytes 2097152 | tf_op jit(solution)/shard_map/all_to_all | solution.py:429
  141.0 2.2 %window.3 = bf16[32,32,512]{2,1,0:T(8,128)(2,1)S(1)} custom-call(bf16[4,256,256]{2,1,0:T(8,128)(2,1)S(1)} %copy-done.2, s32[4,512]{1,0:T(4,128)S(1)} %copy-done.4, bf16[16,64,512]{2,1,0:T(8,128)(2,1)S(1)} %all_to_all.22.traces_ref), custom_call_target="tpu_custom_call" | custom-call | flops 1 | bytes 1 | tf_op jit(solution)/shard_map/window/pallas_call | solution.py:252
  143.3 20.2 %all_to_all.23 = bf16[32,32,512]{2,1,0:T(8,128)(2,1)S(1)} all-to-all(bf16[32,32,512]{2,1,0:T(8,128)(2,1)S(1)} %window.3), channel_id=1, replica_groups=mesh['freq'=32,'src'=4] {'freq'}, dimensions={0} | all-to-all | bytes 2097152 | tf_op jit(solution)/shard_map/all_to_all | solution.py:433
  163.5 1.5 finish.1
  (18 shorter events, 0.3 us)
Async XLA Ops:
  0.1 1.2 copy-start
  1.3 0.7 copy-start.5
  7.4 4.2 %collective-permute-start = (bf16[4,512,256]{2,1,0:T(8,128)(2,1)S(1)}, bf16[4,512,256]{2,1,0:T(8,128)(2,1)S(1)}, u32[]{:S(2)}, u32[]{:S(2)}) collective-permute-start(bf16[4,512,256]{2,1,0:T(8,128)(2,1)S(1)} %get-tuple-element.27), channel_id=1, source_target_pairs={{0,1},{1,0},{2,3},{3,2},{4,5},{5,4},{6,7},{7,6},{8,9},{9,8},{10,11... | collective-permute-start | bytes 3145736 | tf_op jit(solution)/shard_map/ppermute | solution.py:365
  7.5 10.1 %collective-permute-start.1 = (bf16[4,512,256]{2,1,0:T(8,128)(2,1)S(1)}, bf16[4,512,256]{2,1,0:T(8,128)(2,1)S(1)}, u32[]{:S(2)}, u32[]{:S(2)}) collective-permute-start(bf16[4,512,256]{2,1,0:T(8,128)(2,1)S(1)} %get-tuple-element.31), channel_id=1, source_target_pairs={{0,1},{1,0},{2,3},{3,2},{4,5},{5,4},{6,7},{7,6},{8,9},{9,8},{10,11... | collective-permute-start | bytes 3145736 | tf_op jit(solution)/shard_map/ppermute | solution.py:365
  8.0 5.8 %copy-start.6 = (s32[16,4]{0,1:T(4,128)S(1)}, s32[16,4]{0,1:T(4,128)}, u32[]{:S(2)}) copy-start(s32[16,4]{0,1:T(4,128)} %param.7) | copy-start | bytes 772
  11.8 9.0 %collective-permute-start.2 = (bf16[2,512,128]{2,1,0:T(8,128)(2,1)S(1)}, bf16[2,512,128]{2,1,0:T(8,128)(2,1)S(1)}, u32[]{:S(2)}, u32[]{:S(2)}) collective-permute-start(bf16[2,512,128]{2,1,0:T(8,128)(2,1)S(1)} %get-tuple-element.28.refs_2_), channel_id=1, source_target_pairs={{0,2},{1,3},{2,0},{3,1},{4,6},{5,7},{6,4},{7,5},{8,10},{9,11},{10,... | collective-permute-start | bytes 786440 | tf_op jit(solution)/shard_map/ppermute | solution.py:365
  17.5 19.8 %copy-start.3 = (bf16[512,512]{1,0:T(8,128)(2,1)S(1)}, bf16[512,512]{1,0:T(8,128)(2,1)}, u32[]{:S(2)}) copy-start(bf16[512,512]{1,0:T(8,128)(2,1)} %constant.39.clone.pack_ref) | copy-start | bytes 1572868
  17.5 44.6 %copy-start.2 = (bf16[4,256,256]{2,1,0:T(8,128)(2,1)S(1)}, bf16[4,256,256]{2,1,0:T(8,128)(2,1)}, u32[]{:S(2)}) copy-start(bf16[4,256,256]{2,1,0:T(8,128)(2,1)} %constant.40.clone.dft_ref) | copy-start | bytes 1572868
  17.5 44.6 %copy-start.4 = (s32[4,512]{1,0:T(4,128)S(1)}, s32[4,512]{1,0:T(4,128)}, u32[]{:S(2)}) copy-start(s32[4,512]{1,0:T(4,128)} %onsets_ref.3) | copy-start | bytes 24580
  17.5 9.3 %collective-permute-start.5 = (bf16[2,512,128]{2,1,0:T(8,128)(2,1)S(1)}, bf16[2,512,128]{2,1,0:T(8,128)(2,1)S(1)}, u32[]{:S(2)}, u32[]{:S(2)}) collective-permute-start(bf16[2,512,128]{2,1,0:T(8,128)(2,1)S(1)} %get-tuple-element.29.refs_3_), channel_id=1, source_target_pairs={{0,2},{1,3},{2,0},{3,1},{4,6},{5,7},{6,4},{7,5},{8,10},{9,11},{10,... | collective-permute-start | bytes 786440 | tf_op jit(solution)/shard_map/ppermute | solution.py:365
  20.9 67.1 %copy-start.1 = (bf16[2,4,128,512]{3,2,1,0:T(8,128)(2,1)S(1)}, bf16[2,4,128,512]{3,2,1,0:T(8,128)(2,1)}, u32[]{:S(2)}) copy-start(bf16[2,4,128,512]{3,2,1,0:T(8,128)(2,1)} %initial_ref.1) | copy-start | bytes 3145732
  20.9 16.4 %collective-permute-start.3 = (bf16[4,512,128]{2,1,0:T(8,128)(2,1)S(1)}, bf16[4,512,128]{2,1,0:T(8,128)(2,1)S(1)}, u32[]{:S(2)}, u32[]{:S(2)}) collective-permute-start(bf16[4,512,128]{2,1,0:T(8,128)(2,1)S(1)} %add.13.refs_0_), channel_id=1, source_target_pairs={{0,2},{1,3},{2,0},{3,1},{4,6},{5,7},{6,4},{7,5},{8,10},{9,11},{10,... | collective-permute-start | bytes 1572872 | tf_op jit(solution)/shard_map/ppermute | solution.py:365
  23.3 8.4 %collective-permute-start.4 = (bf16[2,512,128]{2,1,0:T(8,128)(2,1)S(1)}, bf16[2,512,128]{2,1,0:T(8,128)(2,1)S(1)}, u32[]{:S(2)}, u32[]{:S(2)}) collective-permute-start(bf16[2,512,128]{2,1,0:T(8,128)(2,1)S(1)} %total.4), channel_id=1, source_target_pairs={{0,18},{1,19},{2,16},{3,17},{4,22},{5,23},{6,20},{7,21},{8,26},{9,... | collective-permute-start | bytes 786440 | tf_op jit(solution)/shard_map/ppermute | solution.py:377
  26.9 9.7 %collective-permute-start.6 = (bf16[2,512,128]{2,1,0:T(8,128)(2,1)S(1)}, bf16[2,512,128]{2,1,0:T(8,128)(2,1)S(1)}, u32[]{:S(2)}, u32[]{:S(2)}) collective-permute-start(bf16[2,512,128]{2,1,0:T(8,128)(2,1)S(1)} %total.5), channel_id=1, source_target_pairs={{0,18},{1,19},{2,16},{3,17},{4,22},{5,23},{6,20},{7,21},{8,26},{9,... | collective-permute-start | bytes 786440 | tf_op jit(solution)/shard_map/ppermute | solution.py:377
  91.4 2.7 %collective-permute-start.7 = (bf16[4,512,256]{2,1,0:T(8,128)(2,1)S(1)}, bf16[4,512,256]{2,1,0:T(8,128)(2,1)S(1)}, u32[]{:S(2)}, u32[]{:S(2)}) collective-permute-start(bf16[4,512,256]{2,1,0:T(8,128)(2,1)S(1)} %get-tuple-element.34), channel_id=1, source_target_pairs={{0,1},{1,0},{2,3},{3,2},{4,5},{5,4},{6,7},{7,6},{8,9},{9,8},{10,11... | collective-permute-start | bytes 3145736 | tf_op jit(solution)/shard_map/ppermute | solution.py:365
  91.5 6.7 %collective-permute-start.8 = (bf16[4,512,256]{2,1,0:T(8,128)(2,1)S(1)}, bf16[4,512,256]{2,1,0:T(8,128)(2,1)S(1)}, u32[]{:S(2)}, u32[]{:S(2)}) collective-permute-start(bf16[4,512,256]{2,1,0:T(8,128)(2,1)S(1)} %get-tuple-element.38), channel_id=1, source_target_pairs={{0,1},{1,0},{2,3},{3,2},{4,5},{5,4},{6,7},{7,6},{8,9},{9,8},{10,11... | collective-permute-start | bytes 3145736 | tf_op jit(solution)/shard_map/ppermute | solution.py:365
  94.3 9.3 %collective-permute-start.9 = (bf16[2,512,128]{2,1,0:T(8,128)(2,1)S(1)}, bf16[2,512,128]{2,1,0:T(8,128)(2,1)S(1)}, u32[]{:S(2)}, u32[]{:S(2)}) collective-permute-start(bf16[2,512,128]{2,1,0:T(8,128)(2,1)S(1)} %get-tuple-element.36.refs_2_), channel_id=1, source_target_pairs={{0,2},{1,3},{2,0},{3,1},{4,6},{5,7},{6,4},{7,5},{8,10},{9,11},{10,... | collective-permute-start | bytes 786440 | tf_op jit(solution)/shard_map/ppermute | solution.py:365
  94.9 14.3 %collective-permute-start.12 = (bf16[2,512,128]{2,1,0:T(8,128)(2,1)S(1)}, bf16[2,512,128]{2,1,0:T(8,128)(2,1)S(1)}, u32[]{:S(2)}, u32[]{:S(2)}) collective-permute-start(bf16[2,512,128]{2,1,0:T(8,128)(2,1)S(1)} %get-tuple-element.37.refs_3_), channel_id=1, source_target_pairs={{0,2},{1,3},{2,0},{3,1},{4,6},{5,7},{6,4},{7,5},{8,10},{9,11},{10,... | collective-permute-start | bytes 786440 | tf_op jit(solution)/shard_map/ppermute | solution.py:365
  103.7 15.9 %collective-permute-start.10 = (bf16[4,512,128]{2,1,0:T(8,128)(2,1)S(1)}, bf16[4,512,128]{2,1,0:T(8,128)(2,1)S(1)}, u32[]{:S(2)}, u32[]{:S(2)}) collective-permute-start(bf16[4,512,128]{2,1,0:T(8,128)(2,1)S(1)} %add.15.refs_0_), channel_id=1, source_target_pairs={{0,2},{1,3},{2,0},{3,1},{4,6},{5,7},{6,4},{7,5},{8,10},{9,11},{10,... | collective-permute-start | bytes 1572872 | tf_op jit(solution)/shard_map/ppermute | solution.py:365
  104.4 8.1 %collective-permute-start.11 = (bf16[2,512,128]{2,1,0:T(8,128)(2,1)S(1)}, bf16[2,512,128]{2,1,0:T(8,128)(2,1)S(1)}, u32[]{:S(2)}, u32[]{:S(2)}) collective-permute-start(bf16[2,512,128]{2,1,0:T(8,128)(2,1)S(1)} %total.6), channel_id=1, source_target_pairs={{0,18},{1,19},{2,16},{3,17},{4,22},{5,23},{6,20},{7,21},{8,26},{9,... | collective-permute-start | bytes 786440 | tf_op jit(solution)/shard_map/ppermute | solution.py:377
  109.3 8.4 %collective-permute-start.13 = (bf16[2,512,128]{2,1,0:T(8,128)(2,1)S(1)}, bf16[2,512,128]{2,1,0:T(8,128)(2,1)S(1)}, u32[]{:S(2)}, u32[]{:S(2)}) collective-permute-start(bf16[2,512,128]{2,1,0:T(8,128)(2,1)S(1)} %total.7), channel_id=1, source_target_pairs={{0,18},{1,19},{2,16},{3,17},{4,22},{5,23},{6,20},{7,21},{8,26},{9,... | collective-permute-start | bytes 786440 | tf_op jit(solution)/shard_map/ppermute | solution.py:377

commit v3 on v2

--- a/solution.py
+++ b/solution.py
@@ -29,12 +29,6 @@
 
 def nt(left, right):
     return lax.dot_general(left, right, NT, preferred_element_type=jnp.float32)
-
-
-def split(values):
-    high = values.astype(BF)
-    low = (values - high.astype(values.dtype)).astype(BF)
-    return high, low
 
 
 def tables(columns, rows, freq_local, focal_block):
@@ -89,15 +83,13 @@
     return pltpu.VMEM((width // LANES, rows, LANES), jnp.float32)
 
 
-def weights(polarity, half, block, initial_ref, update_ref, wide_ref, left_ref, right_ref):
+def weights(polarity, half, block, freqs, initial_ref, wide_ref, left_ref, right_ref):
     _, nfreq, focal, width = initial_ref.shape
-    if update_ref is not None:
-        spread(wide_ref, update_ref)
-    for freq in range(nfreq):
+    for freq in freqs:
         planes = []
         for plane in range(2):
             value = initial_ref[plane, freq].astype(jnp.float32)
-            if update_ref is not None:
+            if wide_ref is not None:
                 value = value + every(wide_ref, 2 * freq + plane, focal, 2 * nfreq)
                 value = value.astype(BF).astype(jnp.float32)
             value = value.reshape(focal // (2 * block), 2, block, width)
@@ -110,7 +102,7 @@
             right_ref[freq, :, here] = right.T.astype(BF)
 
 
-def product_kernel(polarity, rels, build, tokens, focal_rows, where_ref, aperture_ref, reflection_ref, *refs):
+def product_kernel(polarity, rels, build, tokens, focal_rows, blocks_shape, where_ref, reflection_ref, *refs):
     if build:
         source_ref, *refs = refs
     else:
@@ -147,18 +139,17 @@
         begin(piece)
     if build:
         load.wait()
-        weights(polarity, where_ref[1], focal_rows, initial_ref, None, None, left_ref, right_ref)
-
-    source_blocks, receiver_blocks = aperture_ref.shape
+        weights(polarity, where_ref[1], focal_rows, range(nfreq), initial_ref, None, left_ref, right_ref)
+
+    source_blocks, receiver_blocks = blocks_shape
     strips = receiver_blocks // 4
     tall = width // strips
     wide_block = width // source_blocks
 
     def mask_of(place, strip):
         row = blocks[place] * strips + strip
-        parts = [
-            jnp.full((TILE, wide_block), aperture_ref[column, row].astype(jnp.float32)) for column in range(source_blocks)
-        ]
+        within = [where_ref[2 + column * receiver_blocks + row] for column in range(source_blocks)]
+        parts = [jnp.full((TILE, wide_block), value.astype(jnp.float32)) for value in within]
         return jnp.concatenate(parts, axis=1).astype(BF)
 
     for low in range(0, len(pieces), TOGETHER):
@@ -184,7 +175,7 @@
             outs[place][freq] = total.astype(BF)
 
 
-def products(polarity, rels, focal_rows, limit, where, aperture, reflection, initial, built=None, after=()):
+def products(polarity, rels, focal_rows, limit, blocks, where, reflection, initial, built=None, after=()):
     planes, nfreq, receivers, sources = reflection.shape
     focal = initial.shape[2]
     out = jax.ShapeDtypeStruct((nfreq, sources, 2 * focal), BF)
@@ -201,15 +192,15 @@
     else:
         extra, specs = list(built), [VMEM] * 2
     return pl.pallas_call(
-        functools.partial(product_kernel, polarity, rels, build, len(after), focal_rows),
-        in_specs=[smem, smem, anywhere] + specs + [anywhere] * len(after),
+        functools.partial(product_kernel, polarity, rels, build, len(after), focal_rows, blocks),
+        in_specs=[smem, anywhere] + specs + [anywhere] * len(after),
         out_specs=[VMEM] * len(outs),
         scratch_shapes=scratch,
         out_shape=outs,
         compiler_params=pltpu.CompilerParams(vmem_limit_bytes=limit * MIB),
         cost_estimate=LIGHT,
         name="products",
-    )(where, aperture, reflection, *extra, *after)
+    )(where, reflection, *extra, *after)
 
 
 def product_again_kernel(polarity, build, tokens, focal_rows, where_ref, held_ref, *refs):
@@ -217,15 +208,18 @@
         initial_ref, update_ref, *refs = refs
         refs = refs[tokens:]
         *outs, left_ref, right_ref, wide_ref = refs
-        weights(polarity, where_ref[1], focal_rows, initial_ref, update_ref, wide_ref, left_ref, right_ref)
+        spread(wide_ref, update_ref)
     else:
         left_ref, right_ref, *refs = refs
         outs = refs[tokens:]
     nfreq = left_ref.shape[0]
-    for piece in range(held_ref.shape[0]):
-        freq = piece % nfreq
-        total = mm(held_ref[piece, 0], left_ref[freq]) + mm(held_ref[piece, 1], right_ref[freq])
-        outs[piece // nfreq][freq] = total.astype(BF)
+    for freq in range(nfreq):
+        if build:
+            weights(polarity, where_ref[1], focal_rows, (freq,), initial_ref, wide_ref, left_ref, right_ref)
+        for place, out_ref in enumerate(outs):
+            piece = place * nfreq + freq
+            total = mm(held_ref[piece, 0], left_ref[freq]) + mm(held_ref[piece, 1], right_ref[freq])
+            out_ref[freq] = total.astype(BF)
 
 
 def products_again(polarity, focal_rows, where, held, initial, update=None, built=None, after=()):
@@ -282,17 +276,18 @@
 def pack_own_kernel(where_ref, pack_ref, mine_ref, core_ref, far_ref, *refs):
     *outer_refs, out_ref = refs
     nfreq, width, lanes = far_ref.shape
-    devices, rows, _ = out_ref.shape
-    rows = rows // 2
-    half = where_ref[1]
-    own = []
+    group = 2 * nfreq
+    mine = where_ref[1] == 0
+    outer = [ref[f] for ref in outer_refs for f in range(ref.shape[0])]
+    halves = [[], []]
     for f in range(nfreq):
         total = mine_ref[f, :, :lanes].astype(jnp.float32) + core_ref[f, :, :lanes].astype(jnp.float32)
-        own.append((total + far_ref[f].astype(jnp.float32)).astype(BF))
-    outer = [ref[f] for ref in outer_refs for f in range(ref.shape[0])]
-    for h, parts in ((half, own), (1 - half, outer)):
-        packed = nt(pack_ref[...], jnp.concatenate(parts, axis=1)).astype(BF)
-        out_ref[:, pl.ds(pl.multiple_of(h * rows, rows), rows), :] = packed.reshape(devices, rows, width)
+        own = (total + far_ref[f].astype(jnp.float32)).astype(BF)
+        halves[0].append(jnp.where(mine, own, outer[f]))
+        halves[1].append(jnp.where(mine, outer[f], own))
+    packed = [nt(pack_ref[...], jnp.concatenate(parts, axis=1)) for parts in halves]
+    packed = [part.reshape(part.shape[0] // group, group, width) for part in packed]
+    out_ref[...] = jnp.stack(packed, axis=1).reshape(out_ref.shape).astype(BF)
 
 
 def pack_own(where, shape, *args):
@@ -310,19 +305,18 @@
 def window_kernel(dft_ref, onsets_ref, traces_ref, out_ref):
     focal, width = onsets_ref.shape
     devices, rows, _ = traces_ref.shape
-    group = rows // (2 * focal)
+    rows = rows // focal
     nfreq = dft_ref.shape[1] // 2
     step = lax.broadcasted_iota(jnp.int32, (nfreq, width), 0)
-    traces = traces_ref[...].astype(jnp.float32).reshape(2 * devices, focal, group, width)
     results = []
     for j in range(focal):
-        column = traces[:, j].reshape(2 * nfreq, width).astype(BF)
+        column = traces_ref[:, j * rows : (j + 1) * rows, :].reshape(2 * nfreq, width)
         time = mm(dft_ref[0], column) + mm(dft_ref[1], column)
         keep = step < onsets_ref[j : j + 1, :]
         keep = jnp.concatenate([keep, keep], axis=0)
-        high, low = split(jnp.where(keep, time, 0.0))
-        back = mm(dft_ref[2], high) + mm(dft_ref[2], low) + mm(dft_ref[3], high)
-        results.append(back.reshape(2 * devices, group, width))
+        time = jnp.where(keep, time, 0.0).astype(BF)
+        back = mm(dft_ref[2], time) + mm(dft_ref[3], time)
+        results.append(back.reshape(2 * devices, rows // 2, width))
     out_ref[...] = jnp.stack(results, axis=1).reshape(out_ref.shape).astype(BF)
 
 
@@ -388,6 +382,8 @@
     dft = jnp.asarray(np.concatenate([pair(to_time), pair(to_freq)]))
     half = (lax.axis_index("freq") // rows) % 2
     where = jnp.stack([lax.axis_index("src"), half]).astype(jnp.int32)
+    where = jnp.concatenate([where, aperture.T.reshape(-1)])
+    blocks = aperture.shape[::-1]
     plane_groups = [
         [(x * 2 + h) * rows + y for x in range(columns) for y in range(rows)] for h in range(2)
     ]
@@ -405,7 +401,7 @@
             if iteration:
                 return products_again(polarity, focal_rows, where, held[stage], initial, **more)
             rels, limit = STAGES[stage]
-            results = list(products(polarity, rels, focal_rows, limit, where, aperture.T, reflection, initial, **more))
+            results = list(products(polarity, rels, focal_rows, limit, blocks, where, reflection, initial, **more))
             held.append(results.pop(len(rels)))
             return results
 

time: 165 us -> 165 us (level)
  no operation moved by 1% of the time
where the time goes in v3:
time: 165 us; the launch traced here: 164 us
  blocking collectives  87.5 us (53%)
  waiting for transfers between devices  30.1 us (18%)
  Pallas kernels  28.1 us (17%)
  starting transfers between devices  16.1 us (10%)
  local copies, waits for them, and re-layouts  2.02 us (1%)
    all_to_all x2, blocking collectives, local(): update = lax.all_to_all(truncated, 'freq', 0, 0, tiled=True)  43.9 us
    all_to_all x2, blocking collectives, local(): lax.all_to_all(responses, 'freq', 0, 0, tiled=True, axis_index_groups=pla...  43.6 us
    ppermute x10, waiting for transfers between devices, swap(): lax.ppermute(values, 'src', [(i, i ^ bit) for i in range(lax.axis_size('s...  16.5 us
    ppermute x4, waiting for transfers between devices, outward(): return lax.ppermute(values, ('freq', 'src'), pairs)  13.6 us
    pallas_call x3, Pallas kernels, products(): pl.pallas_call(functools.partial(product_kernel, polarity, rels, build, l...  12.5 us
    ppermute x10, starting transfers between devices, swap(): lax.ppermute(values, 'src', [(i, i ^ bit) for i in range(lax.axis_size('s...  8.3 us
    ppermute x4, starting transfers between devices, outward(): return lax.ppermute(values, ('freq', 'src'), pairs)  7.82 us
    pallas_call x3, Pallas kernels, products_again(): pl.pallas_call(functools.partial(product_again_kernel, polarity, build, l...  6.88 us
  transfers between devices with their start and end apart: 14, of which 11 were waited for; matrix products, arithmetic and copies ran while one was open for 0% of the time, Pallas kernels for 7%

profile of v3, /device:TPU:0, one launch (start us, length us, event | category | flops | bytes accessed | tf_op | source)
XLA Modules:
  0.0 164.2 jit_solution(8996544868045007668)
XLA Ops:
  0.0 0.8 reshape.9
  0.8 1.2 copy-done
  2.1 5.4 %products.3 = (bf16[4,512,256]{2,1,0:T(8,128)(2,1)S(1)}, bf16[4,512,256]{2,1,0:T(8,128)(2,1)S(1)}, bf16[8,2,512,512]{3,2,1,0:T(8,128)(2,1)S(1)}, bf16[4,512,256]...) custom-call(s32[66]{0:T(128)S(1)} %pad_add_fusion.where_ref, bf16[2,4,2048,512]{3,2,1,0:T(8,128)(2,1)} %reflection_ref.5, ...), custom_call_target="tpu_custom_call" | custom-call | flops 1 | bytes 1 | tf_op jit(solution)/shard_map/products/pallas_call | solution.py:194
  7.6 0.5 collective-permute-start.1
  8.1 3.6 %products.4 = (bf16[4,512,256]{2,1,0:T(8,128)(2,1)S(1)}, bf16[4,2,512,512]{3,2,1,0:T(8,128)(2,1)S(1)}) custom-call(s32[66]{0:T(128)S(1)} %pad_add_fusion.where_ref, bf16[2,4,2048,512]{3,2,1,0:T(8,128)(2,1)} %reflection_ref.5, bf16[4,512,256]{2,1,0:T(8,128)(2,1)S(1)} %get-tuple-element.22.refs_0_, bf16[4,512,256]{2,1,0:T(8,128)(2,1)S(1)} %get-tuple-element.23.refs_1_), custom_call_target="tpu_custom_call" | custom-call | flops 1 | bytes 1 | tf_op jit(solution)/shard_map/products/pallas_call | solution.py:194
  11.7 0.1 add.14
  11.8 2.1 %collective-permute-start.2 = (bf16[2,512,128]{2,1,0:T(8,128)(2,1)S(1)}, bf16[2,512,128]{2,1,0:T(8,128)(2,1)S(1)}, u32[]{:S(2)}, u32[]{:S(2)}) collective-permute-start(bf16[2,512,128]{2,1,0:T(8,128)(2,1)S(1)} %get-tuple-element.28.refs_2_), channel_id=1, source_target_pairs={{0,2},{1,3},{2,0},{3,1},{4,6},{5,7},{6,4},{7,5},{8,10},{9,11},{10,... | collective-permute-start | bytes 786440 | tf_op jit(solution)/shard_map/ppermute | solution.py:359
  13.9 3.6 %products.5 = (bf16[4,512,256]{2,1,0:T(8,128)(2,1)S(1)}, bf16[4,2,512,512]{3,2,1,0:T(8,128)(2,1)S(1)}) custom-call(s32[66]{0:T(128)S(1)} %pad_add_fusion.where_ref, bf16[2,4,2048,512]{3,2,1,0:T(8,128)(2,1)} %reflection_ref.5, bf16[4,512,256]{2,1,0:T(8,128)(2,1)S(1)} %get-tuple-element.22.refs_0_, bf16[4,512,256]{2,1,0:T(8,128)(2,1)S(1)} %get-tuple-element.23.refs_1_, ...), custom_call_target="tpu_custom_call" | custom-call | flops 1 | bytes 1 | tf_op jit(solution)/shard_map/products/pallas_call | solution.py:194
  17.5 0.1 collective-permute-start.5
  17.6 3.2 %collective-permute-done.2.refs_0_.far_ref = bf16[2,512,128]{2,1,0:T(8,128)(2,1)S(1)} collective-permute-done((bf16[2,512,128]{2,1,0:T(8,128)(2,1)S(1)}, bf16[2,512,128]{2,1,0:T(8,128)(2,1)S(1)}, u32[]{:S(2)}, u32[]{:S(2)}) %collective-permute-start.2) | collective-permute-done | bytes 262176 | tf_op jit(solution)/shard_map/ppermute | solution.py:359
  20.8 0.1 add.15.refs_0_
  21.0 2.3 %collective-permute-start.3 = (bf16[4,512,128]{2,1,0:T(8,128)(2,1)S(1)}, bf16[4,512,128]{2,1,0:T(8,128)(2,1)S(1)}, u32[]{:S(2)}, u32[]{:S(2)}) collective-permute-start(bf16[4,512,128]{2,1,0:T(8,128)(2,1)S(1)} %add.15.refs_0_), channel_id=1, source_target_pairs={{0,2},{1,3},{2,0},{3,1},{4,6},{5,7},{6,4},{7,5},{8,10},{9,11},{10,... | collective-permute-start | bytes 1572872 | tf_op jit(solution)/shard_map/ppermute | solution.py:359
  23.2 0.1 total.4
  23.3 2.3 %collective-permute-start.4 = (bf16[2,512,128]{2,1,0:T(8,128)(2,1)S(1)}, bf16[2,512,128]{2,1,0:T(8,128)(2,1)S(1)}, u32[]{:S(2)}, u32[]{:S(2)}) collective-permute-start(bf16[2,512,128]{2,1,0:T(8,128)(2,1)S(1)} %total.4), channel_id=1, source_target_pairs={{0,18},{1,19},{2,16},{3,17},{4,22},{5,23},{6,20},{7,21},{8,26},{9,... | collective-permute-start | bytes 786440 | tf_op jit(solution)/shard_map/ppermute | solution.py:371
  25.6 1.2 collective-permute-done.5.far_ref
  26.8 0.1 total.5
  26.9 4.1 %collective-permute-start.6 = (bf16[2,512,128]{2,1,0:T(8,128)(2,1)S(1)}, bf16[2,512,128]{2,1,0:T(8,128)(2,1)S(1)}, u32[]{:S(2)}, u32[]{:S(2)}) collective-permute-start(bf16[2,512,128]{2,1,0:T(8,128)(2,1)S(1)} %total.5), channel_id=1, source_target_pairs={{0,18},{1,19},{2,16},{3,17},{4,22},{5,23},{6,20},{7,21},{8,26},{9,... | collective-permute-start | bytes 786440 | tf_op jit(solution)/shard_map/ppermute | solution.py:371
  31.0 0.8 collective-permute-done.4.refs_0_
  31.8 4.8 %collective-permute-done.6.refs_1_ = bf16[2,512,128]{2,1,0:T(8,128)(2,1)S(1)} collective-permute-done((bf16[2,512,128]{2,1,0:T(8,128)(2,1)S(1)}, bf16[2,512,128]{2,1,0:T(8,128)(2,1)S(1)}, u32[]{:S(2)}, u32[]{:S(2)}) %collective-permute-start.6) | collective-permute-done | bytes 262176 | tf_op jit(solution)/shard_map/ppermute | solution.py:371
  36.6 0.7 collective-permute-done.3.far_ref
  37.3 1.4 pack_own.2
  38.7 23.5 %all_to_all.20.traces_ref = bf16[16,64,512]{2,1,0:T(8,128)(2,1)S(1)} all-to-all(bf16[16,64,512]{2,1,0:T(8,128)(2,1)S(1)} %pack_own.2), channel_id=1, replica_groups={{0,4,8,12,32,36,40,44,64,68,72,76,96,100,104,108},{16,20,24,28,48,52,56..., dimensions={0} | all-to-all | bytes 2097152 | tf_op jit(solution)/shard_map/all_to_all | solution.py:425
  62.2 1.8 %window.2 = bf16[32,32,512]{2,1,0:T(8,128)(2,1)S(1)} custom-call(bf16[4,256,256]{2,1,0:T(8,128)(2,1)S(1)} %copy-done.2, s32[4,512]{1,0:T(4,128)S(1)} %copy-done.4, bf16[16,64,512]{2,1,0:T(8,128)(2,1)S(1)} %all_to_all.20.traces_ref), custom_call_target="tpu_custom_call" | custom-call | flops 1 | bytes 1 | tf_op jit(solution)/shard_map/window/pallas_call | solution.py:246
  63.9 23.7 %all_to_all.21 = bf16[32,32,512]{2,1,0:T(8,128)(2,1)S(1)} all-to-all(bf16[32,32,512]{2,1,0:T(8,128)(2,1)S(1)} %window.2), channel_id=1, replica_groups=mesh['freq'=32,'src'=4] {'freq'}, dimensions={0} | all-to-all | bytes 2097152 | tf_op jit(solution)/shard_map/all_to_all | solution.py:429
  87.6 3.3 %products_again.3 = (bf16[4,512,256]{2,1,0:T(8,128)(2,1)S(1)}, bf16[4,512,256]{2,1,0:T(8,128)(2,1)S(1)}, bf16[4,512,256]{2,1,0:T(8,128)(2,1)S(1)}, bf16[4,512,256]{2,1,0:T(8,128)(2,1)S(1)}) custom-call(s32[66]{0:T(128)S(1)} %pad_add_fusion.where_ref, bf16[8,2,512,512]{3,2,1,0:T(8,128)(2,1)S(1)} %get-tuple-element.25.held_ref, ...), custom_call_target="tpu_custom_call" | custom-call | flops 1 | bytes 1 | tf_op jit(solution)/shard_map/products_again/pallas_call | solution.py:231
  91.0 0.5 collective-permute-start.8
  91.5 1.8 %products_again.4.mine_ref = bf16[4,512,256]{2,1,0:T(8,128)(2,1)S(1)} custom-call(s32[66]{0:T(128)S(1)} %pad_add_fusion.where_ref, bf16[4,2,512,512]{3,2,1,0:T(8,128)(2,1)S(1)} %get-tuple-element.24.held_ref, bf16[4,512,256]{2,1,0:T(8,128)(2,1)S(1)} %get-tuple-element.32.refs_0_, bf16[4,512,256]{2,1,0:T(8,128)(2,1)S(1)} %get-tuple-element.33.refs_1_), custom_call_target="tpu_custom_call" | custom-call | flops 1 | bytes 1 | tf_op jit(solution)/shard_map/products_again/pallas_call | solution.py:231
  93.3 0.4 collective-permute-done.7.core_ref
  93.7 0.1 add.16
  93.8 0.6 collective-permute-start.9
  94.4 1.5 collective-permute-start.12
  95.9 1.8 %products_again.5.mine_ref = bf16[4,512,256]{2,1,0:T(8,128)(2,1)S(1)} custom-call(s32[66]{0:T(128)S(1)} %pad_add_fusion.where_ref, bf16[4,2,512,512]{3,2,1,0:T(8,128)(2,1)S(1)} %get-tuple-element.35.held_ref, bf16[4,512,256]{2,1,0:T(8,128)(2,1)S(1)} %get-tuple-element.32.refs_0_, bf16[4,512,256]{2,1,0:T(8,128)(2,1)S(1)} %get-tuple-element.33.refs_1_, ...), custom_call_target="tpu_custom_call" | custom-call | flops 1 | bytes 1 | tf_op jit(solution)/shard_map/products_again/pallas_call | solution.py:231
  97.7 5.3 %collective-permute-done.9.refs_0_.far_ref = bf16[2,512,128]{2,1,0:T(8,128)(2,1)S(1)} collective-permute-done((bf16[2,512,128]{2,1,0:T(8,128)(2,1)S(1)}, bf16[2,512,128]{2,1,0:T(8,128)(2,1)S(1)}, u32[]{:S(2)}, u32[]{:S(2)}) %collective-permute-start.9) | collective-permute-done | bytes 262176 | tf_op jit(solution)/shard_map/ppermute | solution.py:359
  103.0 0.1 add.17.refs_0_
  103.2 0.6 collective-permute-start.10
  103.7 0.1 total.6
  103.8 1.0 collective-permute-start.11
  104.8 3.8 %collective-permute-done.12.far_ref = bf16[2,512,128]{2,1,0:T(8,128)(2,1)S(1)} collective-permute-done((bf16[2,512,128]{2,1,0:T(8,128)(2,1)S(1)}, bf16[2,512,128]{2,1,0:T(8,128)(2,1)S(1)}, u32[]{:S(2)}, u32[]{:S(2)}) %collective-permute-start.12) | collective-permute-done | bytes 262176 | tf_op jit(solution)/shard_map/ppermute | solution.py:359
  108.6 0.1 total.7
  108.7 0.5 collective-permute-start.13
  109.3 2.6 %collective-permute-done.11.refs_0_ = bf16[2,512,128]{2,1,0:T(8,128)(2,1)S(1)} collective-permute-done((bf16[2,512,128]{2,1,0:T(8,128)(2,1)S(1)}, bf16[2,512,128]{2,1,0:T(8,128)(2,1)S(1)}, u32[]{:S(2)}, u32[]{:S(2)}) %collective-permute-start.11) | collective-permute-done | bytes 262176 | tf_op jit(solution)/shard_map/ppermute | solution.py:371
  111.9 5.3 %collective-permute-done.13.refs_1_ = bf16[2,512,128]{2,1,0:T(8,128)(2,1)S(1)} collective-permute-done((bf16[2,512,128]{2,1,0:T(8,128)(2,1)S(1)}, bf16[2,512,128]{2,1,0:T(8,128)(2,1)S(1)}, u32[]{:S(2)}, u32[]{:S(2)}) %collective-permute-start.13) | collective-permute-done | bytes 262176 | tf_op jit(solution)/shard_map/ppermute | solution.py:371
  117.2 1.9 %collective-permute-done.10.far_ref = bf16[4,512,128]{2,1,0:T(8,128)(2,1)S(1)} collective-permute-done((bf16[4,512,128]{2,1,0:T(8,128)(2,1)S(1)}, bf16[4,512,128]{2,1,0:T(8,128)(2,1)S(1)}, u32[]{:S(2)}, u32[]{:S(2)}) %collective-permute-start.10) | collective-permute-done | bytes 524320 | tf_op jit(solution)/shard_map/ppermute | solution.py:359
  119.1 1.4 pack_own.3
  120.5 20.1 %all_to_all.22.traces_ref = bf16[16,64,512]{2,1,0:T(8,128)(2,1)S(1)} all-to-all(bf16[16,64,512]{2,1,0:T(8,128)(2,1)S(1)} %pack_own.3), channel_id=1, replica_groups={{0,4,8,12,32,36,40,44,64,68,72,76,96,100,104,108},{16,20,24,28,48,52,56..., dimensions={0} | all-to-all | bytes 2097152 | tf_op jit(solution)/shard_map/all_to_all | solution.py:425
  140.6 1.8 %window.3 = bf16[32,32,512]{2,1,0:T(8,128)(2,1)S(1)} custom-call(bf16[4,256,256]{2,1,0:T(8,128)(2,1)S(1)} %copy-done.2, s32[4,512]{1,0:T(4,128)S(1)} %copy-done.4, bf16[16,64,512]{2,1,0:T(8,128)(2,1)S(1)} %all_to_all.22.traces_ref), custom_call_target="tpu_custom_call" | custom-call | flops 1 | bytes 1 | tf_op jit(solution)/shard_map/window/pallas_call | solution.py:246
  142.4 20.2 %all_to_all.23 = bf16[32,32,512]{2,1,0:T(8,128)(2,1)S(1)} all-to-all(bf16[32,32,512]{2,1,0:T(8,128)(2,1)S(1)} %window.3), channel_id=1, replica_groups=mesh['freq'=32,'src'=4] {'freq'}, dimensions={0} | all-to-all | bytes 2097152 | tf_op jit(solution)/shard_map/all_to_all | solution.py:429
  162.6 1.5 finish.1
  (15 shorter events, 0.3 us)
Async XLA Ops:
  0.8 1.2 copy-start
  7.5 4.2 %collective-permute-start = (bf16[4,512,256]{2,1,0:T(8,128)(2,1)S(1)}, bf16[4,512,256]{2,1,0:T(8,128)(2,1)S(1)}, u32[]{:S(2)}, u32[]{:S(2)}) collective-permute-start(bf16[4,512,256]{2,1,0:T(8,128)(2,1)S(1)} %get-tuple-element.27), channel_id=1, source_target_pairs={{0,1},{1,0},{2,3},{3,2},{4,5},{5,4},{6,7},{7,6},{8,9},{9,8},{10,11... | collective-permute-start | bytes 3145736 | tf_op jit(solution)/shard_map/ppermute | solution.py:359
  7.6 10.0 %collective-permute-start.1 = (bf16[4,512,256]{2,1,0:T(8,128)(2,1)S(1)}, bf16[4,512,256]{2,1,0:T(8,128)(2,1)S(1)}, u32[]{:S(2)}, u32[]{:S(2)}) collective-permute-start(bf16[4,512,256]{2,1,0:T(8,128)(2,1)S(1)} %get-tuple-element.31), channel_id=1, source_target_pairs={{0,1},{1,0},{2,3},{3,2},{4,5},{5,4},{6,7},{7,6},{8,9},{9,8},{10,11... | collective-permute-start | bytes 3145736 | tf_op jit(solution)/shard_map/ppermute | solution.py:359
  11.8 9.0 %collective-permute-start.2 = (bf16[2,512,128]{2,1,0:T(8,128)(2,1)S(1)}, bf16[2,512,128]{2,1,0:T(8,128)(2,1)S(1)}, u32[]{:S(2)}, u32[]{:S(2)}) collective-permute-start(bf16[2,512,128]{2,1,0:T(8,128)(2,1)S(1)} %get-tuple-element.28.refs_2_), channel_id=1, source_target_pairs={{0,2},{1,3},{2,0},{3,1},{4,6},{5,7},{6,4},{7,5},{8,10},{9,11},{10,... | collective-permute-start | bytes 786440 | tf_op jit(solution)/shard_map/ppermute | solution.py:359
  17.5 19.8 %copy-start.3 = (bf16[512,512]{1,0:T(8,128)(2,1)S(1)}, bf16[512,512]{1,0:T(8,128)(2,1)}, u32[]{:S(2)}) copy-start(bf16[512,512]{1,0:T(8,128)(2,1)} %constant.39.clone.pack_ref) | copy-start | bytes 1572868
  17.5 44.7 %copy-start.2 = (bf16[4,256,256]{2,1,0:T(8,128)(2,1)S(1)}, bf16[4,256,256]{2,1,0:T(8,128)(2,1)}, u32[]{:S(2)}) copy-start(bf16[4,256,256]{2,1,0:T(8,128)(2,1)} %constant.40.clone.dft_ref) | copy-start | bytes 1572868
  17.5 44.7 %copy-start.4 = (s32[4,512]{1,0:T(4,128)S(1)}, s32[4,512]{1,0:T(4,128)}, u32[]{:S(2)}) copy-start(s32[4,512]{1,0:T(4,128)} %onsets_ref.3) | copy-start | bytes 24580
  17.5 9.3 %collective-permute-start.5 = (bf16[2,512,128]{2,1,0:T(8,128)(2,1)S(1)}, bf16[2,512,128]{2,1,0:T(8,128)(2,1)S(1)}, u32[]{:S(2)}, u32[]{:S(2)}) collective-permute-start(bf16[2,512,128]{2,1,0:T(8,128)(2,1)S(1)} %get-tuple-element.29.refs_3_), channel_id=1, source_target_pairs={{0,2},{1,3},{2,0},{3,1},{4,6},{5,7},{6,4},{7,5},{8,10},{9,11},{10,... | collective-permute-start | bytes 786440 | tf_op jit(solution)/shard_map/ppermute | solution.py:359
  20.9 66.7 %copy-start.1 = (bf16[2,4,128,512]{3,2,1,0:T(8,128)(2,1)S(1)}, bf16[2,4,128,512]{3,2,1,0:T(8,128)(2,1)}, u32[]{:S(2)}) copy-start(bf16[2,4,128,512]{3,2,1,0:T(8,128)(2,1)} %initial_ref.1) | copy-start | bytes 3145732
  21.0 16.3 %collective-permute-start.3 = (bf16[4,512,128]{2,1,0:T(8,128)(2,1)S(1)}, bf16[4,512,128]{2,1,0:T(8,128)(2,1)S(1)}, u32[]{:S(2)}, u32[]{:S(2)}) collective-permute-start(bf16[4,512,128]{2,1,0:T(8,128)(2,1)S(1)} %add.15.refs_0_), channel_id=1, source_target_pairs={{0,2},{1,3},{2,0},{3,1},{4,6},{5,7},{6,4},{7,5},{8,10},{9,11},{10,... | collective-permute-start | bytes 1572872 | tf_op jit(solution)/shard_map/ppermute | solution.py:359
  23.3 8.4 %collective-permute-start.4 = (bf16[2,512,128]{2,1,0:T(8,128)(2,1)S(1)}, bf16[2,512,128]{2,1,0:T(8,128)(2,1)S(1)}, u32[]{:S(2)}, u32[]{:S(2)}) collective-permute-start(bf16[2,512,128]{2,1,0:T(8,128)(2,1)S(1)} %total.4), channel_id=1, source_target_pairs={{0,18},{1,19},{2,16},{3,17},{4,22},{5,23},{6,20},{7,21},{8,26},{9,... | collective-permute-start | bytes 786440 | tf_op jit(solution)/shard_map/ppermute | solution.py:371
  26.9 9.7 %collective-permute-start.6 = (bf16[2,512,128]{2,1,0:T(8,128)(2,1)S(1)}, bf16[2,512,128]{2,1,0:T(8,128)(2,1)S(1)}, u32[]{:S(2)}, u32[]{:S(2)}) collective-permute-start(bf16[2,512,128]{2,1,0:T(8,128)(2,1)S(1)} %total.5), channel_id=1, source_target_pairs={{0,18},{1,19},{2,16},{3,17},{4,22},{5,23},{6,20},{7,21},{8,26},{9,... | collective-permute-start | bytes 786440 | tf_op jit(solution)/shard_map/ppermute | solution.py:371
  90.9 2.7 %collective-permute-start.7 = (bf16[4,512,256]{2,1,0:T(8,128)(2,1)S(1)}, bf16[4,512,256]{2,1,0:T(8,128)(2,1)S(1)}, u32[]{:S(2)}, u32[]{:S(2)}) collective-permute-start(bf16[4,512,256]{2,1,0:T(8,128)(2,1)S(1)} %get-tuple-element.34), channel_id=1, source_target_pairs={{0,1},{1,0},{2,3},{3,2},{4,5},{5,4},{6,7},{7,6},{8,9},{9,8},{10,11... | collective-permute-start | bytes 3145736 | tf_op jit(solution)/shard_map/ppermute | solution.py:359
  91.0 6.7 %collective-permute-start.8 = (bf16[4,512,256]{2,1,0:T(8,128)(2,1)S(1)}, bf16[4,512,256]{2,1,0:T(8,128)(2,1)S(1)}, u32[]{:S(2)}, u32[]{:S(2)}) collective-permute-start(bf16[4,512,256]{2,1,0:T(8,128)(2,1)S(1)} %get-tuple-element.38), channel_id=1, source_target_pairs={{0,1},{1,0},{2,3},{3,2},{4,5},{5,4},{6,7},{7,6},{8,9},{9,8},{10,11... | collective-permute-start | bytes 3145736 | tf_op jit(solution)/shard_map/ppermute | solution.py:359
  93.8 9.2 %collective-permute-start.9 = (bf16[2,512,128]{2,1,0:T(8,128)(2,1)S(1)}, bf16[2,512,128]{2,1,0:T(8,128)(2,1)S(1)}, u32[]{:S(2)}, u32[]{:S(2)}) collective-permute-start(bf16[2,512,128]{2,1,0:T(8,128)(2,1)S(1)} %get-tuple-element.36.refs_2_), channel_id=1, source_target_pairs={{0,2},{1,3},{2,0},{3,1},{4,6},{5,7},{6,4},{7,5},{8,10},{9,11},{10,... | collective-permute-start | bytes 786440 | tf_op jit(solution)/shard_map/ppermute | solution.py:359
  94.4 14.3 %collective-permute-start.12 = (bf16[2,512,128]{2,1,0:T(8,128)(2,1)S(1)}, bf16[2,512,128]{2,1,0:T(8,128)(2,1)S(1)}, u32[]{:S(2)}, u32[]{:S(2)}) collective-permute-start(bf16[2,512,128]{2,1,0:T(8,128)(2,1)S(1)} %get-tuple-element.37.refs_3_), channel_id=1, source_target_pairs={{0,2},{1,3},{2,0},{3,1},{4,6},{5,7},{6,4},{7,5},{8,10},{9,11},{10,... | collective-permute-start | bytes 786440 | tf_op jit(solution)/shard_map/ppermute | solution.py:359
  103.2 15.9 %collective-permute-start.10 = (bf16[4,512,128]{2,1,0:T(8,128)(2,1)S(1)}, bf16[4,512,128]{2,1,0:T(8,128)(2,1)S(1)}, u32[]{:S(2)}, u32[]{:S(2)}) collective-permute-start(bf16[4,512,128]{2,1,0:T(8,128)(2,1)S(1)} %add.17.refs_0_), channel_id=1, source_target_pairs={{0,2},{1,3},{2,0},{3,1},{4,6},{5,7},{6,4},{7,5},{8,10},{9,11},{10,... | collective-permute-start | bytes 1572872 | tf_op jit(solution)/shard_map/ppermute | solution.py:359
  103.8 8.1 %collective-permute-start.11 = (bf16[2,512,128]{2,1,0:T(8,128)(2,1)S(1)}, bf16[2,512,128]{2,1,0:T(8,128)(2,1)S(1)}, u32[]{:S(2)}, u32[]{:S(2)}) collective-permute-start(bf16[2,512,128]{2,1,0:T(8,128)(2,1)S(1)} %total.6), channel_id=1, source_target_pairs={{0,18},{1,19},{2,16},{3,17},{4,22},{5,23},{6,20},{7,21},{8,26},{9,... | collective-permute-start | bytes 786440 | tf_op jit(solution)/shard_map/ppermute | solution.py:371
  108.7 8.4 %collective-permute-start.13 = (bf16[2,512,128]{2,1,0:T(8,128)(2,1)S(1)}, bf16[2,512,128]{2,1,0:T(8,128)(2,1)S(1)}, u32[]{:S(2)}, u32[]{:S(2)}) collective-permute-start(bf16[2,512,128]{2,1,0:T(8,128)(2,1)S(1)} %total.7), channel_id=1, source_target_pairs={{0,18},{1,19},{2,16},{3,17},{4,22},{5,23},{6,20},{7,21},{8,26},{9,... | collective-permute-start | bytes 786440 | tf_op jit(solution)/shard_map/ppermute | solution.py:371

commit v4 on v3

--- a/solution.py
+++ b/solution.py
@@ -258,19 +258,24 @@
     outs = refs[tokens:]
     lanes = outs[0].shape[2]
     here = slice(place * lanes, (place + 1) * lanes)
-    for index, out_ref in enumerate(outs):
-        count = out_ref.shape[0]
-        some = slice(index * count, (index + 1) * count)
-        total = mine_ref[some, :, here].astype(jnp.float32) + core_ref[some, :, here].astype(jnp.float32)
+    low = 0
+    for out_ref in outs:
+        some = slice(low, low + out_ref.shape[1])
+        low += out_ref.shape[1]
+        total = mine_ref[:, some, here].astype(jnp.float32) + core_ref[:, some, here].astype(jnp.float32)
         out_ref[...] = total.astype(BF)
 
 
-def total_kernel(index, mine_ref, core_ref, far_ref, *refs):
+def total_kernel(index, pack_ref, mine_ref, core_ref, far_ref, *refs):
     out_ref = refs[-1]
-    count, _, lanes = out_ref.shape
+    nfreq, count, lanes = far_ref.shape
     some = slice(index * count, (index + 1) * count)
-    total = mine_ref[some, :, lanes:].astype(jnp.float32) + core_ref[some, :, lanes:].astype(jnp.float32)
-    out_ref[...] = (total + far_ref[...].astype(jnp.float32)).astype(BF)
+    parts = []
+    for f in range(nfreq):
+        total = mine_ref[f, some, lanes:].astype(jnp.float32) + core_ref[f, some, lanes:].astype(jnp.float32)
+        parts.append((total + far_ref[f].astype(jnp.float32)).astype(BF))
+    packed = nt(pack_ref[...], jnp.concatenate(parts, axis=1))
+    out_ref[...] = packed.reshape(out_ref.shape).astype(BF)
 
 
 def pack_own_kernel(where_ref, pack_ref, mine_ref, core_ref, far_ref, *refs):
@@ -278,14 +283,14 @@
     nfreq, width, lanes = far_ref.shape
     group = 2 * nfreq
     mine = where_ref[1] == 0
-    outer = [ref[f] for ref in outer_refs for f in range(ref.shape[0])]
-    halves = [[], []]
+    parts = []
     for f in range(nfreq):
         total = mine_ref[f, :, :lanes].astype(jnp.float32) + core_ref[f, :, :lanes].astype(jnp.float32)
-        own = (total + far_ref[f].astype(jnp.float32)).astype(BF)
-        halves[0].append(jnp.where(mine, own, outer[f]))
-        halves[1].append(jnp.where(mine, outer[f], own))
-    packed = [nt(pack_ref[...], jnp.concatenate(parts, axis=1)) for parts in halves]
+        parts.append((total + far_ref[f].astype(jnp.float32)).astype(BF))
+    own = nt(pack_ref[...], jnp.concatenate(parts, axis=1))
+    outer = [ref[...].astype(jnp.float32).reshape(own.shape[0], ref.shape[2]) for ref in outer_refs]
+    outer = jnp.concatenate(outer, axis=1)
+    packed = [jnp.where(mine, own, outer), jnp.where(mine, outer, own)]
     packed = [part.reshape(part.shape[0] // group, group, width) for part in packed]
     out_ref[...] = jnp.stack(packed, axis=1).reshape(out_ref.shape).astype(BF)
 
@@ -308,14 +313,22 @@
     rows = rows // focal
     nfreq = dft_ref.shape[1] // 2
     step = lax.broadcasted_iota(jnp.int32, (nfreq, width), 0)
+    size = dft_ref.shape[1]
+    to_time = dft_ref[0:2].reshape(2 * size, size)
+    to_freq = dft_ref[2:4].reshape(2 * size, size)
+
+    def twice(parts, values):
+        both = mm(parts, values)
+        return both[:size] + both[size:]
+
     results = []
     for j in range(focal):
         column = traces_ref[:, j * rows : (j + 1) * rows, :].reshape(2 * nfreq, width)
-        time = mm(dft_ref[0], column) + mm(dft_ref[1], column)
+        time = twice(to_time, column)
         keep = step < onsets_ref[j : j + 1, :]
         keep = jnp.concatenate([keep, keep], axis=0)
         time = jnp.where(keep, time, 0.0).astype(BF)
-        back = mm(dft_ref[2], time) + mm(dft_ref[3], time)
+        back = twice(to_freq, time)
         results.append(back.reshape(2 * devices, rows // 2, width))
     out_ref[...] = jnp.stack(results, axis=1).reshape(out_ref.shape).astype(BF)
 
@@ -389,7 +402,8 @@
     ]
     block_rows = focal_block * freq_local * planes
     part = (freq_local, sources, focal)
-    cut = (freq_local // CUTS, sources, focal)
+    cut = (freq_local, sources // CUTS, focal)
+    packed_cut = (devices // 2, block_rows, sources // CUTS)
 
     focal_rows = rows * focal_block
     held = []
@@ -417,7 +431,7 @@
         outer = []
         for index, far in enumerate(far_other):
             (other,) = call(
-                functools.partial(total_kernel, index), "total", [cut], remote, core_far, far, after=(total,)
+                functools.partial(total_kernel, index), "total", [packed_cut], pack, remote, core_far, far, after=(total,)
             )
             outer.append(outward(other, columns, rows))
         shape = (devices // 2, 2 * block_rows, sources)

time: 165 us -> 164 us (level)
  transfers between devices with their start and end apart: 14 -> 14, of which waited for: 11 -> 11; matrix products, arithmetic and copies ran while one was open for 0% -> 0% of each run, Pallas kernels for 7% -> 8%
where the time goes in v4:
time: 164 us
  blocking collectives  87.6 us (53%)
  waiting for transfers between devices  29 us (18%)
  Pallas kernels  28.5 us (17%)
  starting transfers between devices  16.1 us (10%)
  local copies, waits for them, and re-layouts  2.01 us (1%)
    all_to_all x2, blocking collectives, local(): update = lax.all_to_all(truncated, 'freq', 0, 0, tiled=True)  43.9 us
    all_to_all x2, blocking collectives, local(): lax.all_to_all(responses, 'freq', 0, 0, tiled=True, axis_index_groups=pla...  43.7 us
    ppermute x10, waiting for transfers between devices, swap(): lax.ppermute(values, 'src', [(i, i ^ bit) for i in range(lax.axis_size('s...  15.5 us
    ppermute x4, waiting for transfers between devices, outward(): return lax.ppermute(values, ('freq', 'src'), pairs)  13.6 us
    pallas_call x3, Pallas kernels, products(): pl.pallas_call(functools.partial(product_kernel, polarity, rels, build, l...  12.5 us
    ppermute x10, starting transfers between devices, swap(): lax.ppermute(values, 'src', [(i, i ^ bit) for i in range(lax.axis_size('s...  8.21 us
    ppermute x4, starting transfers between devices, outward(): return lax.ppermute(values, ('freq', 'src'), pairs)  7.9 us
    pallas_call x3, Pallas kernels, products_again(): pl.pallas_call(functools.partial(product_again_kernel, polarity, build, l...  6.88 us
  transfers between devices with their start and end apart: 14, of which 11 were waited for; matrix products, arithmetic and copies ran while one was open for 0% of the time, Pallas kernels for 8%

profile of v4, /device:TPU:0, one launch (start us, length us, event | category | flops | bytes accessed | tf_op | source)
XLA Modules:
  0.0 163.7 jit_solution(1452486413072223988)
XLA Ops:
  0.0 0.8 reshape.9
  0.8 1.2 copy-done.1
  2.1 5.4 %products.3 = (bf16[4,512,256]{2,1,0:T(8,128)(2,1)S(1)}, bf16[4,512,256]{2,1,0:T(8,128)(2,1)S(1)}, bf16[8,2,512,512]{3,2,1,0:T(8,128)(2,1)S(1)}, bf16[4,512,256]...) custom-call(s32[66]{0:T(128)S(1)} %pad_add_fusion.where_ref, bf16[2,4,2048,512]{3,2,1,0:T(8,128)(2,1)} %reflection_ref.5, ...), custom_call_target="tpu_custom_call" | custom-call | flops 1 | bytes 1 | tf_op jit(solution)/shard_map/products/pallas_call | solution.py:194
  7.6 0.5 collective-permute-start.1
  8.1 3.6 %products.4 = (bf16[4,512,256]{2,1,0:T(8,128)(2,1)S(1)}, bf16[4,2,512,512]{3,2,1,0:T(8,128)(2,1)S(1)}) custom-call(s32[66]{0:T(128)S(1)} %pad_add_fusion.where_ref, bf16[2,4,2048,512]{3,2,1,0:T(8,128)(2,1)} %reflection_ref.5, bf16[4,512,256]{2,1,0:T(8,128)(2,1)S(1)} %get-tuple-element.22.refs_0_, bf16[4,512,256]{2,1,0:T(8,128)(2,1)S(1)} %get-tuple-element.23.refs_1_), custom_call_target="tpu_custom_call" | custom-call | flops 1 | bytes 1 | tf_op jit(solution)/shard_map/products/pallas_call | solution.py:194
  11.7 0.1 add.14
  11.8 2.1 %collective-permute-start.2 = (bf16[4,256,128]{2,1,0:T(8,128)(2,1)S(1)}, bf16[4,256,128]{2,1,0:T(8,128)(2,1)S(1)}, u32[]{:S(2)}, u32[]{:S(2)}) collective-permute-start(bf16[4,256,128]{2,1,0:T(8,128)(2,1)S(1)} %get-tuple-element.28.refs_2_), channel_id=1, source_target_pairs={{0,2},{1,3},{2,0},{3,1},{4,6},{5,7},{6,4},{7,5},{8,10},{9,11},{10,... | collective-permute-start | bytes 786440 | tf_op jit(solution)/shard_map/ppermute | solution.py:372
  13.9 3.6 %products.5 = (bf16[4,512,256]{2,1,0:T(8,128)(2,1)S(1)}, bf16[4,2,512,512]{3,2,1,0:T(8,128)(2,1)S(1)}) custom-call(s32[66]{0:T(128)S(1)} %pad_add_fusion.where_ref, bf16[2,4,2048,512]{3,2,1,0:T(8,128)(2,1)} %reflection_ref.5, bf16[4,512,256]{2,1,0:T(8,128)(2,1)S(1)} %get-tuple-element.22.refs_0_, bf16[4,512,256]{2,1,0:T(8,128)(2,1)S(1)} %get-tuple-element.23.refs_1_, ...), custom_call_target="tpu_custom_call" | custom-call | flops 1 | bytes 1 | tf_op jit(solution)/shard_map/products/pallas_call | solution.py:194
  17.4 0.1 collective-permute-start.5
  17.6 3.3 %collective-permute-done.2.refs_0_.far_ref = bf16[4,256,128]{2,1,0:T(8,128)(2,1)S(1)} collective-permute-done((bf16[4,256,128]{2,1,0:T(8,128)(2,1)S(1)}, bf16[4,256,128]{2,1,0:T(8,128)(2,1)S(1)}, u32[]{:S(2)}, u32[]{:S(2)}) %collective-permute-start.2) | collective-permute-done | bytes 262176 | tf_op jit(solution)/shard_map/ppermute | solution.py:372
  20.9 0.1 add.15.refs_0_
  21.0 2.3 %collective-permute-start.3 = (bf16[4,512,128]{2,1,0:T(8,128)(2,1)S(1)}, bf16[4,512,128]{2,1,0:T(8,128)(2,1)S(1)}, u32[]{:S(2)}, u32[]{:S(2)}) collective-permute-start(bf16[4,512,128]{2,1,0:T(8,128)(2,1)S(1)} %add.15.refs_0_), channel_id=1, source_target_pairs={{0,2},{1,3},{2,0},{3,1},{4,6},{5,7},{6,4},{7,5},{8,10},{9,11},{10,... | collective-permute-start | bytes 1572872 | tf_op jit(solution)/shard_map/ppermute | solution.py:372
  23.2 0.4 total.4
  23.6 2.3 %collective-permute-start.4 = (bf16[16,32,256]{2,1,0:T(8,128)(2,1)S(1)}, bf16[16,32,256]{2,1,0:T(8,128)(2,1)S(1)}, u32[]{:S(2)}, u32[]{:S(2)}) collective-permute-start(bf16[16,32,256]{2,1,0:T(8,128)(2,1)S(1)} %total.4), channel_id=1, source_target_pairs={{0,18},{1,19},{2,16},{3,17},{4,22},{5,23},{6,20},{7,21},{8,26},{9,... | collective-permute-start | bytes 786440 | tf_op jit(solution)/shard_map/ppermute | solution.py:384
  25.9 0.8 collective-permute-done.5.far_ref
  26.7 0.4 total.5
  27.1 4.1 %collective-permute-start.6 = (bf16[16,32,256]{2,1,0:T(8,128)(2,1)S(1)}, bf16[16,32,256]{2,1,0:T(8,128)(2,1)S(1)}, u32[]{:S(2)}, u32[]{:S(2)}) collective-permute-start(bf16[16,32,256]{2,1,0:T(8,128)(2,1)S(1)} %total.5), channel_id=1, source_target_pairs={{0,18},{1,19},{2,16},{3,17},{4,22},{5,23},{6,20},{7,21},{8,26},{9,... | collective-permute-start | bytes 786440 | tf_op jit(solution)/shard_map/ppermute | solution.py:384
  31.2 0.8 collective-permute-done.4.refs_0_
  32.1 4.8 %collective-permute-done.6.refs_1_ = bf16[16,32,256]{2,1,0:T(8,128)(2,1)S(1)} collective-permute-done((bf16[16,32,256]{2,1,0:T(8,128)(2,1)S(1)}, bf16[16,32,256]{2,1,0:T(8,128)(2,1)S(1)}, u32[]{:S(2)}, u32[]{:S(2)}) %collective-permute-start.6) | collective-permute-done | bytes 262176 | tf_op jit(solution)/shard_map/ppermute | solution.py:384
  36.9 0.4 collective-permute-done.3.far_ref
  37.3 1.0 pack_own.2
  38.3 23.5 %all_to_all.20.traces_ref = bf16[16,64,512]{2,1,0:T(8,128)(2,1)S(1)} all-to-all(bf16[16,64,512]{2,1,0:T(8,128)(2,1)S(1)} %pack_own.2), channel_id=1, replica_groups={{0,4,8,12,32,36,40,44,64,68,72,76,96,100,104,108},{16,20,24,28,48,52,56..., dimensions={0} | all-to-all | bytes 2097152 | tf_op jit(solution)/shard_map/all_to_all | solution.py:439
  61.9 1.8 %window.2 = bf16[32,32,512]{2,1,0:T(8,128)(2,1)S(1)} custom-call(bf16[4,256,256]{2,1,0:T(8,128)(2,1)S(1)} %copy-done.3, s32[4,512]{1,0:T(4,128)S(1)} %copy-done.4, bf16[16,64,512]{2,1,0:T(8,128)(2,1)S(1)} %all_to_all.20.traces_ref), custom_call_target="tpu_custom_call" | custom-call | flops 1 | bytes 1 | tf_op jit(solution)/shard_map/window/pallas_call | solution.py:246
  63.6 23.7 %all_to_all.21 = bf16[32,32,512]{2,1,0:T(8,128)(2,1)S(1)} all-to-all(bf16[32,32,512]{2,1,0:T(8,128)(2,1)S(1)} %window.2), channel_id=1, replica_groups=mesh['freq'=32,'src'=4] {'freq'}, dimensions={0} | all-to-all | bytes 2097152 | tf_op jit(solution)/shard_map/all_to_all | solution.py:443
  87.4 3.3 %products_again.3 = (bf16[4,512,256]{2,1,0:T(8,128)(2,1)S(1)}, bf16[4,512,256]{2,1,0:T(8,128)(2,1)S(1)}, bf16[4,512,256]{2,1,0:T(8,128)(2,1)S(1)}, bf16[4,512,256]{2,1,0:T(8,128)(2,1)S(1)}) custom-call(s32[66]{0:T(128)S(1)} %pad_add_fusion.where_ref, bf16[8,2,512,512]{3,2,1,0:T(8,128)(2,1)S(1)} %get-tuple-element.25.held_ref, ...), custom_call_target="tpu_custom_call" | custom-call | flops 1 | bytes 1 | tf_op jit(solution)/shard_map/products_again/pallas_call | solution.py:231
  90.8 0.5 collective-permute-start.8
  91.3 1.8 %products_again.4.mine_ref = bf16[4,512,256]{2,1,0:T(8,128)(2,1)S(1)} custom-call(s32[66]{0:T(128)S(1)} %pad_add_fusion.where_ref, bf16[4,2,512,512]{3,2,1,0:T(8,128)(2,1)S(1)} %get-tuple-element.24.held_ref, bf16[4,512,256]{2,1,0:T(8,128)(2,1)S(1)} %get-tuple-element.32.refs_0_, bf16[4,512,256]{2,1,0:T(8,128)(2,1)S(1)} %get-tuple-element.33.refs_1_), custom_call_target="tpu_custom_call" | custom-call | flops 1 | bytes 1 | tf_op jit(solution)/shard_map/products_again/pallas_call | solution.py:231
  93.1 0.4 collective-permute-done.7.core_ref
  93.4 0.1 add.16
  93.6 0.5 collective-permute-start.9
  94.0 1.6 collective-permute-start.12
  95.7 1.8 %products_again.5.mine_ref = bf16[4,512,256]{2,1,0:T(8,128)(2,1)S(1)} custom-call(s32[66]{0:T(128)S(1)} %pad_add_fusion.where_ref, bf16[4,2,512,512]{3,2,1,0:T(8,128)(2,1)S(1)} %get-tuple-element.35.held_ref, bf16[4,512,256]{2,1,0:T(8,128)(2,1)S(1)} %get-tuple-element.32.refs_0_, bf16[4,512,256]{2,1,0:T(8,128)(2,1)S(1)} %get-tuple-element.33.refs_1_, ...), custom_call_target="tpu_custom_call" | custom-call | flops 1 | bytes 1 | tf_op jit(solution)/shard_map/products_again/pallas_call | solution.py:231
  97.5 5.3 %collective-permute-done.9.refs_0_.far_ref = bf16[4,256,128]{2,1,0:T(8,128)(2,1)S(1)} collective-permute-done((bf16[4,256,128]{2,1,0:T(8,128)(2,1)S(1)}, bf16[4,256,128]{2,1,0:T(8,128)(2,1)S(1)}, u32[]{:S(2)}, u32[]{:S(2)}) %collective-permute-start.9) | collective-permute-done | bytes 262176 | tf_op jit(solution)/shard_map/ppermute | solution.py:372
  102.8 0.1 add.17.refs_0_
  102.9 0.5 collective-permute-start.10
  103.4 0.4 total.6
  103.8 1.1 collective-permute-start.11
  104.8 3.6 %collective-permute-done.12.far_ref = bf16[4,256,128]{2,1,0:T(8,128)(2,1)S(1)} collective-permute-done((bf16[4,256,128]{2,1,0:T(8,128)(2,1)S(1)}, bf16[4,256,128]{2,1,0:T(8,128)(2,1)S(1)}, u32[]{:S(2)}, u32[]{:S(2)}) %collective-permute-start.12) | collective-permute-done | bytes 262176 | tf_op jit(solution)/shard_map/ppermute | solution.py:372
  108.4 0.4 total.7
  108.8 0.4 collective-permute-start.13
  109.2 2.5 %collective-permute-done.11.refs_0_ = bf16[16,32,256]{2,1,0:T(8,128)(2,1)S(1)} collective-permute-done((bf16[16,32,256]{2,1,0:T(8,128)(2,1)S(1)}, bf16[16,32,256]{2,1,0:T(8,128)(2,1)S(1)}, u32[]{:S(2)}, u32[]{:S(2)}) %collective-permute-start.11) | collective-permute-done | bytes 262176 | tf_op jit(solution)/shard_map/ppermute | solution.py:384
  111.7 5.4 %collective-permute-done.13.refs_1_ = bf16[16,32,256]{2,1,0:T(8,128)(2,1)S(1)} collective-permute-done((bf16[16,32,256]{2,1,0:T(8,128)(2,1)S(1)}, bf16[16,32,256]{2,1,0:T(8,128)(2,1)S(1)}, u32[]{:S(2)}, u32[]{:S(2)}) %collective-permute-start.13) | collective-permute-done | bytes 262176 | tf_op jit(solution)/shard_map/ppermute | solution.py:384
  117.1 1.7 %collective-permute-done.10.far_ref = bf16[4,512,128]{2,1,0:T(8,128)(2,1)S(1)} collective-permute-done((bf16[4,512,128]{2,1,0:T(8,128)(2,1)S(1)}, bf16[4,512,128]{2,1,0:T(8,128)(2,1)S(1)}, u32[]{:S(2)}, u32[]{:S(2)}) %collective-permute-start.10) | collective-permute-done | bytes 524320 | tf_op jit(solution)/shard_map/ppermute | solution.py:372
  118.8 1.0 pack_own.3
  119.9 20.1 %all_to_all.22.traces_ref = bf16[16,64,512]{2,1,0:T(8,128)(2,1)S(1)} all-to-all(bf16[16,64,512]{2,1,0:T(8,128)(2,1)S(1)} %pack_own.3), channel_id=1, replica_groups={{0,4,8,12,32,36,40,44,64,68,72,76,96,100,104,108},{16,20,24,28,48,52,56..., dimensions={0} | all-to-all | bytes 2097152 | tf_op jit(solution)/shard_map/all_to_all | solution.py:439
  140.0 1.8 %window.3 = bf16[32,32,512]{2,1,0:T(8,128)(2,1)S(1)} custom-call(bf16[4,256,256]{2,1,0:T(8,128)(2,1)S(1)} %copy-done.3, s32[4,512]{1,0:T(4,128)S(1)} %copy-done.4, bf16[16,64,512]{2,1,0:T(8,128)(2,1)S(1)} %all_to_all.22.traces_ref), custom_call_target="tpu_custom_call" | custom-call | flops 1 | bytes 1 | tf_op jit(solution)/shard_map/window/pallas_call | solution.py:246
  141.8 20.2 %all_to_all.23 = bf16[32,32,512]{2,1,0:T(8,128)(2,1)S(1)} all-to-all(bf16[32,32,512]{2,1,0:T(8,128)(2,1)S(1)} %window.3), channel_id=1, replica_groups=mesh['freq'=32,'src'=4] {'freq'}, dimensions={0} | all-to-all | bytes 2097152 | tf_op jit(solution)/shard_map/all_to_all | solution.py:443
  162.0 1.5 finish.1
  (15 shorter events, 0.3 us)
Async XLA Ops:
  0.8 1.2 copy-start.1
  7.5 4.2 %collective-permute-start = (bf16[4,512,256]{2,1,0:T(8,128)(2,1)S(1)}, bf16[4,512,256]{2,1,0:T(8,128)(2,1)S(1)}, u32[]{:S(2)}, u32[]{:S(2)}) collective-permute-start(bf16[4,512,256]{2,1,0:T(8,128)(2,1)S(1)} %get-tuple-element.27), channel_id=1, source_target_pairs={{0,1},{1,0},{2,3},{3,2},{4,5},{5,4},{6,7},{7,6},{8,9},{9,8},{10,11... | collective-permute-start | bytes 3145736 | tf_op jit(solution)/shard_map/ppermute | solution.py:372
  7.6 10.0 %collective-permute-start.1 = (bf16[4,512,256]{2,1,0:T(8,128)(2,1)S(1)}, bf16[4,512,256]{2,1,0:T(8,128)(2,1)S(1)}, u32[]{:S(2)}, u32[]{:S(2)}) collective-permute-start(bf16[4,512,256]{2,1,0:T(8,128)(2,1)S(1)} %get-tuple-element.31), channel_id=1, source_target_pairs={{0,1},{1,0},{2,3},{3,2},{4,5},{5,4},{6,7},{7,6},{8,9},{9,8},{10,11... | collective-permute-start | bytes 3145736 | tf_op jit(solution)/shard_map/ppermute | solution.py:372
  11.8 9.1 %collective-permute-start.2 = (bf16[4,256,128]{2,1,0:T(8,128)(2,1)S(1)}, bf16[4,256,128]{2,1,0:T(8,128)(2,1)S(1)}, u32[]{:S(2)}, u32[]{:S(2)}) collective-permute-start(bf16[4,256,128]{2,1,0:T(8,128)(2,1)S(1)} %get-tuple-element.28.refs_2_), channel_id=1, source_target_pairs={{0,2},{1,3},{2,0},{3,1},{4,6},{5,7},{6,4},{7,5},{8,10},{9,11},{10,... | collective-permute-start | bytes 786440 | tf_op jit(solution)/shard_map/ppermute | solution.py:372
  13.9 9.4 %copy-start = (bf16[512,512]{1,0:T(8,128)(2,1)S(1)}, bf16[512,512]{1,0:T(8,128)(2,1)}, u32[]{:S(2)}) copy-start(bf16[512,512]{1,0:T(8,128)(2,1)} %constant.39.clone.pack_ref) | copy-start | bytes 1572868
  17.4 9.3 %collective-permute-start.5 = (bf16[4,256,128]{2,1,0:T(8,128)(2,1)S(1)}, bf16[4,256,128]{2,1,0:T(8,128)(2,1)S(1)}, u32[]{:S(2)}, u32[]{:S(2)}) collective-permute-start(bf16[4,256,128]{2,1,0:T(8,128)(2,1)S(1)} %get-tuple-element.29.refs_3_), channel_id=1, source_target_pairs={{0,2},{1,3},{2,0},{3,1},{4,6},{5,7},{6,4},{7,5},{8,10},{9,11},{10,... | collective-permute-start | bytes 786440 | tf_op jit(solution)/shard_map/ppermute | solution.py:372
  20.8 41.0 %copy-start.3 = (bf16[4,256,256]{2,1,0:T(8,128)(2,1)S(1)}, bf16[4,256,256]{2,1,0:T(8,128)(2,1)}, u32[]{:S(2)}) copy-start(bf16[4,256,256]{2,1,0:T(8,128)(2,1)} %constant.40.clone.dft_ref) | copy-start | bytes 1572868
  20.9 41.0 %copy-start.4 = (s32[4,512]{1,0:T(4,128)S(1)}, s32[4,512]{1,0:T(4,128)}, u32[]{:S(2)}) copy-start(s32[4,512]{1,0:T(4,128)} %onsets_ref.3) | copy-start | bytes 24580
  21.0 16.3 %collective-permute-start.3 = (bf16[4,512,128]{2,1,0:T(8,128)(2,1)S(1)}, bf16[4,512,128]{2,1,0:T(8,128)(2,1)S(1)}, u32[]{:S(2)}, u32[]{:S(2)}) collective-permute-start(bf16[4,512,128]{2,1,0:T(8,128)(2,1)S(1)} %add.15.refs_0_), channel_id=1, source_target_pairs={{0,2},{1,3},{2,0},{3,1},{4,6},{5,7},{6,4},{7,5},{8,10},{9,11},{10,... | collective-permute-start | bytes 1572872 | tf_op jit(solution)/shard_map/ppermute | solution.py:372
  23.6 63.8 %copy-start.2 = (bf16[2,4,128,512]{3,2,1,0:T(8,128)(2,1)S(1)}, bf16[2,4,128,512]{3,2,1,0:T(8,128)(2,1)}, u32[]{:S(2)}) copy-start(bf16[2,4,128,512]{3,2,1,0:T(8,128)(2,1)} %initial_ref.1) | copy-start | bytes 3145732
  23.6 8.4 %collective-permute-start.4 = (bf16[16,32,256]{2,1,0:T(8,128)(2,1)S(1)}, bf16[16,32,256]{2,1,0:T(8,128)(2,1)S(1)}, u32[]{:S(2)}, u32[]{:S(2)}) collective-permute-start(bf16[16,32,256]{2,1,0:T(8,128)(2,1)S(1)} %total.4), channel_id=1, source_target_pairs={{0,18},{1,19},{2,16},{3,17},{4,22},{5,23},{6,20},{7,21},{8,26},{9,... | collective-permute-start | bytes 786440 | tf_op jit(solution)/shard_map/ppermute | solution.py:384
  27.1 9.8 %collective-permute-start.6 = (bf16[16,32,256]{2,1,0:T(8,128)(2,1)S(1)}, bf16[16,32,256]{2,1,0:T(8,128)(2,1)S(1)}, u32[]{:S(2)}, u32[]{:S(2)}) collective-permute-start(bf16[16,32,256]{2,1,0:T(8,128)(2,1)S(1)} %total.5), channel_id=1, source_target_pairs={{0,18},{1,19},{2,16},{3,17},{4,22},{5,23},{6,20},{7,21},{8,26},{9,... | collective-permute-start | bytes 786440 | tf_op jit(solution)/shard_map/ppermute | solution.py:384
  90.7 2.7 %collective-permute-start.7 = (bf16[4,512,256]{2,1,0:T(8,128)(2,1)S(1)}, bf16[4,512,256]{2,1,0:T(8,128)(2,1)S(1)}, u32[]{:S(2)}, u32[]{:S(2)}) collective-permute-start(bf16[4,512,256]{2,1,0:T(8,128)(2,1)S(1)} %get-tuple-element.34), channel_id=1, source_target_pairs={{0,1},{1,0},{2,3},{3,2},{4,5},{5,4},{6,7},{7,6},{8,9},{9,8},{10,11... | collective-permute-start | bytes 3145736 | tf_op jit(solution)/shard_map/ppermute | solution.py:372
  90.8 6.7 %collective-permute-start.8 = (bf16[4,512,256]{2,1,0:T(8,128)(2,1)S(1)}, bf16[4,512,256]{2,1,0:T(8,128)(2,1)S(1)}, u32[]{:S(2)}, u32[]{:S(2)}) collective-permute-start(bf16[4,512,256]{2,1,0:T(8,128)(2,1)S(1)} %get-tuple-element.38), channel_id=1, source_target_pairs={{0,1},{1,0},{2,3},{3,2},{4,5},{5,4},{6,7},{7,6},{8,9},{9,8},{10,11... | collective-permute-start | bytes 3145736 | tf_op jit(solution)/shard_map/ppermute | solution.py:372
  93.6 9.2 %collective-permute-start.9 = (bf16[4,256,128]{2,1,0:T(8,128)(2,1)S(1)}, bf16[4,256,128]{2,1,0:T(8,128)(2,1)S(1)}, u32[]{:S(2)}, u32[]{:S(2)}) collective-permute-start(bf16[4,256,128]{2,1,0:T(8,128)(2,1)S(1)} %get-tuple-element.36.refs_2_), channel_id=1, source_target_pairs={{0,2},{1,3},{2,0},{3,1},{4,6},{5,7},{6,4},{7,5},{8,10},{9,11},{10,... | collective-permute-start | bytes 786440 | tf_op jit(solution)/shard_map/ppermute | solution.py:372
  94.0 14.4 %collective-permute-start.12 = (bf16[4,256,128]{2,1,0:T(8,128)(2,1)S(1)}, bf16[4,256,128]{2,1,0:T(8,128)(2,1)S(1)}, u32[]{:S(2)}, u32[]{:S(2)}) collective-permute-start(bf16[4,256,128]{2,1,0:T(8,128)(2,1)S(1)} %get-tuple-element.37.refs_3_), channel_id=1, source_target_pairs={{0,2},{1,3},{2,0},{3,1},{4,6},{5,7},{6,4},{7,5},{8,10},{9,11},{10,... | collective-permute-start | bytes 786440 | tf_op jit(solution)/shard_map/ppermute | solution.py:372
  102.9 15.9 %collective-permute-start.10 = (bf16[4,512,128]{2,1,0:T(8,128)(2,1)S(1)}, bf16[4,512,128]{2,1,0:T(8,128)(2,1)S(1)}, u32[]{:S(2)}, u32[]{:S(2)}) collective-permute-start(bf16[4,512,128]{2,1,0:T(8,128)(2,1)S(1)} %add.17.refs_0_), channel_id=1, source_target_pairs={{0,2},{1,3},{2,0},{3,1},{4,6},{5,7},{6,4},{7,5},{8,10},{9,11},{10,... | collective-permute-start | bytes 1572872 | tf_op jit(solution)/shard_map/ppermute | solution.py:372
  103.8 8.0 %collective-permute-start.11 = (bf16[16,32,256]{2,1,0:T(8,128)(2,1)S(1)}, bf16[16,32,256]{2,1,0:T(8,128)(2,1)S(1)}, u32[]{:S(2)}, u32[]{:S(2)}) collective-permute-start(bf16[16,32,256]{2,1,0:T(8,128)(2,1)S(1)} %total.6), channel_id=1, source_target_pairs={{0,18},{1,19},{2,16},{3,17},{4,22},{5,23},{6,20},{7,21},{8,26},{9,... | collective-permute-start | bytes 786440 | tf_op jit(solution)/shard_map/ppermute | solution.py:384
  108.8 8.3 %collective-permute-start.13 = (bf16[16,32,256]{2,1,0:T(8,128)(2,1)S(1)}, bf16[16,32,256]{2,1,0:T(8,128)(2,1)S(1)}, u32[]{:S(2)}, u32[]{:S(2)}) collective-permute-start(bf16[16,32,256]{2,1,0:T(8,128)(2,1)S(1)} %total.7), channel_id=1, source_target_pairs={{0,18},{1,19},{2,16},{3,17},{4,22},{5,23},{6,20},{7,21},{8,26},{9,... | collective-permute-start | bytes 786440 | tf_op jit(solution)/shard_map/ppermute | solution.py:384

commit v5 on v4

--- a/solution.py
+++ b/solution.py
@@ -62,12 +62,6 @@
     return pack, to_time, to_freq
 
 
-def pair(matrix):
-    high = matrix.astype(BF)
-    low = (matrix - high.astype(np.float32)).astype(BF)
-    return np.stack([high, low])
-
-
 def spread(wide_ref, update_ref):
     for slab in range(wide_ref.shape[0]):
         wide_ref[slab] = update_ref[:, slab * LANES : (slab + 1) * LANES].astype(jnp.float32)
@@ -313,22 +307,14 @@
     rows = rows // focal
     nfreq = dft_ref.shape[1] // 2
     step = lax.broadcasted_iota(jnp.int32, (nfreq, width), 0)
-    size = dft_ref.shape[1]
-    to_time = dft_ref[0:2].reshape(2 * size, size)
-    to_freq = dft_ref[2:4].reshape(2 * size, size)
-
-    def twice(parts, values):
-        both = mm(parts, values)
-        return both[:size] + both[size:]
-
     results = []
     for j in range(focal):
         column = traces_ref[:, j * rows : (j + 1) * rows, :].reshape(2 * nfreq, width)
-        time = twice(to_time, column)
+        time = mm(dft_ref[0], column)
         keep = step < onsets_ref[j : j + 1, :]
         keep = jnp.concatenate([keep, keep], axis=0)
         time = jnp.where(keep, time, 0.0).astype(BF)
-        back = twice(to_freq, time)
+        back = mm(dft_ref[1], time)
         results.append(back.reshape(2 * devices, rows // 2, width))
     out_ref[...] = jnp.stack(results, axis=1).reshape(out_ref.shape).astype(BF)
 
@@ -392,7 +378,7 @@
     columns = rows = math.isqrt(devices // 2)
     pack, to_time, to_freq = tables(columns, rows, freq_local, focal_block)
     pack = jnp.asarray(pack, BF)
-    dft = jnp.asarray(np.concatenate([pair(to_time), pair(to_freq)]))
+    dft = jnp.asarray(np.stack([to_time, to_freq]), BF)
     half = (lax.axis_index("freq") // rows) % 2
     where = jnp.stack([lax.axis_index("src"), half]).astype(jnp.int32)
     where = jnp.concatenate([where, aperture.T.reshape(-1)])

time: 164 us -> 163 us (level)
  no operation moved by 1% of the time
where the time goes in v5:
time: 163 us
  blocking collectives  87.6 us (54%)
  waiting for transfers between devices  29 us (18%)
  Pallas kernels  27.4 us (17%)
  starting transfers between devices  16.1 us (10%)
  local copies, waits for them, and re-layouts  2.01 us (1%)
    all_to_all x2, blocking collectives, local(): update = lax.all_to_all(truncated, 'freq', 0, 0, tiled=True)  43.9 us
    all_to_all x2, blocking collectives, local(): lax.all_to_all(responses, 'freq', 0, 0, tiled=True, axis_index_groups=pla...  43.7 us
    ppermute x10, waiting for transfers between devices, swap(): lax.ppermute(values, 'src', [(i, i ^ bit) for i in range(lax.axis_size('s...  15.5 us
    ppermute x4, waiting for transfers between devices, outward(): return lax.ppermute(values, ('freq', 'src'), pairs)  13.6 us
    pallas_call x3, Pallas kernels, products(): pl.pallas_call(functools.partial(product_kernel, polarity, rels, build, l...  12.5 us
    ppermute x10, starting transfers between devices, swap(): lax.ppermute(values, 'src', [(i, i ^ bit) for i in range(lax.axis_size('s...  8.22 us
    ppermute x4, starting transfers between devices, outward(): return lax.ppermute(values, ('freq', 'src'), pairs)  7.9 us
    pallas_call x3, Pallas kernels, products_again(): pl.pallas_call(functools.partial(product_again_kernel, polarity, build, l...  6.88 us
  transfers between devices with their start and end apart: 14, of which 11 were waited for; matrix products, arithmetic and copies ran while one was open for 0% of the time, Pallas kernels for 8%

profile of v5, /device:TPU:0, one launch (start us, length us, event | category | flops | bytes accessed | tf_op | source)
XLA Modules:
  0.0 162.6 jit_solution(12759036931342526053)
XLA Ops:
  0.0 0.8 reshape.9
  0.8 1.2 copy-done.1
  2.1 5.4 %products.3 = (bf16[4,512,256]{2,1,0:T(8,128)(2,1)S(1)}, bf16[4,512,256]{2,1,0:T(8,128)(2,1)S(1)}, bf16[8,2,512,512]{3,2,1,0:T(8,128)(2,1)S(1)}, bf16[4,512,256]...) custom-call(s32[66]{0:T(128)S(1)} %pad_add_fusion.where_ref, bf16[2,4,2048,512]{3,2,1,0:T(8,128)(2,1)} %reflection_ref.5, ...), custom_call_target="tpu_custom_call" | custom-call | flops 1 | bytes 1 | tf_op jit(solution)/shard_map/products/pallas_call | solution.py:188
  7.6 0.5 collective-permute-start.1
  8.1 3.6 %products.4 = (bf16[4,512,256]{2,1,0:T(8,128)(2,1)S(1)}, bf16[4,2,512,512]{3,2,1,0:T(8,128)(2,1)S(1)}) custom-call(s32[66]{0:T(128)S(1)} %pad_add_fusion.where_ref, bf16[2,4,2048,512]{3,2,1,0:T(8,128)(2,1)} %reflection_ref.5, bf16[4,512,256]{2,1,0:T(8,128)(2,1)S(1)} %get-tuple-element.22.refs_0_, bf16[4,512,256]{2,1,0:T(8,128)(2,1)S(1)} %get-tuple-element.23.refs_1_), custom_call_target="tpu_custom_call" | custom-call | flops 1 | bytes 1 | tf_op jit(solution)/shard_map/products/pallas_call | solution.py:188
  11.7 0.1 add.14
  11.8 2.1 %collective-permute-start.2 = (bf16[4,256,128]{2,1,0:T(8,128)(2,1)S(1)}, bf16[4,256,128]{2,1,0:T(8,128)(2,1)S(1)}, u32[]{:S(2)}, u32[]{:S(2)}) collective-permute-start(bf16[4,256,128]{2,1,0:T(8,128)(2,1)S(1)} %get-tuple-element.28.refs_2_), channel_id=1, source_target_pairs={{0,2},{1,3},{2,0},{3,1},{4,6},{5,7},{6,4},{7,5},{8,10},{9,11},{10,... | collective-permute-start | bytes 786440 | tf_op jit(solution)/shard_map/ppermute | solution.py:358
  13.9 3.6 %products.5 = (bf16[4,512,256]{2,1,0:T(8,128)(2,1)S(1)}, bf16[4,2,512,512]{3,2,1,0:T(8,128)(2,1)S(1)}) custom-call(s32[66]{0:T(128)S(1)} %pad_add_fusion.where_ref, bf16[2,4,2048,512]{3,2,1,0:T(8,128)(2,1)} %reflection_ref.5, bf16[4,512,256]{2,1,0:T(8,128)(2,1)S(1)} %get-tuple-element.22.refs_0_, bf16[4,512,256]{2,1,0:T(8,128)(2,1)S(1)} %get-tuple-element.23.refs_1_, ...), custom_call_target="tpu_custom_call" | custom-call | flops 1 | bytes 1 | tf_op jit(solution)/shard_map/products/pallas_call | solution.py:188
  17.4 0.1 collective-permute-start.5
  17.6 3.3 %collective-permute-done.2.refs_0_.far_ref = bf16[4,256,128]{2,1,0:T(8,128)(2,1)S(1)} collective-permute-done((bf16[4,256,128]{2,1,0:T(8,128)(2,1)S(1)}, bf16[4,256,128]{2,1,0:T(8,128)(2,1)S(1)}, u32[]{:S(2)}, u32[]{:S(2)}) %collective-permute-start.2) | collective-permute-done | bytes 262176 | tf_op jit(solution)/shard_map/ppermute | solution.py:358
  20.9 0.1 add.15.refs_0_
  21.0 2.3 %collective-permute-start.3 = (bf16[4,512,128]{2,1,0:T(8,128)(2,1)S(1)}, bf16[4,512,128]{2,1,0:T(8,128)(2,1)S(1)}, u32[]{:S(2)}, u32[]{:S(2)}) collective-permute-start(bf16[4,512,128]{2,1,0:T(8,128)(2,1)S(1)} %add.15.refs_0_), channel_id=1, source_target_pairs={{0,2},{1,3},{2,0},{3,1},{4,6},{5,7},{6,4},{7,5},{8,10},{9,11},{10,... | collective-permute-start | bytes 1572872 | tf_op jit(solution)/shard_map/ppermute | solution.py:358
  23.2 0.4 total.4
  23.6 2.3 %collective-permute-start.4 = (bf16[16,32,256]{2,1,0:T(8,128)(2,1)S(1)}, bf16[16,32,256]{2,1,0:T(8,128)(2,1)S(1)}, u32[]{:S(2)}, u32[]{:S(2)}) collective-permute-start(bf16[16,32,256]{2,1,0:T(8,128)(2,1)S(1)} %total.4), channel_id=1, source_target_pairs={{0,18},{1,19},{2,16},{3,17},{4,22},{5,23},{6,20},{7,21},{8,26},{9,... | collective-permute-start | bytes 786440 | tf_op jit(solution)/shard_map/ppermute | solution.py:370
  25.9 0.8 collective-permute-done.5.far_ref
  26.7 0.4 total.5
  27.1 4.1 %collective-permute-start.6 = (bf16[16,32,256]{2,1,0:T(8,128)(2,1)S(1)}, bf16[16,32,256]{2,1,0:T(8,128)(2,1)S(1)}, u32[]{:S(2)}, u32[]{:S(2)}) collective-permute-start(bf16[16,32,256]{2,1,0:T(8,128)(2,1)S(1)} %total.5), channel_id=1, source_target_pairs={{0,18},{1,19},{2,16},{3,17},{4,22},{5,23},{6,20},{7,21},{8,26},{9,... | collective-permute-start | bytes 786440 | tf_op jit(solution)/shard_map/ppermute | solution.py:370
  31.2 0.8 collective-permute-done.4.refs_0_
  32.1 4.8 %collective-permute-done.6.refs_1_ = bf16[16,32,256]{2,1,0:T(8,128)(2,1)S(1)} collective-permute-done((bf16[16,32,256]{2,1,0:T(8,128)(2,1)S(1)}, bf16[16,32,256]{2,1,0:T(8,128)(2,1)S(1)}, u32[]{:S(2)}, u32[]{:S(2)}) %collective-permute-start.6) | collective-permute-done | bytes 262176 | tf_op jit(solution)/shard_map/ppermute | solution.py:370
  36.9 0.4 collective-permute-done.3.far_ref
  37.3 1.0 pack_own.2
  38.3 23.5 %all_to_all.20.traces_ref = bf16[16,64,512]{2,1,0:T(8,128)(2,1)S(1)} all-to-all(bf16[16,64,512]{2,1,0:T(8,128)(2,1)S(1)} %pack_own.2), channel_id=1, replica_groups={{0,4,8,12,32,36,40,44,64,68,72,76,96,100,104,108},{16,20,24,28,48,52,56..., dimensions={0} | all-to-all | bytes 2097152 | tf_op jit(solution)/shard_map/all_to_all | solution.py:425
  61.9 1.2 window.2
  63.1 23.7 %all_to_all.21 = bf16[32,32,512]{2,1,0:T(8,128)(2,1)S(1)} all-to-all(bf16[32,32,512]{2,1,0:T(8,128)(2,1)S(1)} %window.2), channel_id=1, replica_groups=mesh['freq'=32,'src'=4] {'freq'}, dimensions={0} | all-to-all | bytes 2097152 | tf_op jit(solution)/shard_map/all_to_all | solution.py:429
  86.8 3.3 %products_again.3 = (bf16[4,512,256]{2,1,0:T(8,128)(2,1)S(1)}, bf16[4,512,256]{2,1,0:T(8,128)(2,1)S(1)}, bf16[4,512,256]{2,1,0:T(8,128)(2,1)S(1)}, bf16[4,512,256]{2,1,0:T(8,128)(2,1)S(1)}) custom-call(s32[66]{0:T(128)S(1)} %pad_add_fusion.where_ref, bf16[8,2,512,512]{3,2,1,0:T(8,128)(2,1)S(1)} %get-tuple-element.25.held_ref, ...), custom_call_target="tpu_custom_call" | custom-call | flops 1 | bytes 1 | tf_op jit(solution)/shard_map/products_again/pallas_call | solution.py:225
  90.2 0.5 collective-permute-start.8
  90.7 1.8 %products_again.4.mine_ref = bf16[4,512,256]{2,1,0:T(8,128)(2,1)S(1)} custom-call(s32[66]{0:T(128)S(1)} %pad_add_fusion.where_ref, bf16[4,2,512,512]{3,2,1,0:T(8,128)(2,1)S(1)} %get-tuple-element.24.held_ref, bf16[4,512,256]{2,1,0:T(8,128)(2,1)S(1)} %get-tuple-element.32.refs_0_, bf16[4,512,256]{2,1,0:T(8,128)(2,1)S(1)} %get-tuple-element.33.refs_1_), custom_call_target="tpu_custom_call" | custom-call | flops 1 | bytes 1 | tf_op jit(solution)/shard_map/products_again/pallas_call | solution.py:225
  92.5 0.4 collective-permute-done.7.core_ref
  92.9 0.1 add.16
  93.0 0.5 collective-permute-start.9
  93.5 1.6 collective-permute-start.12
  95.1 1.8 %products_again.5.mine_ref = bf16[4,512,256]{2,1,0:T(8,128)(2,1)S(1)} custom-call(s32[66]{0:T(128)S(1)} %pad_add_fusion.where_ref, bf16[4,2,512,512]{3,2,1,0:T(8,128)(2,1)S(1)} %get-tuple-element.35.held_ref, bf16[4,512,256]{2,1,0:T(8,128)(2,1)S(1)} %get-tuple-element.32.refs_0_, bf16[4,512,256]{2,1,0:T(8,128)(2,1)S(1)} %get-tuple-element.33.refs_1_, ...), custom_call_target="tpu_custom_call" | custom-call | flops 1 | bytes 1 | tf_op jit(solution)/shard_map/products_again/pallas_call | solution.py:225
  96.9 5.3 %collective-permute-done.9.refs_0_.far_ref = bf16[4,256,128]{2,1,0:T(8,128)(2,1)S(1)} collective-permute-done((bf16[4,256,128]{2,1,0:T(8,128)(2,1)S(1)}, bf16[4,256,128]{2,1,0:T(8,128)(2,1)S(1)}, u32[]{:S(2)}, u32[]{:S(2)}) %collective-permute-start.9) | collective-permute-done | bytes 262176 | tf_op jit(solution)/shard_map/ppermute | solution.py:358
  102.2 0.1 add.17.refs_0_
  102.4 0.5 collective-permute-start.10
  102.8 0.4 total.6
  103.2 1.1 collective-permute-start.11
  104.3 3.6 %collective-permute-done.12.far_ref = bf16[4,256,128]{2,1,0:T(8,128)(2,1)S(1)} collective-permute-done((bf16[4,256,128]{2,1,0:T(8,128)(2,1)S(1)}, bf16[4,256,128]{2,1,0:T(8,128)(2,1)S(1)}, u32[]{:S(2)}, u32[]{:S(2)}) %collective-permute-start.12) | collective-permute-done | bytes 262176 | tf_op jit(solution)/shard_map/ppermute | solution.py:358
  107.9 0.4 total.7
  108.2 0.4 collective-permute-start.13
  108.7 2.5 %collective-permute-done.11.refs_0_ = bf16[16,32,256]{2,1,0:T(8,128)(2,1)S(1)} collective-permute-done((bf16[16,32,256]{2,1,0:T(8,128)(2,1)S(1)}, bf16[16,32,256]{2,1,0:T(8,128)(2,1)S(1)}, u32[]{:S(2)}, u32[]{:S(2)}) %collective-permute-start.11) | collective-permute-done | bytes 262176 | tf_op jit(solution)/shard_map/ppermute | solution.py:370
  111.2 5.4 %collective-permute-done.13.refs_1_ = bf16[16,32,256]{2,1,0:T(8,128)(2,1)S(1)} collective-permute-done((bf16[16,32,256]{2,1,0:T(8,128)(2,1)S(1)}, bf16[16,32,256]{2,1,0:T(8,128)(2,1)S(1)}, u32[]{:S(2)}, u32[]{:S(2)}) %collective-permute-start.13) | collective-permute-done | bytes 262176 | tf_op jit(solution)/shard_map/ppermute | solution.py:370
  116.6 1.7 %collective-permute-done.10.far_ref = bf16[4,512,128]{2,1,0:T(8,128)(2,1)S(1)} collective-permute-done((bf16[4,512,128]{2,1,0:T(8,128)(2,1)S(1)}, bf16[4,512,128]{2,1,0:T(8,128)(2,1)S(1)}, u32[]{:S(2)}, u32[]{:S(2)}) %collective-permute-start.10) | collective-permute-done | bytes 524320 | tf_op jit(solution)/shard_map/ppermute | solution.py:358
  118.3 1.0 pack_own.3
  119.3 20.1 %all_to_all.22.traces_ref = bf16[16,64,512]{2,1,0:T(8,128)(2,1)S(1)} all-to-all(bf16[16,64,512]{2,1,0:T(8,128)(2,1)S(1)} %pack_own.3), channel_id=1, replica_groups={{0,4,8,12,32,36,40,44,64,68,72,76,96,100,104,108},{16,20,24,28,48,52,56..., dimensions={0} | all-to-all | bytes 2097152 | tf_op jit(solution)/shard_map/all_to_all | solution.py:425
  139.5 1.2 window.3
  140.7 20.2 %all_to_all.23 = bf16[32,32,512]{2,1,0:T(8,128)(2,1)S(1)} all-to-all(bf16[32,32,512]{2,1,0:T(8,128)(2,1)S(1)} %window.3), channel_id=1, replica_groups=mesh['freq'=32,'src'=4] {'freq'}, dimensions={0} | all-to-all | bytes 2097152 | tf_op jit(solution)/shard_map/all_to_all | solution.py:429
  160.9 1.5 finish.1
  (15 shorter events, 0.3 us)
Async XLA Ops:
  0.8 1.2 copy-start.1
  7.5 4.2 %collective-permute-start = (bf16[4,512,256]{2,1,0:T(8,128)(2,1)S(1)}, bf16[4,512,256]{2,1,0:T(8,128)(2,1)S(1)}, u32[]{:S(2)}, u32[]{:S(2)}) collective-permute-start(bf16[4,512,256]{2,1,0:T(8,128)(2,1)S(1)} %get-tuple-element.27), channel_id=1, source_target_pairs={{0,1},{1,0},{2,3},{3,2},{4,5},{5,4},{6,7},{7,6},{8,9},{9,8},{10,11... | collective-permute-start | bytes 3145736 | tf_op jit(solution)/shard_map/ppermute | solution.py:358
  7.6 10.0 %collective-permute-start.1 = (bf16[4,512,256]{2,1,0:T(8,128)(2,1)S(1)}, bf16[4,512,256]{2,1,0:T(8,128)(2,1)S(1)}, u32[]{:S(2)}, u32[]{:S(2)}) collective-permute-start(bf16[4,512,256]{2,1,0:T(8,128)(2,1)S(1)} %get-tuple-element.31), channel_id=1, source_target_pairs={{0,1},{1,0},{2,3},{3,2},{4,5},{5,4},{6,7},{7,6},{8,9},{9,8},{10,11... | collective-permute-start | bytes 3145736 | tf_op jit(solution)/shard_map/ppermute | solution.py:358
  11.8 9.1 %collective-permute-start.2 = (bf16[4,256,128]{2,1,0:T(8,128)(2,1)S(1)}, bf16[4,256,128]{2,1,0:T(8,128)(2,1)S(1)}, u32[]{:S(2)}, u32[]{:S(2)}) collective-permute-start(bf16[4,256,128]{2,1,0:T(8,128)(2,1)S(1)} %get-tuple-element.28.refs_2_), channel_id=1, source_target_pairs={{0,2},{1,3},{2,0},{3,1},{4,6},{5,7},{6,4},{7,5},{8,10},{9,11},{10,... | collective-permute-start | bytes 786440 | tf_op jit(solution)/shard_map/ppermute | solution.py:358
  13.9 9.4 %copy-start = (bf16[512,512]{1,0:T(8,128)(2,1)S(1)}, bf16[512,512]{1,0:T(8,128)(2,1)}, u32[]{:S(2)}) copy-start(bf16[512,512]{1,0:T(8,128)(2,1)} %constant.39.clone.pack_ref) | copy-start | bytes 1572868
  17.4 9.3 %collective-permute-start.5 = (bf16[4,256,128]{2,1,0:T(8,128)(2,1)S(1)}, bf16[4,256,128]{2,1,0:T(8,128)(2,1)S(1)}, u32[]{:S(2)}, u32[]{:S(2)}) collective-permute-start(bf16[4,256,128]{2,1,0:T(8,128)(2,1)S(1)} %get-tuple-element.29.refs_3_), channel_id=1, source_target_pairs={{0,2},{1,3},{2,0},{3,1},{4,6},{5,7},{6,4},{7,5},{8,10},{9,11},{10,... | collective-permute-start | bytes 786440 | tf_op jit(solution)/shard_map/ppermute | solution.py:358
  20.8 41.0 %copy-start.3 = (bf16[2,256,256]{2,1,0:T(8,128)(2,1)S(1)}, bf16[2,256,256]{2,1,0:T(8,128)(2,1)}, u32[]{:S(2)}) copy-start(bf16[2,256,256]{2,1,0:T(8,128)(2,1)} %constant.40.clone.dft_ref) | copy-start | bytes 786436
  20.9 41.0 %copy-start.4 = (s32[4,512]{1,0:T(4,128)S(1)}, s32[4,512]{1,0:T(4,128)}, u32[]{:S(2)}) copy-start(s32[4,512]{1,0:T(4,128)} %onsets_ref.3) | copy-start | bytes 24580
  21.0 16.3 %collective-permute-start.3 = (bf16[4,512,128]{2,1,0:T(8,128)(2,1)S(1)}, bf16[4,512,128]{2,1,0:T(8,128)(2,1)S(1)}, u32[]{:S(2)}, u32[]{:S(2)}) collective-permute-start(bf16[4,512,128]{2,1,0:T(8,128)(2,1)S(1)} %add.15.refs_0_), channel_id=1, source_target_pairs={{0,2},{1,3},{2,0},{3,1},{4,6},{5,7},{6,4},{7,5},{8,10},{9,11},{10,... | collective-permute-start | bytes 1572872 | tf_op jit(solution)/shard_map/ppermute | solution.py:358
  23.6 63.2 %copy-start.2 = (bf16[2,4,128,512]{3,2,1,0:T(8,128)(2,1)S(1)}, bf16[2,4,128,512]{3,2,1,0:T(8,128)(2,1)}, u32[]{:S(2)}) copy-start(bf16[2,4,128,512]{3,2,1,0:T(8,128)(2,1)} %initial_ref.1) | copy-start | bytes 3145732
  23.6 8.4 %collective-permute-start.4 = (bf16[16,32,256]{2,1,0:T(8,128)(2,1)S(1)}, bf16[16,32,256]{2,1,0:T(8,128)(2,1)S(1)}, u32[]{:S(2)}, u32[]{:S(2)}) collective-permute-start(bf16[16,32,256]{2,1,0:T(8,128)(2,1)S(1)} %total.4), channel_id=1, source_target_pairs={{0,18},{1,19},{2,16},{3,17},{4,22},{5,23},{6,20},{7,21},{8,26},{9,... | collective-permute-start | bytes 786440 | tf_op jit(solution)/shard_map/ppermute | solution.py:370
  27.1 9.8 %collective-permute-start.6 = (bf16[16,32,256]{2,1,0:T(8,128)(2,1)S(1)}, bf16[16,32,256]{2,1,0:T(8,128)(2,1)S(1)}, u32[]{:S(2)}, u32[]{:S(2)}) collective-permute-start(bf16[16,32,256]{2,1,0:T(8,128)(2,1)S(1)} %total.5), channel_id=1, source_target_pairs={{0,18},{1,19},{2,16},{3,17},{4,22},{5,23},{6,20},{7,21},{8,26},{9,... | collective-permute-start | bytes 786440 | tf_op jit(solution)/shard_map/ppermute | solution.py:370
  90.1 2.7 %collective-permute-start.7 = (bf16[4,512,256]{2,1,0:T(8,128)(2,1)S(1)}, bf16[4,512,256]{2,1,0:T(8,128)(2,1)S(1)}, u32[]{:S(2)}, u32[]{:S(2)}) collective-permute-start(bf16[4,512,256]{2,1,0:T(8,128)(2,1)S(1)} %get-tuple-element.34), channel_id=1, source_target_pairs={{0,1},{1,0},{2,3},{3,2},{4,5},{5,4},{6,7},{7,6},{8,9},{9,8},{10,11... | collective-permute-start | bytes 3145736 | tf_op jit(solution)/shard_map/ppermute | solution.py:358
  90.2 6.7 %collective-permute-start.8 = (bf16[4,512,256]{2,1,0:T(8,128)(2,1)S(1)}, bf16[4,512,256]{2,1,0:T(8,128)(2,1)S(1)}, u32[]{:S(2)}, u32[]{:S(2)}) collective-permute-start(bf16[4,512,256]{2,1,0:T(8,128)(2,1)S(1)} %get-tuple-element.38), channel_id=1, source_target_pairs={{0,1},{1,0},{2,3},{3,2},{4,5},{5,4},{6,7},{7,6},{8,9},{9,8},{10,11... | collective-permute-start | bytes 3145736 | tf_op jit(solution)/shard_map/ppermute | solution.py:358
  93.0 9.2 %collective-permute-start.9 = (bf16[4,256,128]{2,1,0:T(8,128)(2,1)S(1)}, bf16[4,256,128]{2,1,0:T(8,128)(2,1)S(1)}, u32[]{:S(2)}, u32[]{:S(2)}) collective-permute-start(bf16[4,256,128]{2,1,0:T(8,128)(2,1)S(1)} %get-tuple-element.36.refs_2_), channel_id=1, source_target_pairs={{0,2},{1,3},{2,0},{3,1},{4,6},{5,7},{6,4},{7,5},{8,10},{9,11},{10,... | collective-permute-start | bytes 786440 | tf_op jit(solution)/shard_map/ppermute | solution.py:358
  93.5 14.4 %collective-permute-start.12 = (bf16[4,256,128]{2,1,0:T(8,128)(2,1)S(1)}, bf16[4,256,128]{2,1,0:T(8,128)(2,1)S(1)}, u32[]{:S(2)}, u32[]{:S(2)}) collective-permute-start(bf16[4,256,128]{2,1,0:T(8,128)(2,1)S(1)} %get-tuple-element.37.refs_3_), channel_id=1, source_target_pairs={{0,2},{1,3},{2,0},{3,1},{4,6},{5,7},{6,4},{7,5},{8,10},{9,11},{10,... | collective-permute-start | bytes 786440 | tf_op jit(solution)/shard_map/ppermute | solution.py:358
  102.4 15.9 %collective-permute-start.10 = (bf16[4,512,128]{2,1,0:T(8,128)(2,1)S(1)}, bf16[4,512,128]{2,1,0:T(8,128)(2,1)S(1)}, u32[]{:S(2)}, u32[]{:S(2)}) collective-permute-start(bf16[4,512,128]{2,1,0:T(8,128)(2,1)S(1)} %add.17.refs_0_), channel_id=1, source_target_pairs={{0,2},{1,3},{2,0},{3,1},{4,6},{5,7},{6,4},{7,5},{8,10},{9,11},{10,... | collective-permute-start | bytes 1572872 | tf_op jit(solution)/shard_map/ppermute | solution.py:358
  103.2 8.0 %collective-permute-start.11 = (bf16[16,32,256]{2,1,0:T(8,128)(2,1)S(1)}, bf16[16,32,256]{2,1,0:T(8,128)(2,1)S(1)}, u32[]{:S(2)}, u32[]{:S(2)}) collective-permute-start(bf16[16,32,256]{2,1,0:T(8,128)(2,1)S(1)} %total.6), channel_id=1, source_target_pairs={{0,18},{1,19},{2,16},{3,17},{4,22},{5,23},{6,20},{7,21},{8,26},{9,... | collective-permute-start | bytes 786440 | tf_op jit(solution)/shard_map/ppermute | solution.py:370
  108.2 8.3 %collective-permute-start.13 = (bf16[16,32,256]{2,1,0:T(8,128)(2,1)S(1)}, bf16[16,32,256]{2,1,0:T(8,128)(2,1)S(1)}, u32[]{:S(2)}, u32[]{:S(2)}) collective-permute-start(bf16[16,32,256]{2,1,0:T(8,128)(2,1)S(1)} %total.7), channel_id=1, source_target_pairs={{0,18},{1,19},{2,16},{3,17},{4,22},{5,23},{6,20},{7,21},{8,26},{9,... | collective-permute-start | bytes 786440 | tf_op jit(solution)/shard_map/ppermute | solution.py:370

commit v6 on v5

--- a/solution.py
+++ b/solution.py
@@ -10,7 +10,7 @@
 from jax.sharding import PartitionSpec as P
 
 ITERS = 2
-AHEAD = 4
+AHEAD = 6
 TOGETHER = 2
 CUTS = 2
 TILE = 16

time: 163 us -> 163 us (level)
  no operation moved by 1% of the time
where the time goes in v6:
time: 163 us; the launch traced here: 162 us
  blocking collectives  87.6 us (54%)
  waiting for transfers between devices  29 us (18%)
  Pallas kernels  27.2 us (17%)
  starting transfers between devices  16.1 us (10%)
  local copies, waits for them, and re-layouts  2.01 us (1%)
    all_to_all x2, blocking collectives, local(): update = lax.all_to_all(truncated, 'freq', 0, 0, tiled=True)  44 us
    all_to_all x2, blocking collectives, local(): lax.all_to_all(responses, 'freq', 0, 0, tiled=True, axis_index_groups=pla...  43.7 us
    ppermute x10, waiting for transfers between devices, swap(): lax.ppermute(values, 'src', [(i, i ^ bit) for i in range(lax.axis_size('s...  15.5 us
    ppermute x4, waiting for transfers between devices, outward(): return lax.ppermute(values, ('freq', 'src'), pairs)  13.6 us
    pallas_call x3, Pallas kernels, products(): pl.pallas_call(functools.partial(product_kernel, polarity, rels, build, l...  12.3 us
    ppermute x10, starting transfers between devices, swap(): lax.ppermute(values, 'src', [(i, i ^ bit) for i in range(lax.axis_size('s...  8.19 us
    ppermute x4, starting transfers between devices, outward(): return lax.ppermute(values, ('freq', 'src'), pairs)  7.91 us
    pallas_call x3, Pallas kernels, products_again(): pl.pallas_call(functools.partial(product_again_kernel, polarity, build, l...  6.88 us
  transfers between devices with their start and end apart: 14, of which 11 were waited for; matrix products, arithmetic and copies ran while one was open for 0% of the time, Pallas kernels for 8%

profile of v6, /device:TPU:0, one launch (start us, length us, event | category | flops | bytes accessed | tf_op | source)
XLA Modules:
  0.0 162.4 jit_solution(2892253305880951681)
XLA Ops:
  0.0 0.8 reshape.9
  0.8 1.2 copy-done.1
  2.1 5.2 %products.3 = (bf16[4,512,256]{2,1,0:T(8,128)(2,1)S(1)}, bf16[4,512,256]{2,1,0:T(8,128)(2,1)S(1)}, bf16[8,2,512,512]{3,2,1,0:T(8,128)(2,1)S(1)}, bf16[4,512,256]...) custom-call(s32[66]{0:T(128)S(1)} %pad_add_fusion.where_ref, bf16[2,4,2048,512]{3,2,1,0:T(8,128)(2,1)} %reflection_ref.5, ...), custom_call_target="tpu_custom_call" | custom-call | flops 1 | bytes 1 | tf_op jit(solution)/shard_map/products/pallas_call | solution.py:188
  7.4 0.5 collective-permute-start.1
  7.8 3.6 %products.4 = (bf16[4,512,256]{2,1,0:T(8,128)(2,1)S(1)}, bf16[4,2,512,512]{3,2,1,0:T(8,128)(2,1)S(1)}) custom-call(s32[66]{0:T(128)S(1)} %pad_add_fusion.where_ref, bf16[2,4,2048,512]{3,2,1,0:T(8,128)(2,1)} %reflection_ref.5, bf16[4,512,256]{2,1,0:T(8,128)(2,1)S(1)} %get-tuple-element.22.refs_0_, bf16[4,512,256]{2,1,0:T(8,128)(2,1)S(1)} %get-tuple-element.23.refs_1_), custom_call_target="tpu_custom_call" | custom-call | flops 1 | bytes 1 | tf_op jit(solution)/shard_map/products/pallas_call | solution.py:188
  11.4 0.1 add.14
  11.6 2.1 %collective-permute-start.2 = (bf16[4,256,128]{2,1,0:T(8,128)(2,1)S(1)}, bf16[4,256,128]{2,1,0:T(8,128)(2,1)S(1)}, u32[]{:S(2)}, u32[]{:S(2)}) collective-permute-start(bf16[4,256,128]{2,1,0:T(8,128)(2,1)S(1)} %get-tuple-element.28.refs_2_), channel_id=1, source_target_pairs={{0,2},{1,3},{2,0},{3,1},{4,6},{5,7},{6,4},{7,5},{8,10},{9,11},{10,... | collective-permute-start | bytes 786440 | tf_op jit(solution)/shard_map/ppermute | solution.py:358
  13.6 3.6 %products.5 = (bf16[4,512,256]{2,1,0:T(8,128)(2,1)S(1)}, bf16[4,2,512,512]{3,2,1,0:T(8,128)(2,1)S(1)}) custom-call(s32[66]{0:T(128)S(1)} %pad_add_fusion.where_ref, bf16[2,4,2048,512]{3,2,1,0:T(8,128)(2,1)} %reflection_ref.5, bf16[4,512,256]{2,1,0:T(8,128)(2,1)S(1)} %get-tuple-element.22.refs_0_, bf16[4,512,256]{2,1,0:T(8,128)(2,1)S(1)} %get-tuple-element.23.refs_1_, ...), custom_call_target="tpu_custom_call" | custom-call | flops 1 | bytes 1 | tf_op jit(solution)/shard_map/products/pallas_call | solution.py:188
  17.2 0.1 collective-permute-start.5
  17.3 3.3 %collective-permute-done.2.refs_0_.far_ref = bf16[4,256,128]{2,1,0:T(8,128)(2,1)S(1)} collective-permute-done((bf16[4,256,128]{2,1,0:T(8,128)(2,1)S(1)}, bf16[4,256,128]{2,1,0:T(8,128)(2,1)S(1)}, u32[]{:S(2)}, u32[]{:S(2)}) %collective-permute-start.2) | collective-permute-done | bytes 262176 | tf_op jit(solution)/shard_map/ppermute | solution.py:358
  20.6 0.1 add.15.refs_0_
  20.7 2.3 %collective-permute-start.3 = (bf16[4,512,128]{2,1,0:T(8,128)(2,1)S(1)}, bf16[4,512,128]{2,1,0:T(8,128)(2,1)S(1)}, u32[]{:S(2)}, u32[]{:S(2)}) collective-permute-start(bf16[4,512,128]{2,1,0:T(8,128)(2,1)S(1)} %add.15.refs_0_), channel_id=1, source_target_pairs={{0,2},{1,3},{2,0},{3,1},{4,6},{5,7},{6,4},{7,5},{8,10},{9,11},{10,... | collective-permute-start | bytes 1572872 | tf_op jit(solution)/shard_map/ppermute | solution.py:358
  23.0 0.4 total.4
  23.4 2.3 %collective-permute-start.4 = (bf16[16,32,256]{2,1,0:T(8,128)(2,1)S(1)}, bf16[16,32,256]{2,1,0:T(8,128)(2,1)S(1)}, u32[]{:S(2)}, u32[]{:S(2)}) collective-permute-start(bf16[16,32,256]{2,1,0:T(8,128)(2,1)S(1)} %total.4), channel_id=1, source_target_pairs={{0,18},{1,19},{2,16},{3,17},{4,22},{5,23},{6,20},{7,21},{8,26},{9,... | collective-permute-start | bytes 786440 | tf_op jit(solution)/shard_map/ppermute | solution.py:370
  25.7 0.8 collective-permute-done.5.far_ref
  26.5 0.4 total.5
  26.9 4.1 %collective-permute-start.6 = (bf16[16,32,256]{2,1,0:T(8,128)(2,1)S(1)}, bf16[16,32,256]{2,1,0:T(8,128)(2,1)S(1)}, u32[]{:S(2)}, u32[]{:S(2)}) collective-permute-start(bf16[16,32,256]{2,1,0:T(8,128)(2,1)S(1)} %total.5), channel_id=1, source_target_pairs={{0,18},{1,19},{2,16},{3,17},{4,22},{5,23},{6,20},{7,21},{8,26},{9,... | collective-permute-start | bytes 786440 | tf_op jit(solution)/shard_map/ppermute | solution.py:370
  31.0 0.8 collective-permute-done.4.refs_0_
  31.8 4.8 %collective-permute-done.6.refs_1_ = bf16[16,32,256]{2,1,0:T(8,128)(2,1)S(1)} collective-permute-done((bf16[16,32,256]{2,1,0:T(8,128)(2,1)S(1)}, bf16[16,32,256]{2,1,0:T(8,128)(2,1)S(1)}, u32[]{:S(2)}, u32[]{:S(2)}) %collective-permute-start.6) | collective-permute-done | bytes 262176 | tf_op jit(solution)/shard_map/ppermute | solution.py:370
  36.7 0.4 collective-permute-done.3.far_ref
  37.1 1.0 pack_own.2
  38.1 23.5 %all_to_all.20.traces_ref = bf16[16,64,512]{2,1,0:T(8,128)(2,1)S(1)} all-to-all(bf16[16,64,512]{2,1,0:T(8,128)(2,1)S(1)} %pack_own.2), channel_id=1, replica_groups={{0,4,8,12,32,36,40,44,64,68,72,76,96,100,104,108},{16,20,24,28,48,52,56..., dimensions={0} | all-to-all | bytes 2097152 | tf_op jit(solution)/shard_map/all_to_all | solution.py:425
  61.6 1.2 window.2
  62.8 23.8 %all_to_all.21 = bf16[32,32,512]{2,1,0:T(8,128)(2,1)S(1)} all-to-all(bf16[32,32,512]{2,1,0:T(8,128)(2,1)S(1)} %window.2), channel_id=1, replica_groups=mesh['freq'=32,'src'=4] {'freq'}, dimensions={0} | all-to-all | bytes 2097152 | tf_op jit(solution)/shard_map/all_to_all | solution.py:429
  86.6 3.3 %products_again.3 = (bf16[4,512,256]{2,1,0:T(8,128)(2,1)S(1)}, bf16[4,512,256]{2,1,0:T(8,128)(2,1)S(1)}, bf16[4,512,256]{2,1,0:T(8,128)(2,1)S(1)}, bf16[4,512,256]{2,1,0:T(8,128)(2,1)S(1)}) custom-call(s32[66]{0:T(128)S(1)} %pad_add_fusion.where_ref, bf16[8,2,512,512]{3,2,1,0:T(8,128)(2,1)S(1)} %get-tuple-element.25.held_ref, ...), custom_call_target="tpu_custom_call" | custom-call | flops 1 | bytes 1 | tf_op jit(solution)/shard_map/products_again/pallas_call | solution.py:225
  90.0 0.5 collective-permute-start.8
  90.5 1.8 %products_again.4.mine_ref = bf16[4,512,256]{2,1,0:T(8,128)(2,1)S(1)} custom-call(s32[66]{0:T(128)S(1)} %pad_add_fusion.where_ref, bf16[4,2,512,512]{3,2,1,0:T(8,128)(2,1)S(1)} %get-tuple-element.24.held_ref, bf16[4,512,256]{2,1,0:T(8,128)(2,1)S(1)} %get-tuple-element.32.refs_0_, bf16[4,512,256]{2,1,0:T(8,128)(2,1)S(1)} %get-tuple-element.33.refs_1_), custom_call_target="tpu_custom_call" | custom-call | flops 1 | bytes 1 | tf_op jit(solution)/shard_map/products_again/pallas_call | solution.py:225
  92.3 0.4 collective-permute-done.7.core_ref
  92.7 0.1 add.16
  92.8 0.5 collective-permute-start.9
  93.3 1.6 %collective-permute-start.12 = (bf16[4,256,128]{2,1,0:T(8,128)(2,1)S(1)}, bf16[4,256,128]{2,1,0:T(8,128)(2,1)S(1)}, u32[]{:S(2)}, u32[]{:S(2)}) collective-permute-start(bf16[4,256,128]{2,1,0:T(8,128)(2,1)S(1)} %get-tuple-element.37.refs_3_), channel_id=1, source_target_pairs={{0,2},{1,3},{2,0},{3,1},{4,6},{5,7},{6,4},{7,5},{8,10},{9,11},{10,... | collective-permute-start | bytes 786440 | tf_op jit(solution)/shard_map/ppermute | solution.py:358
  94.9 1.8 %products_again.5.mine_ref = bf16[4,512,256]{2,1,0:T(8,128)(2,1)S(1)} custom-call(s32[66]{0:T(128)S(1)} %pad_add_fusion.where_ref, bf16[4,2,512,512]{3,2,1,0:T(8,128)(2,1)S(1)} %get-tuple-element.35.held_ref, bf16[4,512,256]{2,1,0:T(8,128)(2,1)S(1)} %get-tuple-element.32.refs_0_, bf16[4,512,256]{2,1,0:T(8,128)(2,1)S(1)} %get-tuple-element.33.refs_1_, ...), custom_call_target="tpu_custom_call" | custom-call | flops 1 | bytes 1 | tf_op jit(solution)/shard_map/products_again/pallas_call | solution.py:225
  96.7 5.3 %collective-permute-done.9.refs_0_.far_ref = bf16[4,256,128]{2,1,0:T(8,128)(2,1)S(1)} collective-permute-done((bf16[4,256,128]{2,1,0:T(8,128)(2,1)S(1)}, bf16[4,256,128]{2,1,0:T(8,128)(2,1)S(1)}, u32[]{:S(2)}, u32[]{:S(2)}) %collective-permute-start.9) | collective-permute-done | bytes 262176 | tf_op jit(solution)/shard_map/ppermute | solution.py:358
  102.0 0.1 add.17.refs_0_
  102.2 0.5 collective-permute-start.10
  102.6 0.4 total.6
  103.0 1.1 collective-permute-start.11
  104.1 3.6 %collective-permute-done.12.far_ref = bf16[4,256,128]{2,1,0:T(8,128)(2,1)S(1)} collective-permute-done((bf16[4,256,128]{2,1,0:T(8,128)(2,1)S(1)}, bf16[4,256,128]{2,1,0:T(8,128)(2,1)S(1)}, u32[]{:S(2)}, u32[]{:S(2)}) %collective-permute-start.12) | collective-permute-done | bytes 262176 | tf_op jit(solution)/shard_map/ppermute | solution.py:358
  107.6 0.4 total.7
  108.0 0.4 collective-permute-start.13
  108.5 2.5 %collective-permute-done.11.refs_0_ = bf16[16,32,256]{2,1,0:T(8,128)(2,1)S(1)} collective-permute-done((bf16[16,32,256]{2,1,0:T(8,128)(2,1)S(1)}, bf16[16,32,256]{2,1,0:T(8,128)(2,1)S(1)}, u32[]{:S(2)}, u32[]{:S(2)}) %collective-permute-start.11) | collective-permute-done | bytes 262176 | tf_op jit(solution)/shard_map/ppermute | solution.py:370
  111.0 5.4 %collective-permute-done.13.refs_1_ = bf16[16,32,256]{2,1,0:T(8,128)(2,1)S(1)} collective-permute-done((bf16[16,32,256]{2,1,0:T(8,128)(2,1)S(1)}, bf16[16,32,256]{2,1,0:T(8,128)(2,1)S(1)}, u32[]{:S(2)}, u32[]{:S(2)}) %collective-permute-start.13) | collective-permute-done | bytes 262176 | tf_op jit(solution)/shard_map/ppermute | solution.py:370
  116.3 1.7 %collective-permute-done.10.far_ref = bf16[4,512,128]{2,1,0:T(8,128)(2,1)S(1)} collective-permute-done((bf16[4,512,128]{2,1,0:T(8,128)(2,1)S(1)}, bf16[4,512,128]{2,1,0:T(8,128)(2,1)S(1)}, u32[]{:S(2)}, u32[]{:S(2)}) %collective-permute-start.10) | collective-permute-done | bytes 524320 | tf_op jit(solution)/shard_map/ppermute | solution.py:358
  118.1 1.0 pack_own.3
  119.1 20.1 %all_to_all.22.traces_ref = bf16[16,64,512]{2,1,0:T(8,128)(2,1)S(1)} all-to-all(bf16[16,64,512]{2,1,0:T(8,128)(2,1)S(1)} %pack_own.3), channel_id=1, replica_groups={{0,4,8,12,32,36,40,44,64,68,72,76,96,100,104,108},{16,20,24,28,48,52,56..., dimensions={0} | all-to-all | bytes 2097152 | tf_op jit(solution)/shard_map/all_to_all | solution.py:425
  139.3 1.2 window.3
  140.5 20.2 %all_to_all.23 = bf16[32,32,512]{2,1,0:T(8,128)(2,1)S(1)} all-to-all(bf16[32,32,512]{2,1,0:T(8,128)(2,1)S(1)} %window.3), channel_id=1, replica_groups=mesh['freq'=32,'src'=4] {'freq'}, dimensions={0} | all-to-all | bytes 2097152 | tf_op jit(solution)/shard_map/all_to_all | solution.py:429
  160.7 1.5 finish.1
  (15 shorter events, 0.3 us)
Async XLA Ops:
  0.8 1.2 copy-start.1
  7.3 4.2 %collective-permute-start = (bf16[4,512,256]{2,1,0:T(8,128)(2,1)S(1)}, bf16[4,512,256]{2,1,0:T(8,128)(2,1)S(1)}, u32[]{:S(2)}, u32[]{:S(2)}) collective-permute-start(bf16[4,512,256]{2,1,0:T(8,128)(2,1)S(1)} %get-tuple-element.27), channel_id=1, source_target_pairs={{0,1},{1,0},{2,3},{3,2},{4,5},{5,4},{6,7},{7,6},{8,9},{9,8},{10,11... | collective-permute-start | bytes 3145736 | tf_op jit(solution)/shard_map/ppermute | solution.py:358
  7.4 10.0 %collective-permute-start.1 = (bf16[4,512,256]{2,1,0:T(8,128)(2,1)S(1)}, bf16[4,512,256]{2,1,0:T(8,128)(2,1)S(1)}, u32[]{:S(2)}, u32[]{:S(2)}) collective-permute-start(bf16[4,512,256]{2,1,0:T(8,128)(2,1)S(1)} %get-tuple-element.31), channel_id=1, source_target_pairs={{0,1},{1,0},{2,3},{3,2},{4,5},{5,4},{6,7},{7,6},{8,9},{9,8},{10,11... | collective-permute-start | bytes 3145736 | tf_op jit(solution)/shard_map/ppermute | solution.py:358
  11.6 9.0 %collective-permute-start.2 = (bf16[4,256,128]{2,1,0:T(8,128)(2,1)S(1)}, bf16[4,256,128]{2,1,0:T(8,128)(2,1)S(1)}, u32[]{:S(2)}, u32[]{:S(2)}) collective-permute-start(bf16[4,256,128]{2,1,0:T(8,128)(2,1)S(1)} %get-tuple-element.28.refs_2_), channel_id=1, source_target_pairs={{0,2},{1,3},{2,0},{3,1},{4,6},{5,7},{6,4},{7,5},{8,10},{9,11},{10,... | collective-permute-start | bytes 786440 | tf_op jit(solution)/shard_map/ppermute | solution.py:358
  13.6 9.4 %copy-start = (bf16[512,512]{1,0:T(8,128)(2,1)S(1)}, bf16[512,512]{1,0:T(8,128)(2,1)}, u32[]{:S(2)}) copy-start(bf16[512,512]{1,0:T(8,128)(2,1)} %constant.39.clone.pack_ref) | copy-start | bytes 1572868
  17.2 9.3 %collective-permute-start.5 = (bf16[4,256,128]{2,1,0:T(8,128)(2,1)S(1)}, bf16[4,256,128]{2,1,0:T(8,128)(2,1)S(1)}, u32[]{:S(2)}, u32[]{:S(2)}) collective-permute-start(bf16[4,256,128]{2,1,0:T(8,128)(2,1)S(1)} %get-tuple-element.29.refs_3_), channel_id=1, source_target_pairs={{0,2},{1,3},{2,0},{3,1},{4,6},{5,7},{6,4},{7,5},{8,10},{9,11},{10,... | collective-permute-start | bytes 786440 | tf_op jit(solution)/shard_map/ppermute | solution.py:358
  20.6 41.0 %copy-start.3 = (bf16[2,256,256]{2,1,0:T(8,128)(2,1)S(1)}, bf16[2,256,256]{2,1,0:T(8,128)(2,1)}, u32[]{:S(2)}) copy-start(bf16[2,256,256]{2,1,0:T(8,128)(2,1)} %constant.40.clone.dft_ref) | copy-start | bytes 786436
  20.6 41.0 %copy-start.4 = (s32[4,512]{1,0:T(4,128)S(1)}, s32[4,512]{1,0:T(4,128)}, u32[]{:S(2)}) copy-start(s32[4,512]{1,0:T(4,128)} %onsets_ref.3) | copy-start | bytes 24580
  20.7 16.3 %collective-permute-start.3 = (bf16[4,512,128]{2,1,0:T(8,128)(2,1)S(1)}, bf16[4,512,128]{2,1,0:T(8,128)(2,1)S(1)}, u32[]{:S(2)}, u32[]{:S(2)}) collective-permute-start(bf16[4,512,128]{2,1,0:T(8,128)(2,1)S(1)} %add.15.refs_0_), channel_id=1, source_target_pairs={{0,2},{1,3},{2,0},{3,1},{4,6},{5,7},{6,4},{7,5},{8,10},{9,11},{10,... | collective-permute-start | bytes 1572872 | tf_op jit(solution)/shard_map/ppermute | solution.py:358
  23.4 63.2 %copy-start.2 = (bf16[2,4,128,512]{3,2,1,0:T(8,128)(2,1)S(1)}, bf16[2,4,128,512]{3,2,1,0:T(8,128)(2,1)}, u32[]{:S(2)}) copy-start(bf16[2,4,128,512]{3,2,1,0:T(8,128)(2,1)} %initial_ref.1) | copy-start | bytes 3145732
  23.4 8.4 %collective-permute-start.4 = (bf16[16,32,256]{2,1,0:T(8,128)(2,1)S(1)}, bf16[16,32,256]{2,1,0:T(8,128)(2,1)S(1)}, u32[]{:S(2)}, u32[]{:S(2)}) collective-permute-start(bf16[16,32,256]{2,1,0:T(8,128)(2,1)S(1)} %total.4), channel_id=1, source_target_pairs={{0,18},{1,19},{2,16},{3,17},{4,22},{5,23},{6,20},{7,21},{8,26},{9,... | collective-permute-start | bytes 786440 | tf_op jit(solution)/shard_map/ppermute | solution.py:370
  26.9 9.8 %collective-permute-start.6 = (bf16[16,32,256]{2,1,0:T(8,128)(2,1)S(1)}, bf16[16,32,256]{2,1,0:T(8,128)(2,1)S(1)}, u32[]{:S(2)}, u32[]{:S(2)}) collective-permute-start(bf16[16,32,256]{2,1,0:T(8,128)(2,1)S(1)} %total.5), channel_id=1, source_target_pairs={{0,18},{1,19},{2,16},{3,17},{4,22},{5,23},{6,20},{7,21},{8,26},{9,... | collective-permute-start | bytes 786440 | tf_op jit(solution)/shard_map/ppermute | solution.py:370
  89.9 2.7 %collective-permute-start.7 = (bf16[4,512,256]{2,1,0:T(8,128)(2,1)S(1)}, bf16[4,512,256]{2,1,0:T(8,128)(2,1)S(1)}, u32[]{:S(2)}, u32[]{:S(2)}) collective-permute-start(bf16[4,512,256]{2,1,0:T(8,128)(2,1)S(1)} %get-tuple-element.34), channel_id=1, source_target_pairs={{0,1},{1,0},{2,3},{3,2},{4,5},{5,4},{6,7},{7,6},{8,9},{9,8},{10,11... | collective-permute-start | bytes 3145736 | tf_op jit(solution)/shard_map/ppermute | solution.py:358
  90.0 6.7 %collective-permute-start.8 = (bf16[4,512,256]{2,1,0:T(8,128)(2,1)S(1)}, bf16[4,512,256]{2,1,0:T(8,128)(2,1)S(1)}, u32[]{:S(2)}, u32[]{:S(2)}) collective-permute-start(bf16[4,512,256]{2,1,0:T(8,128)(2,1)S(1)} %get-tuple-element.38), channel_id=1, source_target_pairs={{0,1},{1,0},{2,3},{3,2},{4,5},{5,4},{6,7},{7,6},{8,9},{9,8},{10,11... | collective-permute-start | bytes 3145736 | tf_op jit(solution)/shard_map/ppermute | solution.py:358
  92.8 9.2 %collective-permute-start.9 = (bf16[4,256,128]{2,1,0:T(8,128)(2,1)S(1)}, bf16[4,256,128]{2,1,0:T(8,128)(2,1)S(1)}, u32[]{:S(2)}, u32[]{:S(2)}) collective-permute-start(bf16[4,256,128]{2,1,0:T(8,128)(2,1)S(1)} %get-tuple-element.36.refs_2_), channel_id=1, source_target_pairs={{0,2},{1,3},{2,0},{3,1},{4,6},{5,7},{6,4},{7,5},{8,10},{9,11},{10,... | collective-permute-start | bytes 786440 | tf_op jit(solution)/shard_map/ppermute | solution.py:358
  93.3 14.4 %collective-permute-start.12 = (bf16[4,256,128]{2,1,0:T(8,128)(2,1)S(1)}, bf16[4,256,128]{2,1,0:T(8,128)(2,1)S(1)}, u32[]{:S(2)}, u32[]{:S(2)}) collective-permute-start(bf16[4,256,128]{2,1,0:T(8,128)(2,1)S(1)} %get-tuple-element.37.refs_3_), channel_id=1, source_target_pairs={{0,2},{1,3},{2,0},{3,1},{4,6},{5,7},{6,4},{7,5},{8,10},{9,11},{10,... | collective-permute-start | bytes 786440 | tf_op jit(solution)/shard_map/ppermute | solution.py:358
  102.2 15.9 %collective-permute-start.10 = (bf16[4,512,128]{2,1,0:T(8,128)(2,1)S(1)}, bf16[4,512,128]{2,1,0:T(8,128)(2,1)S(1)}, u32[]{:S(2)}, u32[]{:S(2)}) collective-permute-start(bf16[4,512,128]{2,1,0:T(8,128)(2,1)S(1)} %add.17.refs_0_), channel_id=1, source_target_pairs={{0,2},{1,3},{2,0},{3,1},{4,6},{5,7},{6,4},{7,5},{8,10},{9,11},{10,... | collective-permute-start | bytes 1572872 | tf_op jit(solution)/shard_map/ppermute | solution.py:358
  103.0 8.0 %collective-permute-start.11 = (bf16[16,32,256]{2,1,0:T(8,128)(2,1)S(1)}, bf16[16,32,256]{2,1,0:T(8,128)(2,1)S(1)}, u32[]{:S(2)}, u32[]{:S(2)}) collective-permute-start(bf16[16,32,256]{2,1,0:T(8,128)(2,1)S(1)} %total.6), channel_id=1, source_target_pairs={{0,18},{1,19},{2,16},{3,17},{4,22},{5,23},{6,20},{7,21},{8,26},{9,... | collective-permute-start | bytes 786440 | tf_op jit(solution)/shard_map/ppermute | solution.py:370
  108.0 8.3 %collective-permute-start.13 = (bf16[16,32,256]{2,1,0:T(8,128)(2,1)S(1)}, bf16[16,32,256]{2,1,0:T(8,128)(2,1)S(1)}, u32[]{:S(2)}, u32[]{:S(2)}) collective-permute-start(bf16[16,32,256]{2,1,0:T(8,128)(2,1)S(1)} %total.7), channel_id=1, source_target_pairs={{0,18},{1,19},{2,16},{3,17},{4,22},{5,23},{6,20},{7,21},{8,26},{9,... | collective-permute-start | bytes 786440 | tf_op jit(solution)/shard_map/ppermute | solution.py:370
